TPU v7x, 128 devices: a whole 4x4x4 slice. The times are simulated.
128 devices in a mesh: dp: 16 (over z_hi, x, core), seq: 8 (over z_lo, y).
Axes of the slice: x: 4, y: 4, z: 4 (z_hi: 2, z_lo: 2; z = z_hi * 2 + z_lo), core: 2. Of those that a mesh axis runs over, the one named last changes fastest.
Arguments:
- queries: bfloat16 [16, 1024, 12288], P('dp', 'seq'), may hold values from -10 to 10
- latents: bfloat16 [16, 1024, 576], P('dp', 'seq'), may hold values from -6 to 6
- kv_weight: bfloat16 [512, 16384], P(None, 'seq'), may hold values from -0.25 to 0.25
- out_grad: bfloat16 [16, 1024, 8192], P('dp', 'seq'), may hold values from -6 to 6
Outputs:
- query_grad: bfloat16 [16, 1024, 12288], P('dp', 'seq')
- latent_grad: bfloat16 [16, 1024, 576], P('dp', 'seq')
- weight_grad: float32 [512, 16384], P(None, 'seq')
All inputs are finite; a program needn't handle non-finite values.
Results may differ from a plain program's by a relative error of at most 0.023.
Values may be sent and summed in bfloat16 or wider, within the bound.
No kernel may reach another device: no remote copies, remote signals or barrier semaphores. Data moves between devices by JAX's collectives and lax.ppermute only.
A program may use at most 192 MiB of HBM per device.

v0:
```python
import jax
import jax.numpy as jnp
from jax import lax
from jax.sharding import PartitionSpec as P

NOPE = 128
ROPE = 64
VDIM = 128
LATENT = 512


def attend_block(q_rows, g_rows, key_nope, key_rope, values, first, scale):
    rows = q_rows.shape[0]
    count = key_nope.shape[0]
    scores = jnp.einsum(
        "qhd,khd->hqk", q_rows[:, :, :NOPE], key_nope, preferred_element_type=jnp.float32
    )
    scores = scores + jnp.einsum(
        "qhd,kd->hqk", q_rows[:, :, NOPE:], key_rope, preferred_element_type=jnp.float32
    )
    scores = scores * scale
    query_pos = first + lax.broadcasted_iota(jnp.int32, (rows, count), 0)
    key_pos = lax.broadcasted_iota(jnp.int32, (rows, count), 1)
    scores = jnp.where((key_pos <= query_pos)[None], scores, -jnp.inf)
    top = jnp.max(scores, axis=2, keepdims=True)
    expo = jnp.exp(scores - top)
    probs = expo / jnp.sum(expo, axis=2, keepdims=True)
    probs_low = probs.astype(jnp.bfloat16)
    attended = jnp.einsum("hqk,khd->qhd", probs_low, values, preferred_element_type=jnp.float32)
    delta = jnp.sum(g_rows.astype(jnp.float32) * attended, axis=2)
    dprobs = jnp.einsum("qhd,khd->hqk", g_rows, values, preferred_element_type=jnp.float32)
    dscores = (probs * (dprobs - delta.T[:, :, None])).astype(jnp.bfloat16)
    dq_nope = (
        jnp.einsum("hqk,khd->qhd", dscores, key_nope, preferred_element_type=jnp.float32) * scale
    )
    dq_rope = (
        jnp.einsum("hqk,kd->qhd", dscores, key_rope, preferred_element_type=jnp.float32) * scale
    )
    dquery = jnp.concatenate([dq_nope, dq_rope], axis=2).astype(jnp.bfloat16)
    dkey_nope = (
        jnp.einsum("hqk,qhd->khd", dscores, q_rows[:, :, :NOPE], preferred_element_type=jnp.float32)
        * scale
    )
    dkey_rope = (
        jnp.einsum("hqk,qhd->khd", dscores, q_rows[:, :, NOPE:], preferred_element_type=jnp.float32)
        * scale
    )
    dvalue = jnp.einsum("hqk,qhd->khd", probs_low, g_rows, preferred_element_type=jnp.float32)
    return (dquery, dkey_nope, dkey_rope, dvalue)


def run_heads(query_all, grad_all, keyval, key_rope, scale):
    span = keyval.shape[0]
    count = keyval.shape[1]
    key_nope = keyval[:, :, :NOPE]
    values = keyval[:, :, NOPE:]
    block = min(512, span)
    dquery_parts = []
    dkey_nope = jnp.zeros((span, count, NOPE), jnp.float32)
    dkey_rope = jnp.zeros((span, count, ROPE), jnp.float32)
    dvalue = jnp.zeros((span, count, VDIM), jnp.float32)
    for index in range(span // block):
        first = index * block
        limit = first + block
        dquery, nope_part, rope_part, value_part = attend_block(
            query_all[first:limit],
            grad_all[first:limit],
            key_nope[:limit],
            key_rope[:limit],
            values[:limit],
            first,
            scale,
        )
        dquery_parts.append(dquery)
        dkey_nope = dkey_nope.at[:limit].add(nope_part)
        dkey_rope = dkey_rope.at[:limit].add(rope_part)
        dvalue = dvalue.at[:limit].add(value_part)
    dquery_all = jnp.concatenate(dquery_parts, axis=0)
    dkeyval = jnp.concatenate([dkey_nope, dvalue], axis=2).astype(jnp.bfloat16)
    return (dquery_all, dkeyval, dkey_rope)


def shards(queries, latents, kv_weight, out_grad):
    groups = lax.axis_size("seq")
    tokens_here = queries.shape[1]
    heads_all = queries.shape[2] // (NOPE + ROPE)
    heads_here = heads_all // groups
    span = tokens_here * groups
    width_kv = NOPE + VDIM
    scale = (NOPE + ROPE) ** (-0.5)
    own_latent = latents[0]
    latent_all = lax.all_gather(own_latent, "seq", axis=0, tiled=True)
    keyval = jnp.dot(latent_all[:, :LATENT], kv_weight, preferred_element_type=jnp.float32).astype(
        jnp.bfloat16
    )
    keyval = keyval.reshape(span, heads_here, width_kv)
    key_rope = latent_all[:, LATENT:]
    query_heads = queries[0].reshape(tokens_here, heads_all, NOPE + ROPE)
    grad_heads = out_grad[0].reshape(tokens_here, heads_all, VDIM)
    query_all, grad_all = (
        lax.all_to_all(query_heads, "seq", split_axis=1, concat_axis=0, tiled=True),
        lax.all_to_all(grad_heads, "seq", split_axis=1, concat_axis=0, tiled=True),
    )
    dquery_all, dkeyval_heads, drope_heads = run_heads(query_all, grad_all, keyval, key_rope, scale)
    dkey_rope = jnp.sum(drope_heads, axis=1)
    dquery_back = lax.all_to_all(dquery_all, "seq", split_axis=0, concat_axis=1, tiled=True)
    query_grad = dquery_back.reshape(1, tokens_here, heads_all * (NOPE + ROPE))
    dkeyval = dkeyval_heads.reshape(span, heads_here * width_kv)
    back = jnp.einsum("rk,lk->rl", dkeyval, kv_weight, preferred_element_type=jnp.float32)
    latent_sum = lax.psum_scatter(
        jnp.concatenate([back, dkey_rope], axis=1).astype(jnp.bfloat16),
        "seq",
        scatter_dimension=0,
        tiled=True,
    )
    latent_grad = latent_sum[None]
    weight_part = jnp.einsum(
        "kl,kw->lw", latent_all[:, :LATENT], dkeyval, preferred_element_type=jnp.float32
    )
    weight_grad = lax.psum(weight_part.astype(jnp.bfloat16), "dp").astype(
        jnp.float32
    ) / lax.axis_size("dp")
    return (query_grad, latent_grad, weight_grad)


def solution(mesh):
    placed = (P("dp", "seq", None), P("dp", "seq", None), P(None, "seq"), P("dp", "seq", None))
    return jax.shard_map(
        shards,
        mesh=mesh,
        in_specs=placed,
        out_specs=(P("dp", "seq", None), P("dp", "seq", None), P(None, "seq")),
        check_vma=False,
    )
```

profile of v0, /device:TPU:0, one launch (start us, length us, event | category | flops | bytes accessed | tf_op | source)
XLA Modules:
  0.0 452.0 jit_solution(12207992615881511514)
XLA Ops:
  7.2 4.2 copy.121
  11.4 4.1 copy.122
  15.5 5.9 %all-to-all-start.1 = ((bf16[128,64,128]{2,0,1:T(8,128)(2,1)}), bf16[128,64,128]{2,0,1:T(8,128)(2,1)}, u32[]{:S(2)}, u32[]{:S(2)}) async-start(bf16[128,64,128]{2,0,1:T(8,128)(2,1)} %copy.122), calls=%async_computation.1 | async-start | bytes 4194304 | tf_op jit(solution)/shard_map/all_to_all | solution.py:102
  22.1 4.6 %copy.117 = bf16[1,128,12288]{1,2,0:T(8,128)(2,1)} copy(bf16[1,128,12288]{2,1,0:T(8,128)(2,1)} %param.22) | data formatting | bytes 6291456 | tf_op args[0]
  26.7 26.5 %all-to-all-done.1 = bf16[128,64,128]{2,0,1:T(8,128)(2,1)} async-done(((bf16[128,64,128]{2,0,1:T(8,128)(2,1)}), bf16[128,64,128]{2,0,1:T(8,128)(2,1)}, u32[]{:S(2)}, u32[]{:S(2)}) %all-to-all-start.1) | async-done | bytes 2097184 | tf_op jit(solution)/shard_map/all_to_all | solution.py:102
  53.2 5.0 %all-to-all-start = ((bf16[128,64,192]{0,2,1:T(8,128)(2,1)}), bf16[128,64,192]{0,2,1:T(8,128)(2,1)}, u32[]{:S(2)}, u32[]{:S(2)}) async-start(bf16[128,64,192]{0,2,1:T(8,128)(2,1)} %bitcast.136), calls=%async_computation | async-start | bytes 6291456 | tf_op jit(solution)/shard_map/all_to_all | solution.py:101
  65.6 40.5 %all-gather.3.cloned.1.call-done = bf16[1,1024,576]{1,2,0:T(8,128)(2,1)} async-done(((bf16[1,128,576]{1,2,0:T(8,128)(2,1)}), bf16[1,1024,576]{1,2,0:T(8,128)(2,1)}) %all-gather.3.cloned.1.call-update) | async-done | bytes 1179664 | tf_op jit(solution)/shard_map/all_gather | solution.py:92
  106.1 3.6 convolution_convert_fusion
  114.5 3.8 fusion.53
  118.3 3.9 copy.118
  122.1 5.7 %fusion.43 = f32[8,512,512]{2,1,0:T(8,128)} fusion(bf16[512,8,192]{2,0,1:T(8,128)(2,1)} %bitcast.131, bf16[512,8,128]{2,1,0:T(8,128)(2,1)S(1)} %get-tuple-element.112), kind=kOutput, calls=%fused_computation.67 | convolution fusion | flops 536870912 | bytes 10485760 | tf_op jit(solution)/shard_map/qhd,khd->hqk/dot_general | solution.py:15
  127.8 10.1 %fusion.56 = (f32[8,512]{1,0:T(8,128)S(1)}, f32[8,512,512]{1,2,0:T(8,128)}) fusion(f32[8,512,512]{2,1,0:T(8,128)} %fusion.43, pred[512,512]{0,1:T(8,128)(4,1)S(1)} %iota_compare_fusion.1, bf16[512,8,192]{2,0,1:T(8,128)(2,1)} %bitcast.132, bf16[1024,576]{0,1:T(8,128)(2,1)} %bitcast.154), kind=kOutput, calls=%fused_computation.83 | convolution fusion | flops 278921728 | bytes 18169856 | tf_op jit(solution)/shard_map/sub | solution.py:26
  138.0 4.8 %fusion.11 = bf16[8,512,512]{1,2,0:T(8,128)(2,1)S(1)} fusion(f32[8,512,512]{1,2,0:T(8,128)} %get-tuple-element.122, f32[8,512]{1,0:T(8,128)S(1)} %get-tuple-element.121), kind=kLoop, calls=%fused_computation.24 | loop fusion | flops 4194304 | bytes 12599296 | tf_op jit(solution)/shard_map/convert_element_type | solution.py:28
  156.6 3.9 copy.132
  160.5 10.0 %fusion.21 = f32[8,1024,512]{2,1,0:T(8,128)} fusion(bf16[1024,8,128]{2,1,0:T(8,128)(2,1)} %get-tuple-element.114, bf16[512,8,192]{2,0,1:T(8,128)(2,1)} %bitcast.137), kind=kOutput, calls=%fused_computation.44 | convolution fusion | flops 1073741824 | bytes 19922944 | tf_op jit(solution)/shard_map/qhd,khd->hqk/dot_general | solution.py:15
  170.5 12.8 %fusion.55 = (f32[8,512]{1,0:T(8,128)S(1)}, f32[8,512,1024]{1,2,0:T(8,128)}) fusion(f32[8,1024,512]{2,1,0:T(8,128)} %fusion.21, pred[512,1024]{0,1:T(8,128)(4,1)S(1)} %copy-done.12, bf16[512,8,192]{2,0,1:T(8,128)(2,1)} %bitcast.138, bf16[1024,576]{0,1:T(8,128)(2,1)} %bitcast.156), kind=kOutput, calls=%fused_computation.82 | convolution fusion | flops 557843456 | bytes 35274752 | tf_op jit(solution)/shard_map/sub | solution.py:26
  183.3 7.3 %fusion.8 = bf16[8,512,1024]{1,2,0:T(8,128)(2,1)S(1)} fusion(f32[8,512,1024]{1,2,0:T(8,128)} %get-tuple-element.120, f32[8,512]{1,0:T(8,128)S(1)} %get-tuple-element.119), kind=kLoop, calls=%fused_computation.15 | loop fusion | flops 8388608 | bytes 25182208 | tf_op jit(solution)/shard_map/convert_element_type | solution.py:28
  193.8 8.5 %fusion.2 = bf16[8,512,1024]{1,2,0:T(8,128)(2,1)S(1)} fusion(bf16[512,8,128]{2,0,1:T(8,128)(2,1)} %bitcast.149, f32[8,512]{1,0:T(8,128)S(1)} %bitcast.160, f32[8,512,1024]{1,2,0:T(8,128)} %get-tuple-element.120, f32[8,512]{1,0:T(8,128)S(1)} %get-tuple-element.119, bf16[1024,8,128]{2,1,0:T(8,128)(2,1)} %get-tuple-element.113), kind=kOutput, calls=%fused_computation.3 | convolution fusion | flops 1090519040 | bytes 28344320 | tf_op jit(solution)/shard_map/qhd,khd->hqk/dot_general | solution.py:31
  205.4 3.3 fusion.32
  208.8 8.5 %fusion.9 = bf16[1024,8,128]{0,2,1:T(8,128)(2,1)} fusion(f32[512,8,128]{0,2,1:T(8,128)} %convolution_bitcast_fusion, bf16[8,512,1024]{1,2,0:T(8,128)(2,1)} %copy-done.4, bf16[512,8,128]{2,0,1:T(8,128)(2,1)} %bitcast.150), kind=kOutput, calls=%fused_computation.18 | convolution fusion | flops 1075838976 | bytes 13631488 | tf_op jit(solution)/shard_map/hqk,qhd->khd/dot_general | solution.py:48
  217.3 6.2 %fusion.10 = bf16[1024,8,128]{0,2,1:T(8,128)(2,1)} fusion(f32[512,8,128]{0,2,1:T(8,128)} %multiply_bitcast_fusion, bf16[8,512,1024]{1,2,0:T(8,128)(2,1)S(1)} %fusion.2, bf16[512,8,192]{2,0,1:T(8,128)(2,1)} %bitcast.139), kind=kOutput, calls=%fused_computation.20 | convolution fusion | flops 1076887552 | bytes 13631488 | tf_op jit(solution)/shard_map/hqk,qhd->khd/dot_general | solution.py:41
  228.2 3.7 fusion.12
  235.0 6.8 %copy.142 = bf16[1024,8,192]{2,1,0:T(8,128)(2,1)} copy(bf16[1024,8,192]{0,2,1:T(8,128)(2,1)} %maximum_maximum_fusion) | data formatting | bytes 6291456 | tf_op jit(solution)/shard_map/concatenate | solution.py:78
  241.9 6.0 %all-to-all-start.2 = ((bf16[1024,8,192]{2,1,0:T(8,128)(2,1)}), bf16[1024,8,192]{2,1,0:T(8,128)(2,1)}, u32[]{:S(2)}, u32[]{:S(2)}) async-start(bf16[1024,8,192]{2,1,0:T(8,128)(2,1)} %copy.142), calls=%async_computation.2 | async-start | bytes 8388608 | tf_op jit(solution)/shard_map/all_to_all | solution.py:106
  248.1 4.0 fusion.29
  252.2 6.3 %fusion.13 = bf16[1024,64]{0,1:T(8,128)(2,1)S(1)} fusion(f32[512,8,64]{0,2,1:T(8,128)S(1)} %fusion.29, bf16[8,512,1024]{1,2,0:T(8,128)(2,1)} %copy-done.2, bf16[512,8,192]{2,0,1:T(8,128)(2,1)S(1)} %bitcast.140), kind=kOutput, calls=%fused_computation.29 | convolution fusion | flops 538378240 | bytes 10616832 | tf_op jit(solution)/shard_map/hqk,qhd->khd/dot_general | solution.py:45
  262.4 126.3 %all-reduce.5.cloned.1.call-done = bf16[512,2048]{0,1:T(8,128)(2,1)} async-done(((bf16[512,2048]{0,1:T(8,128)(2,1)}), bf16[512,2048]{0,1:T(8,128)(2,1)}) %all-reduce.5.cloned.1.call-update) | async-done | bytes 2097168 | tf_op jit(solution)/shard_map/psum | solution.py:120
  388.7 4.1 convert_multiply_fusion
  392.8 5.3 %copy.158 = f32[512,2048]{1,0:T(8,128)} copy(f32[512,2048]{0,1:T(8,128)} %convert_multiply_fusion) | data formatting | bytes 8388608
  398.1 34.2 %reduce-scatter.4.cloned.1.call-done = bf16[128,576]{1,0:T(8,128)(2,1)} async-done(((bf16[1024,576]{1,0:T(8,128)(2,1)}), bf16[128,576]{1,0:T(8,128)(2,1)}) %reduce-scatter.4.cloned.1.call-update) | async-done | bytes 147472
  434.0 6.6 %copy.144 = bf16[128,8,8,192]{0,3,2,1:T(8,128)(2,1)} copy(bf16[128,8,8,192]{3,2,0,1:T(8,128)(2,1)} %bitcast.31) | data formatting | bytes 6291456 | tf_op jit(solution)/shard_map/all_to_all | solution.py:106
  440.6 4.6 %copy.157 = bf16[1,128,12288]{2,1,0:T(8,128)(2,1)} copy(bf16[1,128,12288]{1,2,0:T(8,128)(2,1)} %bitcast.135) | data formatting | bytes 6291456
  (69 shorter events, 46.5 us)
Async XLA Ops:
  7.2 98.9 %copy-start = (bf16[512,2048]{1,0:T(8,128)(2,1)S(1)}, bf16[512,2048]{1,0:T(8,128)(2,1)}, u32[]{:S(2)}) copy-start(bf16[512,2048]{1,0:T(8,128)(2,1)} %param.24) | copy-start | bytes 6291460
  15.5 37.7 %all-to-all-start.1 = ((bf16[128,64,128]{2,0,1:T(8,128)(2,1)}), bf16[128,64,128]{2,0,1:T(8,128)(2,1)}, u32[]{:S(2)}, u32[]{:S(2)}) async-start(bf16[128,64,128]{2,0,1:T(8,128)(2,1)} %copy.122), calls=%async_computation.1 | async-start | bytes 4194304 | tf_op jit(solution)/shard_map/all_to_all | solution.py:102
  21.4 84.7 %all-gather.3.cloned.1.call-start = ((), (), s32[]{:S(2)}) async-start(), calls=%async_computation.5 | async-start | bytes 1327104 | tf_op jit(solution)/shard_map/all_gather | solution.py:92
  53.2 61.3 %all-to-all-start = ((bf16[128,64,192]{0,2,1:T(8,128)(2,1)}), bf16[128,64,192]{0,2,1:T(8,128)(2,1)}, u32[]{:S(2)}, u32[]{:S(2)}) async-start(bf16[128,64,192]{0,2,1:T(8,128)(2,1)} %bitcast.136), calls=%async_computation | async-start | bytes 6291456 | tf_op jit(solution)/shard_map/all_to_all | solution.py:101
  58.2 330.5 %all-reduce.5.cloned.1.call-start = ((), (), s32[]{:S(2)}) async-start(), calls=%async_computation.4 | async-start | bytes 4194304 | tf_op jit(solution)/shard_map/psum | solution.py:120
  138.0 4.8 %copy-start.8 = (bf16[4,128,8,128]{3,1,0,2:T(8,128)(2,1)S(1)}, bf16[4,128,8,128]{3,1,0,2:T(8,128)(2,1)}, u32[]{:S(2)}) copy-start(bf16[4,128,8,128]{3,1,0,2:T(8,128)(2,1)} %copy.124) | copy-start | bytes 3145732
  138.0 9.4 %slice-start = ((s8[8388608]{0:T(1024)(128)(4,1)}), s8[4194304]{0:T(1024)(128)(4,1)S(1)}, s32[]{:S(2)}) async-start(s8[8388608]{0:T(1024)(128)(4,1)} %bitcast.127), calls=%async_computation.7 | async-start | bytes 8388608
  142.7 2.8 copy-start.14
  142.8 4.6 %slice-start.1 = ((s8[8388608]{0:T(1024)(128)(4,1)}), s8[4194304]{0:T(1024)(128)(4,1)S(1)}, s32[]{:S(2)}) async-start(s8[8388608]{0:T(1024)(128)(4,1)} %bitcast.127), calls=%async_computation.8 | async-start | bytes 8388608
  148.9 4.8 %copy-start.1 = (bf16[8,512,512]{1,2,0:T(8,128)(2,1)}, bf16[8,512,512]{1,2,0:T(8,128)(2,1)S(1)}, u32[]{:S(2)}) copy-start(bf16[8,512,512]{1,2,0:T(8,128)(2,1)S(1)} %fusion.5) | copy-start | bytes 12582916
  148.9 4.8 %copy-start.5 = (bf16[4,128,8,192]{3,1,0,2:T(8,128)(2,1)S(1)}, bf16[4,128,8,192]{3,1,0,2:T(8,128)(2,1)}, u32[]{:S(2)}) copy-start(bf16[4,128,8,192]{3,1,0,2:T(8,128)(2,1)} %copy.118) | copy-start | bytes 4718596
  160.5 10.0 %copy-start.12 = (pred[512,1024]{0,1:T(8,128)(4,1)S(1)}, pred[512,1024]{0,1:T(8,128)(4,1)}, u32[]{:S(2)}) copy-start(pred[512,1024]{0,1:T(8,128)(4,1)} %iota_compare_fusion) | copy-start | bytes 1572868
  183.3 7.4 %copy-start.11 = (bf16[4,128,8,128]{3,1,0,2:T(8,128)(2,1)S(1)}, bf16[4,128,8,128]{3,1,0,2:T(8,128)(2,1)}, u32[]{:S(2)}) copy-start(bf16[4,128,8,128]{3,1,0,2:T(8,128)(2,1)} %copy.135) | copy-start | bytes 3145732
  183.3 7.4 %copy-start.13 = (bf16[1024,8,128]{2,1,0:T(8,128)(2,1)S(1)}, bf16[1024,8,128]{2,1,0:T(8,128)(2,1)}, u32[]{:S(2)}) copy-start(bf16[1024,8,128]{2,1,0:T(8,128)(2,1)} %get-tuple-element.113) | copy-start | bytes 6291460
  190.6 3.2 copy-start.4
  193.8 8.6 %copy-start.3 = (bf16[1024,8,128]{2,1,0:T(8,128)(2,1)S(1)}, bf16[1024,8,128]{2,1,0:T(8,128)(2,1)}, u32[]{:S(2)}) copy-start(bf16[1024,8,128]{2,1,0:T(8,128)(2,1)} %get-tuple-element.114) | copy-start | bytes 6291460
  202.4 14.9 %copy-start.2 = (bf16[8,512,1024]{1,2,0:T(8,128)(2,1)}, bf16[8,512,1024]{1,2,0:T(8,128)(2,1)S(1)}, u32[]{:S(2)}) copy-start(bf16[8,512,1024]{1,2,0:T(8,128)(2,1)S(1)} %fusion.2) | copy-start | bytes 25165828
  223.5 4.7 %copy-start.15 = (bf16[1,1024,576]{1,2,0:T(8,128)(2,1)S(1)}, bf16[1,1024,576]{1,2,0:T(8,128)(2,1)}, u32[]{:S(2)}) copy-start(bf16[1,1024,576]{1,2,0:T(8,128)(2,1)} %all-gather.3.cloned.1.call-done) | copy-start | bytes 3538948
  226.2 1.9 copy-start.9
  228.2 3.8 copy-start.7
  241.9 192.2 %all-to-all-start.2 = ((bf16[1024,8,192]{2,1,0:T(8,128)(2,1)}), bf16[1024,8,192]{2,1,0:T(8,128)(2,1)}, u32[]{:S(2)}, u32[]{:S(2)}) async-start(bf16[1024,8,192]{2,1,0:T(8,128)(2,1)} %copy.142), calls=%async_computation.2 | async-start | bytes 8388608 | tf_op jit(solution)/shard_map/all_to_all | solution.py:106
  247.9 184.5 %reduce-scatter.4.cloned.1.call-start = ((), (), s32[]{:S(2)}) async-start(), calls=%async_computation.6 | async-start | bytes 1474560
  248.1 4.0 copy-start.6
  252.1 6.3 %copy-start.10 = (bf16[1024,8,256]{0,2,1:T(8,128)(2,1)S(1)}, bf16[1024,8,256]{0,2,1:T(8,128)(2,1)}, u32[]{:S(2)}) copy-start(bf16[1024,8,256]{0,2,1:T(8,128)(2,1)} %copy-done.9) | copy-start | bytes 12582916
Sparse Core Ops, SparseCore 0:
  23.8 82.2 all-gather.2
  232.0 156.5 all-reduce.4
  391.7 40.6 reduce-scatter.3
where the time goes:
time: 460 us; the launch traced here: 452 us
  waiting for transfers between devices  228 us (50%)
  matrix products  105 us (23%)
  local copies, waits for them, and re-layouts  64 us (14%)
  other arithmetic  23.4 us (5%)
  starting transfers between devices  17.2 us (4%)
  between operations  14.2 us (3%)
    psum x1, waiting for transfers between devices, shards(): lax.psum(weight_part.astype(jnp.bfloat16), 'dp').astype(jnp.float32)  126 us
    all_gather x1, waiting for transfers between devices, shards(): latent_all = lax.all_gather(own_latent, 'seq', axis=0, tiled=True)  40.5 us
    unnamed x4, waiting for transfers between devices  34.9 us
    all_to_all x1, waiting for transfers between devices, shards(): lax.all_to_all(grad_heads, 'seq', split_axis=1, concat_axis=0, tiled=True)  26.5 us
    unnamed x43, local copies, waits for them, and re-layouts  25.6 us
    sub x2, matrix products, attend_block(): expo = jnp.exp(scores - top)  22.9 us
    dot_general x2, matrix products, attend_block(): jnp.einsum('qhd,khd->hqk', q_rows[:, :, :NOPE], key_nope, preferred_eleme...  15.7 us
    convert_element_type x2, other arithmetic, attend_block(): probs_low = probs.astype(jnp.bfloat16)  12.1 us
  transfers between devices with their start and end apart: 6, of which 4 were waited for; matrix products, arithmetic and copies ran while one was open for 12% of the time, Pallas kernels for 0%

commit v1 on v0

v1 whole, which is shorter than its diff:
```python
import functools

import jax
import jax.numpy as jnp
from jax import lax
from jax.experimental import pallas as pl
from jax.experimental.pallas import tpu as pltpu
from jax.sharding import PartitionSpec as P

NOPE = 128
ROPE = 64
VDIM = 128
LATENT = 512
QPAIR = 2 * (NOPE + ROPE)
GPAIR = 2 * VDIM
PAIR = QPAIR + GPAIR
KVPAIR = 2 * (NOPE + VDIM)
LATPAD = 640
LOG2E = 1.4426950408889634
VMEM = 56 * 1024 * 1024
EARLY = 2
LINE = 4


def dot(a, b, dims):
    return lax.dot_general(a, b, (dims, ((), ())), preferred_element_type=jnp.float32)


def pack_kernel(plans, with_latents, *refs):
    refs = list(refs)
    q_ref, g_ref = refs[:2]
    lat_ref = refs[2] if with_latents else None
    outs = refs[2 + with_latents : 2 + with_latents + len(plans)]
    sems = refs[-1]
    groups = outs[0].shape[0]
    per_group = q_ref.shape[1] // (groups * QPAIR)
    copies = []
    for (first, pairs), out in zip(plans, outs, strict=True):
        for j in range(groups):
            for pair in range(pairs):
                at = j * per_group + first + pair
                base = pair * PAIR
                for ref, width, to in ((q_ref, QPAIR, base), (g_ref, GPAIR, base + QPAIR)):
                    copies.append(
                        pltpu.make_async_copy(
                            ref.at[:, at * width : (at + 1) * width],
                            out.at[j, :, to : to + width],
                            sems.at[len(copies)],
                        )
                    )
    for copy in copies:
        copy.start()
    if with_latents:
        base = plans[0][1] * PAIR
        rows = lat_ref[...].T
        pad = jnp.zeros((rows.shape[0], LATPAD - rows.shape[1]), rows.dtype)
        rows = jnp.concatenate([rows, pad], axis=1)
        for j in range(groups):
            outs[0][j, :, base:] = rows
    for copy in copies:
        copy.wait()


def pack(q, g, latents, groups, plans):
    tokens = q.shape[0]
    has = latents is not None
    hbm = pl.BlockSpec(memory_space=pl.ANY)
    vmem = pl.BlockSpec(memory_space=pltpu.VMEM)
    shapes = []
    for index, (_, pairs) in enumerate(plans):
        width = pairs * PAIR + (LATPAD if has and index == 0 else 0)
        shapes.append(jax.ShapeDtypeStruct((groups, tokens, width), q.dtype))
    count = sum(2 * groups * pairs for _, pairs in plans)
    return pl.pallas_call(
        functools.partial(pack_kernel, plans, has),
        in_specs=[hbm, hbm] + [vmem] * has,
        out_specs=[vmem] * len(plans),
        out_shape=shapes,
        scratch_shapes=[pltpu.SemaphoreType.DMA((count,))],
        compiler_params=pltpu.CompilerParams(vmem_limit_bytes=VMEM),
        cost_estimate=pl.CostEstimate(
            flops=0, bytes_accessed=sum(4 * s.size for s in shapes), transcendentals=0
        ),
        name="pack",
    )(*([q, g] + [latents] * has))


def unpack_kernel(first, pairs, has_total, with_latents, *refs):
    refs = list(refs)
    if has_total:
        refs.pop(0)
    part_ref, out_ref = refs[:2]
    groups = part_ref.shape[0]
    per_group = out_ref.shape[1] // (groups * QPAIR)
    width = pairs * QPAIR
    sems, held = refs[-2:]
    fetches, copies = [], []
    for j in range(groups):
        at = (j * per_group + first) * QPAIR
        fetches.append(pltpu.make_async_copy(part_ref.at[j], held.at[j], sems.at[0, j]))
        copies.append(
            pltpu.make_async_copy(
                held.at[j, :, :width], out_ref.at[:, at : at + width], sems.at[1, j]
            )
        )
    for fetch in fetches:
        fetch.start()
    for fetch, copy in zip(fetches, copies, strict=True):
        fetch.wait()
        copy.start()
    if with_latents:
        total = held[0, :, width:].astype(jnp.float32)
        for j in range(1, groups):
            total += held[j, :, width:].astype(jnp.float32)
        refs[2][...] = total.T[: LATENT + ROPE].astype(part_ref.dtype)
    for copy in copies:
        copy.wait()


def unpack(total, part, first, pairs, per_group, with_latents):
    groups, tokens, _ = part.shape
    hbm = pl.BlockSpec(memory_space=pl.ANY)
    out_specs = [hbm]
    shapes = [jax.ShapeDtypeStruct((tokens, groups * per_group * QPAIR), part.dtype)]
    if with_latents:
        out_specs.append(pl.BlockSpec(memory_space=pltpu.VMEM))
        shapes.append(jax.ShapeDtypeStruct((LATENT + ROPE, tokens), part.dtype))
    has = total is not None
    return pl.pallas_call(
        functools.partial(unpack_kernel, first, pairs, has, with_latents),
        in_specs=[hbm] * (1 + has),
        out_specs=out_specs,
        out_shape=shapes,
        scratch_shapes=[
            pltpu.SemaphoreType.DMA((2, groups)),
            pltpu.VMEM(part.shape, part.dtype),
        ],
        input_output_aliases={0: 0} if has else {},
        compiler_params=pltpu.CompilerParams(vmem_limit_bytes=VMEM),
        cost_estimate=pl.CostEstimate(
            flops=0, bytes_accessed=4 * groups * tokens * pairs * QPAIR, transcendentals=0
        ),
        name="unpack",
    )(*([total] * has + [part]))


def one_head(q_ref, q_at, g_ref, g_at, key, value, dk_ref, dv_ref, scale, block):
    span = key.shape[0]
    dq_rows = []
    for index in reversed(range(span // block)):
        first, limit = index * block, (index + 1) * block
        q = q_ref[first:limit, q_at : q_at + 256]
        g = g_ref[first:limit, g_at : g_at + VDIM]
        keys, values = key[:limit], value[:limit]
        scores = dot(keys, q, ((1,), (1,)))
        key_pos = lax.broadcasted_iota(jnp.int32, (block, block), 0)
        query_pos = lax.broadcasted_iota(jnp.int32, (block, block), 1)
        last = jnp.where(key_pos <= query_pos, scores[first:], -jnp.inf)
        scores = jnp.concatenate([scores[:first], last], axis=0) if index else last
        top = jnp.max(scores, axis=0, keepdims=True)
        expo = jnp.exp2((scores - top) * (scale * LOG2E))
        probs = expo * (1.0 / jnp.sum(expo, axis=0, keepdims=True))
        dprobs = dot(values, g, ((1,), (1,)))
        delta = jnp.sum(probs * dprobs, axis=0, keepdims=True)
        dscores = (probs * (dprobs - delta)).astype(jnp.bfloat16)
        dv = dot(probs.astype(jnp.bfloat16), g, ((1,), (0,)))
        dk = dot(dscores, q, ((1,), (0,)))
        if limit == span:
            dv_ref[...] = dv
            dk_ref[...] = dk
        else:
            dv_ref[:limit] += dv
            dk_ref[:limit] += dk
        dq_rows.append(dot(dscores, keys, ((0,), (0,))))
    return jnp.concatenate(dq_rows[::-1], axis=0)


def attend_kernel(has_sum, last, *refs):
    refs = list(refs)
    place, lat_ref, w_ref, x_ref = refs[:4]
    rest = refs[4:]
    sum_in = rest.pop(0) if has_sum else None
    if has_sum and not last:
        rest = rest[3:]
    if last:
        dq_ref, keep_ref, send_ref, total, dk0, dv0, dk1, dv1 = rest
    else:
        dq_ref, keep_ref, send_ref, out_ref, total, dk0, dv0, dk1, dv1 = rest
    step = pl.program_id(0)
    scale = (NOPE + ROPE) ** (-0.5)
    half = NOPE // 2
    span = lat_ref.shape[0]
    block = min(256, span)
    plain = lat_ref[:, :LATENT]
    rope = lat_ref[:, LATENT:]
    keyval = dot(plain, w_ref[...], ((1,), (0,)))
    lane = lax.broadcasted_iota(jnp.int32, (span, NOPE), 1)
    key0 = jnp.concatenate([keyval[:, :NOPE].astype(jnp.bfloat16), rope], axis=1)
    value0 = keyval[:, NOPE : 2 * NOPE].astype(jnp.bfloat16)
    moved = pltpu.roll(keyval[:, 2 * NOPE : 3 * NOPE], half, 1)
    rope_moved = pltpu.roll(rope.astype(jnp.float32), half, 1)
    key1 = jnp.concatenate(
        [jnp.where(lane < half, 0.0, moved), jnp.where(lane < half, moved, rope_moved)], axis=1
    ).astype(jnp.bfloat16)
    value1 = keyval[:, 3 * NOPE :].astype(jnp.bfloat16)
    q_ref, g_at = x_ref, QPAIR
    dq0 = one_head(q_ref, 0, x_ref, g_at, key0, value0, dk0, dv0, scale, block)
    dq1 = one_head(q_ref, NOPE, x_ref, g_at + VDIM, key1, value1, dk1, dv1, scale, block)
    dq = jnp.concatenate([dq0[:, :NOPE], dq0[:, NOPE:] + dq1[:, :NOPE], dq1[:, NOPE:]], axis=1)
    dq = (dq * scale).astype(jnp.bfloat16)
    if last:
        dq_ref[:, pl.ds(pl.multiple_of(step * QPAIR, QPAIR), QPAIR)] = dq
    else:
        dq_ref[...] = dq
    left = pltpu.roll(dk1[:, :NOPE], half, 1)
    right = pltpu.roll(dk1[:, NOPE:], half, 1)
    dkeyval = jnp.concatenate(
        [
            dk0[:, :NOPE] * scale,
            dv0[...],
            jnp.where(lane < half, left, right) * scale,
            dv1[...],
        ],
        axis=1,
    ).astype(jnp.bfloat16)
    drope = jnp.where(lane < half, (dk0[:, NOPE:] + right) * scale, 0.0)
    back = dot(dkeyval, w_ref[...], ((1,), (1,)))
    dw = dot(plain, dkeyval, ((0,), (0,))).astype(jnp.bfloat16)
    rows = LATENT // 2 // LINE
    for at in range(2 * LINE):
        to = lax.rem(at % LINE - place[1] + LINE, LINE)
        to = pl.ds(pl.multiple_of(to * rows, rows), rows)
        piece = dw[at * rows : (at + 1) * rows]

        @pl.when(place[0] == at // LINE)
        def _():
            keep_ref[to, :] = piece

        @pl.when(place[0] != at // LINE)
        def _():
            send_ref[to, :] = piece

    @pl.when(step == 0)
    def _():
        if has_sum:
            total[:, :LATENT] = back + sum_in[:, :LATENT]
            total[:, LATENT:] = drope + sum_in[:, LATENT:]
        else:
            total[:, :LATENT] = back
            total[:, LATENT:] = drope

    @pl.when(step > 0)
    def _():
        total[:, :LATENT] += back
        total[:, LATENT:] += drope

    @pl.when(step == pl.num_programs(0) - 1)
    def _():
        if last:
            dq_ref[:, dq_ref.shape[1] - LATPAD :] = total[...].astype(jnp.bfloat16)
        else:
            out_ref[...] = total[...]


def attend(place, lat, lat_block, weight, first, x, pairs, held, last):
    span = lat.shape[0]
    f32, bf16 = jnp.float32, jnp.bfloat16
    whole = lambda j: (0, 0)
    hbm = pl.BlockSpec(memory_space=pl.ANY)
    specs = [
        pl.BlockSpec(memory_space=pltpu.SMEM),
        pl.BlockSpec((span, LATPAD), lambda j: (0, lat_block)),
        pl.BlockSpec((LATENT, KVPAIR), lambda j: (0, first + j)),
        pl.BlockSpec((span, PAIR), lambda j: (0, j)),
    ]
    args = [place, lat, weight, x]
    aliases = {}
    if held is not None:
        specs.append(pl.BlockSpec((span, LATPAD), whole))
        args.append(held[3])
    start = 0 if last else first
    dw_specs = [pl.BlockSpec((LATENT // 2, KVPAIR), lambda j: (0, start + j))] * 2
    dw_shapes = [jax.ShapeDtypeStruct((LATENT // 2, (pairs if last else EARLY) * KVPAIR), bf16)] * 2
    if last:
        width = pairs * QPAIR + LATPAD
        out_specs = [pl.BlockSpec((span, width), whole)] + dw_specs
        shapes = [jax.ShapeDtypeStruct((span, width), bf16)] + dw_shapes
    else:
        out_specs = [pl.BlockSpec((span, QPAIR), lambda j: (0, first + j))] + dw_specs
        out_specs.append(pl.BlockSpec((span, LATPAD), whole))
        shapes = [jax.ShapeDtypeStruct((span, EARLY * QPAIR), bf16)] + dw_shapes
        shapes.append(jax.ShapeDtypeStruct((span, LATPAD), f32))
        if held is not None:
            aliases = {5: 0, 6: 1, 7: 2}
            specs += [hbm] * 3
            args += held[:3]
    return pl.pallas_call(
        functools.partial(attend_kernel, held is not None, last),
        grid=(pairs,),
        in_specs=specs,
        out_specs=out_specs,
        out_shape=shapes,
        input_output_aliases=aliases,
        scratch_shapes=[
            pltpu.VMEM((span, LATPAD), f32),
            pltpu.VMEM((span, 2 * NOPE), f32),
            pltpu.VMEM((span, VDIM), f32),
            pltpu.VMEM((span, 2 * NOPE), f32),
            pltpu.VMEM((span, VDIM), f32),
        ],
        compiler_params=pltpu.CompilerParams(vmem_limit_bytes=VMEM),
        cost_estimate=pl.CostEstimate(
            flops=pairs * 5_000_000_000, bytes_accessed=pairs * 6_000_000, transcendentals=0
        ),
        name="attend",
    )(*args)


def exchange(x, axis, groups=None):
    return lax.all_to_all(x, axis, split_axis=0, concat_axis=0, tiled=True, axis_index_groups=groups)


def send(x, step):
    slabs = lax.axis_size("dp")
    return lax.ppermute(x, "dp", [(i, step(i)) for i in range(slabs)])


def along(step):
    def to(i):
        near = 2 * LINE
        return i // near * near + ((i // 2 + step) % LINE) * 2 + i % 2

    return to


def add_kernel(*refs):
    *parts, out_ref = refs
    total = parts[0][...].astype(jnp.float32)
    for part in parts[1:]:
        total += part[...].astype(jnp.float32)
    out_ref[...] = total.astype(out_ref.dtype)


def add(*parts):
    return pl.pallas_call(add_kernel, out_shape=parts[0], name="add")(*parts)


def split_kernel(keep_ref, got_ref, *out_refs):
    total = keep_ref[...].astype(jnp.float32) + got_ref[...].astype(jnp.float32)
    rows = out_refs[0].shape[0]
    for index, out_ref in enumerate(out_refs):
        out_ref[...] = total[index * rows : (index + 1) * rows].astype(out_ref.dtype)


def split(keep, got):
    shape = jax.ShapeDtypeStruct((keep.shape[0] // LINE, keep.shape[1]), keep.dtype)
    return pl.pallas_call(split_kernel, out_shape=[shape] * LINE, name="split")(keep, got)


def scatter_slabs(keep, give):
    own, *others = split(keep, send(give, lambda i: i ^ 1))
    part = add(own, *[send(x, along(k + 1)) for k, x in enumerate(others)])
    near = 2 * LINE
    return add(part, send(part, lambda i: (i + near) % (2 * near)))


def gather_slabs(part):
    mine = jnp.concatenate([part] + [send(part, along(k)) for k in range(1, LINE)], axis=0)
    return mine, send(mine, lambda i: i ^ 1)


def place_kernel(slabs, place, *refs):
    *parts, out_ref = refs
    rows = parts[0].shape[0] // LINE
    column = 0
    for mine, other in zip(parts[::2], parts[1::2], strict=True):
        width = mine.shape[1]
        for ref, core in ((mine, place[0]), (other, 1 - place[0])):
            for k in range(LINE):
                at = core * LINE + lax.rem(place[1] - k + LINE, LINE)
                to = pl.ds(pl.multiple_of(at * rows, rows), rows)
                piece = ref[k * rows : (k + 1) * rows].astype(jnp.float32)
                out_ref[to, column : column + width] = piece * (1.0 / slabs)
        column += width


def place_slabs(place, *parts):
    width = sum(part.shape[1] for part in parts) // 2
    vmem = pl.BlockSpec(memory_space=pltpu.VMEM)
    return pl.pallas_call(
        functools.partial(place_kernel, lax.axis_size("dp")),
        in_specs=[pl.BlockSpec(memory_space=pltpu.SMEM)] + [vmem] * len(parts),
        out_specs=vmem,
        out_shape=jax.ShapeDtypeStruct((LATENT, width), jnp.float32),
        compiler_params=pltpu.CompilerParams(vmem_limit_bytes=VMEM),
        name="place",
    )(place, *parts)


def after(x, *others):
    return lax.optimization_barrier((x,) + others)


def shards(queries, latents, kv_weight, out_grad):
    groups = lax.axis_size("seq")
    tokens = queries.shape[1]
    span = tokens * groups
    per_group = kv_weight.shape[1] // KVPAIR
    late = per_group - EARLY
    q, g, lat = queries[0], out_grad[0], latents[0].T
    me = lax.axis_index("dp")
    place = jnp.stack([me % 2, me // 2 % LINE]).astype(jnp.int32)

    (x0,) = pack(q, g, lat, groups, ((0, 1),))
    x1, x2 = pack(q, g, None, groups, ((1, 1), (2, late)))
    got0 = exchange(x0, "seq")
    x1, got0 = after(x1, got0)
    got1 = exchange(x1, "seq")
    got0 = got0.reshape(span, got0.shape[2])
    held = attend(place, got0, 1, kv_weight, 0, got0, 1, None, False)
    x2, got1, *held = after(x2, got1, *held)
    got2 = exchange(x2, "seq")
    dq, keep0, give0, total = attend(
        place, got0, 1, kv_weight, 1, got1.reshape(span, PAIR), 1, held, False
    )
    back0 = exchange(dq.reshape(groups, tokens, EARLY * QPAIR), "seq")
    part0 = scatter_slabs(keep0, give0)
    total, part0 = after(total, part0)
    send1, keep1, give1 = attend(
        place, got0, 1, kv_weight, 2, got2.reshape(span, late * PAIR), late, (0, 0, 0, total), True
    )
    keep1, give1, part0, back0 = after(keep1, give1, part0, back0)
    back1 = exchange(send1.reshape(groups, tokens, send1.shape[1]), "seq")
    part1 = scatter_slabs(keep1, give1)
    (query_grad,) = unpack(None, back0, 0, EARLY, per_group, False)
    weight_grad = place_slabs(place, *gather_slabs(part0), *gather_slabs(part1))
    query_grad, latent_grad = unpack(query_grad, back1, EARLY, late, per_group, True)
    return (query_grad[None], latent_grad.T[None], weight_grad)


def solution(mesh):
    placed = (P("dp", "seq", None), P("dp", "seq", None), P(None, "seq"), P("dp", "seq", None))
    return jax.shard_map(
        shards,
        mesh=mesh,
        in_specs=placed,
        out_specs=(P("dp", "seq", None), P("dp", "seq", None), P(None, "seq")),
        check_vma=False,
    )
```

time: 460 us -> 233 us (0.51)
  waiting for transfers between devices: 228 us -> 80.5 us
  matrix products: 105 us -> 0 us
  Pallas kernels: 0 us -> 73.8 us
  local copies, waits for them, and re-layouts: 64 us -> 12.2 us
  starting transfers between devices: 17.2 us -> 60.5 us
  other arithmetic: 23.4 us -> 1.53 us
  between operations: 14.2 us -> 1.03 us
    psum x1 -> x0, waiting for transfers between devices: 126 us -> none  [shards(): lax.psum(weight_part.astype(jnp.bfloat16), 'dp').astype(jnp.float32)]
    dot_general x19 -> x0, matrix products: 82 us -> none  [the longest x2 15.7 us: attend_block(): jnp.einsum('qhd,khd->hqk', q_rows[:, :, :NOPE], key_nope, preferred_eleme...]
    pallas_call x0 -> x14, Pallas kernels: none -> 73.8 us  [the longest x3 45 us: attend(): pl.pallas_call(functools.partial(attend_kernel, held is not None, last),...]
    all_gather x1 -> x0, waiting for transfers between devices: 40.5 us -> none  [shards(): latent_all = lax.all_gather(own_latent, 'seq', axis=0, tiled=True)]
    unnamed x4 -> x0, waiting for transfers between devices: 34.9 us -> none
    ppermute x0 -> x18, starting transfers between devices: none -> 28.8 us  [send(): return lax.ppermute(x, 'dp', [(i, step(i)) for i in range(slabs)])]
    ppermute x0 -> x18, waiting for transfers between devices: none -> 27.4 us  [send(): return lax.ppermute(x, 'dp', [(i, step(i)) for i in range(slabs)])]
    all_to_all x3 -> x5, waiting for transfers between devices: 26.5 us -> 53.1 us  [exchange(): lax.all_to_all(x, axis, split_axis=0, concat_axis=0, tiled=True, axis_ind...]
  transfers between devices with their start and end apart: 6 -> 23, of which waited for: 4 -> 13; matrix products, arithmetic and copies ran while one was open for 12% -> 2% of each run, Pallas kernels for 0% -> 29%
where the time goes in v1:
time: 233 us; the launch traced here: 230 us
  waiting for transfers between devices  80.5 us (35%)
  Pallas kernels  73.8 us (32%)
  starting transfers between devices  60.5 us (26%)
  local copies, waits for them, and re-layouts  12.2 us (5%)
    all_to_all x5, waiting for transfers between devices, exchange(): lax.all_to_all(x, axis, split_axis=0, concat_axis=0, tiled=True, axis_ind...  53.1 us
    pallas_call x3, Pallas kernels, attend(): pl.pallas_call(functools.partial(attend_kernel, held is not None, last),...  45 us
    all_to_all x5, starting transfers between devices, exchange(): lax.all_to_all(x, axis, split_axis=0, concat_axis=0, tiled=True, axis_ind...  31.7 us
    ppermute x18, starting transfers between devices, send(): return lax.ppermute(x, 'dp', [(i, step(i)) for i in range(slabs)])  28.8 us
    ppermute x18, waiting for transfers between devices, send(): return lax.ppermute(x, 'dp', [(i, step(i)) for i in range(slabs)])  27.4 us
    unnamed x39, local copies, waits for them, and re-layouts  11.2 us
    pallas_call x2, Pallas kernels, pack(): pl.pallas_call(functools.partial(pack_kernel, plans, has), in_specs=[hbm,...  8.46 us
    pallas_call x4, Pallas kernels, add(): return pl.pallas_call(add_kernel, out_shape=parts[0], name='add')(*parts)  6.94 us
  transfers between devices with their start and end apart: 23, of which 13 were waited for; matrix products, arithmetic and copies ran while one was open for 2% of the time, Pallas kernels for 29%

profile of v1, /device:TPU:0, one launch (start us, length us, event | category | flops | bytes accessed | tf_op | source)
XLA Modules:
  0.0 229.6 jit_solution(2447220214746794049)
XLA Ops:
  0.6 3.9 %pack.3 = bf16[8,128,1280]{2,1,0:T(8,128)(2,1)} custom-call(bf16[128,12288]{1,0:T(8,128)(2,1)} %bitcast.17, bf16[128,8192]{1,0:T(8,128)(2,1)} %bitcast.19, bf16[576,128]{1,0:T(8,128)(2,1)} %bitcast.28), custom_call_target="tpu_custom_call" | custom-call | bytes 5242880 | tf_op jit(solution)/shard_map/pack/pallas_call | solution.py:74
  4.6 5.9 %all-to-all-start = ((bf16[8,128,1280]{2,1,0:T(8,128)(2,1)}), bf16[8,128,1280]{2,1,0:T(8,128)(2,1)S(1)}, u32[]{:S(2)}, u32[]{:S(2)}) async-start(bf16[8,128,1280]{2,1,0:T(8,128)(2,1)} %pack.3), calls=%async_computation | async-start | bytes 5242880 | tf_op jit(solution)/shard_map/all_to_all | solution.py:320
  10.5 4.5 %pack.2 = (bf16[8,128,640]{2,1,0:T(8,128)(2,1)}, bf16[8,128,1280]{2,1,0:T(8,128)(2,1)}) custom-call(bf16[128,12288]{1,0:T(8,128)(2,1)} %bitcast.18, bf16[128,8192]{1,0:T(8,128)(2,1)} %bitcast.20), custom_call_target="tpu_custom_call" | custom-call | bytes 7864320 | tf_op jit(solution)/shard_map/pack/pallas_call | solution.py:74
  15.0 28.0 %all-to-all-done = bf16[8,128,1280]{2,1,0:T(8,128)(2,1)S(1)} async-done(((bf16[8,128,1280]{2,1,0:T(8,128)(2,1)}), bf16[8,128,1280]{2,1,0:T(8,128)(2,1)S(1)}, u32[]{:S(2)}, u32[]{:S(2)}) %all-to-all-start) | async-done | bytes 2621472 | tf_op jit(solution)/shard_map/all_to_all | solution.py:320
  43.0 8.9 %all-to-all-start.1 = ((bf16[8,128,640]{2,1,0:T(8,128)(2,1)}), bf16[8,128,640]{2,1,0:T(8,128)(2,1)}, u32[]{:S(2)}, u32[]{:S(2)}) async-start(bf16[8,128,640]{2,1,0:T(8,128)(2,1)} %get-tuple-element.43), calls=%async_computation.1 | async-start | bytes 2621440 | tf_op jit(solution)/shard_map/all_to_all | solution.py:320
  52.6 11.6 %attend.3 = (bf16[1024,768]{1,0:T(8,128)(2,1)}, bf16[256,1024]{1,0:T(8,128)(2,1)}, bf16[256,1024]{1,0:T(8,128)(2,1)}, f32[1024,640]{1,0:T(8,128)}) custom-call(s32[2]{0:T(128)} %pad_add_fusion.refs_0_.place, bf16[1024,1280]{1,0:T(8,128)(2,1)} %bitcast.22, bf16[512,2048]{1,0:T(8,128)(2,1)} %refs_2_.5, bf16[1024,1280]{1,0:T(8,128)(2,1)} %bitcast.23), custom_call_target="tpu_custom_call" | custom-call | flops 5000000000 | bytes 6000000 | tf_op jit(solution)/shard_map/attend/pallas_call | solution.py:297
  64.2 5.2 %all-to-all-done.1 = bf16[8,128,640]{2,1,0:T(8,128)(2,1)} async-done(((bf16[8,128,640]{2,1,0:T(8,128)(2,1)}), bf16[8,128,640]{2,1,0:T(8,128)(2,1)}, u32[]{:S(2)}, u32[]{:S(2)}) %all-to-all-start.1) | async-done | bytes 1310752 | tf_op jit(solution)/shard_map/all_to_all | solution.py:320
  69.3 3.8 %all-to-all-start.2 = ((bf16[8,128,1280]{2,1,0:T(8,128)(2,1)}), bf16[8,128,1280]{2,1,0:T(8,128)(2,1)S(1)}, u32[]{:S(2)}, u32[]{:S(2)}) async-start(bf16[8,128,1280]{2,1,0:T(8,128)(2,1)} %get-tuple-element.48), calls=%async_computation.2 | async-start | bytes 5242880 | tf_op jit(solution)/shard_map/all_to_all | solution.py:320
  73.2 12.5 %attend.4 = (bf16[1024,768]{1,0:T(8,128)(2,1)}, bf16[256,1024]{1,0:T(8,128)(2,1)}, bf16[256,1024]{1,0:T(8,128)(2,1)}, f32[1024,640]{1,0:T(8,128)}) custom-call(s32[2]{0:T(128)} %pad_add_fusion.refs_0_.place, bf16[1024,1280]{1,0:T(8,128)(2,1)} %bitcast.24, bf16[512,2048]{1,0:T(8,128)(2,1)} %refs_2_.5, ...), custom_call_target="tpu_custom_call", output_to_operand_aliasing={{0}: (5, {}), {1}: (6, {}), {2}: (7, {})} | custom-call | flops 5000000000 | bytes 6000000 | tf_op jit(solution)/shard_map/attend/pallas_call | solution.py:297
  85.6 19.9 %all-to-all-done.2 = bf16[8,128,1280]{2,1,0:T(8,128)(2,1)S(1)} async-done(((bf16[8,128,1280]{2,1,0:T(8,128)(2,1)}), bf16[8,128,1280]{2,1,0:T(8,128)(2,1)S(1)}, u32[]{:S(2)}, u32[]{:S(2)}) %all-to-all-start.2) | async-done | bytes 2621472 | tf_op jit(solution)/shard_map/all_to_all | solution.py:320
  107.1 9.4 %all-to-all-start.3 = ((bf16[8,128,768]{2,1,0:T(8,128)(2,1)}), bf16[8,128,768]{2,1,0:T(8,128)(2,1)S(1)}, u32[]{:S(2)}, u32[]{:S(2)}) async-start(bf16[8,128,768]{2,1,0:T(8,128)(2,1)} %bitcast.27), calls=%async_computation.3 | async-start | bytes 3145728 | tf_op jit(solution)/shard_map/all_to_all | solution.py:320
  117.3 2.0 split.2
  120.8 2.7 %collective-permute-start.2 = (bf16[64,1024]{1,0:T(8,128)(2,1)}, bf16[64,1024]{1,0:T(8,128)(2,1)S(1)}, u32[]{:S(2)}, u32[]{:S(2)}) collective-permute-start(bf16[64,1024]{1,0:T(8,128)(2,1)} %get-tuple-element.59), channel_id=1, source_target_pairs={{0,32},{8,40},{16,48},{24,56},{32,0},{40,8},{48,16},{56,24},{64,96... | collective-permute-start | bytes 393224 | tf_op jit(solution)/shard_map/ppermute | solution.py:325
  124.9 2.0 collective-permute-done.1.refs_1_
  129.3 1.8 add.16.refs_0_
  131.2 3.6 %collective-permute-start.4 = (bf16[64,1024]{1,0:T(8,128)(2,1)}, bf16[64,1024]{1,0:T(8,128)(2,1)S(1)}, u32[]{:S(2)}, u32[]{:S(2)}) collective-permute-start(bf16[64,1024]{1,0:T(8,128)(2,1)} %add.16.refs_0_), channel_id=1, source_target_pairs={{0,64},{8,72},{16,80},{24,88},{32,96},{40,104},{48,112},{56,120},{... | collective-permute-start | bytes 393224 | tf_op jit(solution)/shard_map/ppermute | solution.py:325
  134.8 5.5 %collective-permute-done.4.refs_1_ = bf16[64,1024]{1,0:T(8,128)(2,1)S(1)} collective-permute-done((bf16[64,1024]{1,0:T(8,128)(2,1)}, bf16[64,1024]{1,0:T(8,128)(2,1)S(1)}, u32[]{:S(2)}, u32[]{:S(2)}) %collective-permute-start.4) | collective-permute-done | bytes 131104 | tf_op jit(solution)/shard_map/ppermute | solution.py:325
  142.6 20.9 %attend.5 = (bf16[1024,1408]{1,0:T(8,128)(2,1)}, bf16[256,1024]{1,0:T(8,128)(2,1)}, bf16[256,1024]{1,0:T(8,128)(2,1)}) custom-call(s32[2]{0:T(128)} %pad_add_fusion.refs_0_.place, bf16[1024,1280]{1,0:T(8,128)(2,1)} %bitcast.25, bf16[512,2048]{1,0:T(8,128)(2,1)} %refs_2_.5, bf16[1024,1280]{1,0:T(8,128)(2,1)} %bitcast.26, f32[1024,640]{1,0:T(8,128)} %get-tuple-element.61.refs_4_), custom_call_target="tpu_custom_call" | custom-call | flops 10000000000 | bytes 12000000 | tf_op jit(solution)/shard_map/attend/pallas_call | solution.py:297
  164.7 3.7 %all-to-all-start.4 = ((bf16[8,128,1408]{2,1,0:T(8,128)(2,1)}), bf16[8,128,1408]{2,1,0:T(8,128)(2,1)S(1)}, u32[]{:S(2)}, u32[]{:S(2)}) async-start(bf16[8,128,1408]{2,1,0:T(8,128)(2,1)} %bitcast.21), calls=%async_computation.4 | async-start | bytes 5767168 | tf_op jit(solution)/shard_map/all_to_all | solution.py:320
  168.4 2.1 collective-permute-done.9.got_ref
  171.3 2.0 split.3
  174.8 2.7 %collective-permute-start.11 = (bf16[64,1024]{1,0:T(8,128)(2,1)}, bf16[64,1024]{1,0:T(8,128)(2,1)S(1)}, u32[]{:S(2)}, u32[]{:S(2)}) collective-permute-start(bf16[64,1024]{1,0:T(8,128)(2,1)} %get-tuple-element.75), channel_id=1, source_target_pairs={{0,32},{8,40},{16,48},{24,56},{32,0},{40,8},{48,16},{56,24},{64,96... | collective-permute-start | bytes 393224 | tf_op jit(solution)/shard_map/ppermute | solution.py:325
  179.6 2.6 %collective-permute-start.7 = (bf16[64,1024]{1,0:T(8,128)(2,1)S(1)}, bf16[64,1024]{1,0:T(8,128)(2,1)}, u32[]{:S(2)}, u32[]{:S(2)}) collective-permute-start(bf16[64,1024]{1,0:T(8,128)(2,1)S(1)} %copy-done.8), channel_id=1, source_target_pairs={{0,48},{8,56},{16,0},{24,8},{32,16},{40,24},{48,32},{56,40},{64,11... | collective-permute-start | bytes 393224 | tf_op jit(solution)/shard_map/ppermute | solution.py:325
  182.2 2.4 %collective-permute-start.6 = (bf16[64,1024]{1,0:T(8,128)(2,1)S(1)}, bf16[64,1024]{1,0:T(8,128)(2,1)}, u32[]{:S(2)}, u32[]{:S(2)}) collective-permute-start(bf16[64,1024]{1,0:T(8,128)(2,1)S(1)} %copy-done.8), channel_id=1, source_target_pairs={{0,32},{8,40},{16,48},{24,56},{32,0},{40,8},{48,16},{56,24},{64,96... | collective-permute-start | bytes 393224 | tf_op jit(solution)/shard_map/ppermute | solution.py:325
  185.6 1.8 add.18.refs_0_
  187.4 3.1 %collective-permute-start.13 = (bf16[64,1024]{1,0:T(8,128)(2,1)}, bf16[64,1024]{1,0:T(8,128)(2,1)}, u32[]{:S(2)}, u32[]{:S(2)}) collective-permute-start(bf16[64,1024]{1,0:T(8,128)(2,1)} %add.18.refs_0_), channel_id=1, source_target_pairs={{0,64},{8,72},{16,80},{24,88},{32,96},{40,104},{48,112},{56,120},{... | collective-permute-start | bytes 393224 | tf_op jit(solution)/shard_map/ppermute | solution.py:325
  191.4 11.8 %collective-permute-done.13.refs_1_ = bf16[64,1024]{1,0:T(8,128)(2,1)} collective-permute-done((bf16[64,1024]{1,0:T(8,128)(2,1)}, bf16[64,1024]{1,0:T(8,128)(2,1)}, u32[]{:S(2)}, u32[]{:S(2)}) %collective-permute-start.13) | collective-permute-done | bytes 131104 | tf_op jit(solution)/shard_map/ppermute | solution.py:325
  203.2 1.7 add.19
  204.9 2.7 %collective-permute-start.16 = (bf16[64,1024]{1,0:T(8,128)(2,1)}, bf16[64,1024]{1,0:T(8,128)(2,1)S(1)}, u32[]{:S(2)}, u32[]{:S(2)}) collective-permute-start(bf16[64,1024]{1,0:T(8,128)(2,1)} %add.19), channel_id=1, source_target_pairs={{0,48},{8,56},{16,0},{24,8},{32,16},{40,24},{48,32},{56,40},{64,11... | collective-permute-start | bytes 393224 | tf_op jit(solution)/shard_map/ppermute | solution.py:325
  216.7 2.4 %unpack.2.refs_0_ = bf16[128,12288]{1,0:T(8,128)(2,1)} custom-call(bf16[8,128,768]{2,1,0:T(8,128)(2,1)} %copy-done.1), custom_call_target="tpu_custom_call" | custom-call | bytes 3145728 | tf_op jit(solution)/shard_map/unpack/pallas_call | solution.py:129
  220.8 3.8 %place.1 = f32[512,2048]{1,0:T(8,128)} custom-call(s32[2]{0:T(128)} %pad_add_fusion.refs_0_.place, bf16[256,1024]{1,0:T(8,128)(2,1)} %copy-done.5, bf16[256,1024]{1,0:T(8,128)(2,1)} %copy-done.6, bf16[256,1024]{1,0:T(8,128)(2,1)} %copy-done.4, bf16[256,1024]{1,0:T(8,128)(2,1)} %copy-done.7), custom_call_target="tpu_custom_call" | custom-call | tf_op jit(solution)/shard_map/place/pallas_call | solution.py:390
  226.2 3.2 %unpack.3 = (bf16[128,12288]{1,0:T(8,128)(2,1)}, bf16[576,128]{1,0:T(8,128)(2,1)}) custom-call(bf16[128,12288]{1,0:T(8,128)(2,1)} %unpack.2.refs_0_, bf16[8,128,1408]{2,1,0:T(8,128)(2,1)} %copy-done), custom_call_target="tpu_custom_call", output_to_operand_aliasing={{0}: (0, {})} | custom-call | bytes 3145728 | tf_op jit(solution)/shard_map/unpack/pallas_call | solution.py:129
  (70 shorter events, 30.2 us)
Async XLA Ops:
  4.6 38.5 %all-to-all-start = ((bf16[8,128,1280]{2,1,0:T(8,128)(2,1)}), bf16[8,128,1280]{2,1,0:T(8,128)(2,1)S(1)}, u32[]{:S(2)}, u32[]{:S(2)}) async-start(bf16[8,128,1280]{2,1,0:T(8,128)(2,1)} %pack.3), calls=%async_computation | async-start | bytes 5242880 | tf_op jit(solution)/shard_map/all_to_all | solution.py:320
  43.0 9.5 %copy-start.2 = (bf16[8,128,1280]{2,1,0:T(8,128)(2,1)}, bf16[8,128,1280]{2,1,0:T(8,128)(2,1)S(1)}, u32[]{:S(2)}) copy-start(bf16[8,128,1280]{2,1,0:T(8,128)(2,1)S(1)} %all-to-all-done) | copy-start | bytes 7864324
  43.0 26.3 %all-to-all-start.1 = ((bf16[8,128,640]{2,1,0:T(8,128)(2,1)}), bf16[8,128,640]{2,1,0:T(8,128)(2,1)}, u32[]{:S(2)}, u32[]{:S(2)}) async-start(bf16[8,128,640]{2,1,0:T(8,128)(2,1)} %get-tuple-element.43), calls=%async_computation.1 | async-start | bytes 2621440 | tf_op jit(solution)/shard_map/all_to_all | solution.py:320
  69.3 36.2 %all-to-all-start.2 = ((bf16[8,128,1280]{2,1,0:T(8,128)(2,1)}), bf16[8,128,1280]{2,1,0:T(8,128)(2,1)S(1)}, u32[]{:S(2)}, u32[]{:S(2)}) async-start(bf16[8,128,1280]{2,1,0:T(8,128)(2,1)} %get-tuple-element.48), calls=%async_computation.2 | async-start | bytes 5242880 | tf_op jit(solution)/shard_map/all_to_all | solution.py:320
  85.6 30.8 %collective-permute-start = (bf16[256,1024]{1,0:T(8,128)(2,1)}, bf16[256,1024]{1,0:T(8,128)(2,1)S(1)}, u32[]{:S(2)}, u32[]{:S(2)}) collective-permute-start(bf16[256,1024]{1,0:T(8,128)(2,1)} %get-tuple-element.56), channel_id=1, source_target_pairs={{0,8},{8,0},{16,24},{24,16},{32,40},{40,32},{48,56},{56,48},{64,72... | collective-permute-start | bytes 1572872 | tf_op jit(solution)/shard_map/ppermute | solution.py:325
  105.6 1.5 copy-start.3
  107.1 56.5 %all-to-all-start.3 = ((bf16[8,128,768]{2,1,0:T(8,128)(2,1)}), bf16[8,128,768]{2,1,0:T(8,128)(2,1)S(1)}, u32[]{:S(2)}, u32[]{:S(2)}) async-start(bf16[8,128,768]{2,1,0:T(8,128)(2,1)} %bitcast.27), calls=%async_computation.3 | async-start | bytes 3145728 | tf_op jit(solution)/shard_map/all_to_all | solution.py:320
  119.3 7.6 %collective-permute-start.1 = (bf16[64,1024]{1,0:T(8,128)(2,1)}, bf16[64,1024]{1,0:T(8,128)(2,1)S(1)}, u32[]{:S(2)}, u32[]{:S(2)}) collective-permute-start(bf16[64,1024]{1,0:T(8,128)(2,1)} %get-tuple-element.58), channel_id=1, source_target_pairs={{0,16},{8,24},{16,32},{24,40},{32,48},{40,56},{48,0},{56,8},{64,80... | collective-permute-start | bytes 393224 | tf_op jit(solution)/shard_map/ppermute | solution.py:325
  120.8 7.5 %collective-permute-start.2 = (bf16[64,1024]{1,0:T(8,128)(2,1)}, bf16[64,1024]{1,0:T(8,128)(2,1)S(1)}, u32[]{:S(2)}, u32[]{:S(2)}) collective-permute-start(bf16[64,1024]{1,0:T(8,128)(2,1)} %get-tuple-element.59), channel_id=1, source_target_pairs={{0,32},{8,40},{16,48},{24,56},{32,0},{40,8},{48,16},{56,24},{64,96... | collective-permute-start | bytes 393224 | tf_op jit(solution)/shard_map/ppermute | solution.py:325
  123.5 5.2 %collective-permute-start.3 = (bf16[64,1024]{1,0:T(8,128)(2,1)}, bf16[64,1024]{1,0:T(8,128)(2,1)S(1)}, u32[]{:S(2)}, u32[]{:S(2)}) collective-permute-start(bf16[64,1024]{1,0:T(8,128)(2,1)} %get-tuple-element.60), channel_id=1, source_target_pairs={{0,48},{8,56},{16,0},{24,8},{32,16},{40,24},{48,32},{56,40},{64,11... | collective-permute-start | bytes 393224 | tf_op jit(solution)/shard_map/ppermute | solution.py:325
  126.9 1.8 copy-start.14
  131.2 9.1 %collective-permute-start.4 = (bf16[64,1024]{1,0:T(8,128)(2,1)}, bf16[64,1024]{1,0:T(8,128)(2,1)S(1)}, u32[]{:S(2)}, u32[]{:S(2)}) collective-permute-start(bf16[64,1024]{1,0:T(8,128)(2,1)} %add.16.refs_0_), channel_id=1, source_target_pairs={{0,64},{8,72},{16,80},{24,88},{32,96},{40,104},{48,112},{56,120},{... | collective-permute-start | bytes 393224 | tf_op jit(solution)/shard_map/ppermute | solution.py:325
  163.5 1.1 copy-start.1
  163.6 15.4 %copy-start.8 = (bf16[64,1024]{1,0:T(8,128)(2,1)S(1)}, bf16[64,1024]{1,0:T(8,128)(2,1)}, u32[]{:S(2)}) copy-start(bf16[64,1024]{1,0:T(8,128)(2,1)} %add.17) | copy-start | bytes 393220
  164.7 59.9 %all-to-all-start.4 = ((bf16[8,128,1408]{2,1,0:T(8,128)(2,1)}), bf16[8,128,1408]{2,1,0:T(8,128)(2,1)S(1)}, u32[]{:S(2)}, u32[]{:S(2)}) async-start(bf16[8,128,1408]{2,1,0:T(8,128)(2,1)} %bitcast.21), calls=%async_computation.4 | async-start | bytes 5767168 | tf_op jit(solution)/shard_map/all_to_all | solution.py:320
  168.4 2.2 collective-permute-start.9
  173.4 8.8 %collective-permute-start.10 = (bf16[64,1024]{1,0:T(8,128)(2,1)}, bf16[64,1024]{1,0:T(8,128)(2,1)S(1)}, u32[]{:S(2)}, u32[]{:S(2)}) collective-permute-start(bf16[64,1024]{1,0:T(8,128)(2,1)} %get-tuple-element.74), channel_id=1, source_target_pairs={{0,16},{8,24},{16,32},{24,40},{32,48},{40,56},{48,0},{56,8},{64,80... | collective-permute-start | bytes 393224 | tf_op jit(solution)/shard_map/ppermute | solution.py:325
  174.8 10.1 %collective-permute-start.11 = (bf16[64,1024]{1,0:T(8,128)(2,1)}, bf16[64,1024]{1,0:T(8,128)(2,1)S(1)}, u32[]{:S(2)}, u32[]{:S(2)}) collective-permute-start(bf16[64,1024]{1,0:T(8,128)(2,1)} %get-tuple-element.75), channel_id=1, source_target_pairs={{0,32},{8,40},{16,48},{24,56},{32,0},{40,8},{48,16},{56,24},{64,96... | collective-permute-start | bytes 393224 | tf_op jit(solution)/shard_map/ppermute | solution.py:325
  177.5 7.3 %collective-permute-start.12 = (bf16[64,1024]{1,0:T(8,128)(2,1)}, bf16[64,1024]{1,0:T(8,128)(2,1)S(1)}, u32[]{:S(2)}, u32[]{:S(2)}) collective-permute-start(bf16[64,1024]{1,0:T(8,128)(2,1)} %get-tuple-element.76), channel_id=1, source_target_pairs={{0,48},{8,56},{16,0},{24,8},{32,16},{40,24},{48,32},{56,40},{64,11... | collective-permute-start | bytes 393224 | tf_op jit(solution)/shard_map/ppermute | solution.py:325
  179.0 11.5 %collective-permute-start.5 = (bf16[64,1024]{1,0:T(8,128)(2,1)S(1)}, bf16[64,1024]{1,0:T(8,128)(2,1)}, u32[]{:S(2)}, u32[]{:S(2)}) collective-permute-start(bf16[64,1024]{1,0:T(8,128)(2,1)S(1)} %copy-done.8), channel_id=1, source_target_pairs={{0,16},{8,24},{16,32},{24,40},{32,48},{40,56},{48,0},{56,8},{64,80... | collective-permute-start | bytes 393224 | tf_op jit(solution)/shard_map/ppermute | solution.py:325
  179.6 31.2 %collective-permute-start.7 = (bf16[64,1024]{1,0:T(8,128)(2,1)S(1)}, bf16[64,1024]{1,0:T(8,128)(2,1)}, u32[]{:S(2)}, u32[]{:S(2)}) collective-permute-start(bf16[64,1024]{1,0:T(8,128)(2,1)S(1)} %copy-done.8), channel_id=1, source_target_pairs={{0,48},{8,56},{16,0},{24,8},{32,16},{40,24},{48,32},{56,40},{64,11... | collective-permute-start | bytes 393224 | tf_op jit(solution)/shard_map/ppermute | solution.py:325
  182.2 2.7 %copy-start.11 = (bf16[64,1024]{1,0:T(8,128)(2,1)}, bf16[64,1024]{1,0:T(8,128)(2,1)S(1)}, u32[]{:S(2)}) copy-start(bf16[64,1024]{1,0:T(8,128)(2,1)S(1)} %collective-permute-done.10.refs_1_) | copy-start | bytes 393220
  182.2 27.7 %collective-permute-start.6 = (bf16[64,1024]{1,0:T(8,128)(2,1)S(1)}, bf16[64,1024]{1,0:T(8,128)(2,1)}, u32[]{:S(2)}, u32[]{:S(2)}) collective-permute-start(bf16[64,1024]{1,0:T(8,128)(2,1)S(1)} %copy-done.8), channel_id=1, source_target_pairs={{0,32},{8,40},{16,48},{24,56},{32,0},{40,8},{48,16},{56,24},{64,96... | collective-permute-start | bytes 393224 | tf_op jit(solution)/shard_map/ppermute | solution.py:325
  187.4 15.9 %collective-permute-start.13 = (bf16[64,1024]{1,0:T(8,128)(2,1)}, bf16[64,1024]{1,0:T(8,128)(2,1)}, u32[]{:S(2)}, u32[]{:S(2)}) collective-permute-start(bf16[64,1024]{1,0:T(8,128)(2,1)} %add.18.refs_0_), channel_id=1, source_target_pairs={{0,64},{8,72},{16,80},{24,88},{32,96},{40,104},{48,112},{56,120},{... | collective-permute-start | bytes 393224 | tf_op jit(solution)/shard_map/ppermute | solution.py:325
  204.9 8.0 %collective-permute-start.16 = (bf16[64,1024]{1,0:T(8,128)(2,1)}, bf16[64,1024]{1,0:T(8,128)(2,1)S(1)}, u32[]{:S(2)}, u32[]{:S(2)}) collective-permute-start(bf16[64,1024]{1,0:T(8,128)(2,1)} %add.19), channel_id=1, source_target_pairs={{0,48},{8,56},{16,0},{24,8},{32,16},{40,24},{48,32},{56,40},{64,11... | collective-permute-start | bytes 393224 | tf_op jit(solution)/shard_map/ppermute | solution.py:325
  207.6 6.8 %collective-permute-start.15 = (bf16[64,1024]{1,0:T(8,128)(2,1)}, bf16[64,1024]{1,0:T(8,128)(2,1)S(1)}, u32[]{:S(2)}, u32[]{:S(2)}) collective-permute-start(bf16[64,1024]{1,0:T(8,128)(2,1)} %add.19), channel_id=1, source_target_pairs={{0,32},{8,40},{16,48},{24,56},{32,0},{40,8},{48,16},{56,24},{64,96... | collective-permute-start | bytes 393224 | tf_op jit(solution)/shard_map/ppermute | solution.py:325
  208.5 7.2 %collective-permute-start.14 = (bf16[64,1024]{1,0:T(8,128)(2,1)}, bf16[64,1024]{1,0:T(8,128)(2,1)S(1)}, u32[]{:S(2)}, u32[]{:S(2)}) collective-permute-start(bf16[64,1024]{1,0:T(8,128)(2,1)} %add.19), channel_id=1, source_target_pairs={{0,16},{8,24},{16,32},{24,40},{32,48},{40,56},{48,0},{56,8},{64,80... | collective-permute-start | bytes 393224 | tf_op jit(solution)/shard_map/ppermute | solution.py:325
  211.7 7.4 %copy-start.5 = (bf16[256,1024]{1,0:T(8,128)(2,1)}, bf16[256,1024]{1,0:T(8,128)(2,1)S(1)}, u32[]{:S(2)}) copy-start(bf16[256,1024]{1,0:T(8,128)(2,1)S(1)} %constant_dynamic-update-slice_fusion.refs_0_) | copy-start | bytes 1572868
  211.7 7.4 %collective-permute-start.8 = (bf16[256,1024]{1,0:T(8,128)(2,1)S(1)}, bf16[256,1024]{1,0:T(8,128)(2,1)S(1)}, u32[]{:S(2)}, u32[]{:S(2)}) collective-permute-start(bf16[256,1024]{1,0:T(8,128)(2,1)S(1)} %constant_dynamic-update-slice_fusion.refs_0_), channel_id=1, source_target_pairs={{0,8},{8,0},{16,24},{24,16},{32,40},{40,32},{48,56},{56,48},{64,72... | collective-permute-start | bytes 1572872 | tf_op jit(solution)/shard_map/ppermute | solution.py:325
  216.6 2.5 %copy-start.4 = (bf16[256,1024]{1,0:T(8,128)(2,1)}, bf16[256,1024]{1,0:T(8,128)(2,1)S(1)}, u32[]{:S(2)}) copy-start(bf16[256,1024]{1,0:T(8,128)(2,1)S(1)} %pad_maximum_fusion.refs_2_) | copy-start | bytes 1572868
  216.7 2.5 %collective-permute-start.17 = (bf16[256,1024]{1,0:T(8,128)(2,1)S(1)}, bf16[256,1024]{1,0:T(8,128)(2,1)S(1)}, u32[]{:S(2)}, u32[]{:S(2)}) collective-permute-start(bf16[256,1024]{1,0:T(8,128)(2,1)S(1)} %pad_maximum_fusion.refs_2_), channel_id=1, source_target_pairs={{0,8},{8,0},{16,24},{24,16},{32,40},{40,32},{48,56},{56,48},{64,72... | collective-permute-start | bytes 1572872 | tf_op jit(solution)/shard_map/ppermute | solution.py:325
  224.6 1.5 copy-start
  (9 other events, 6.6 us)

commit v2 on v1

v2 whole, which is shorter than its diff:
```python
import functools

import jax
import jax.numpy as jnp
from jax import lax
from jax.experimental import pallas as pl
from jax.experimental.pallas import tpu as pltpu
from jax.sharding import PartitionSpec as P

NOPE = 128
ROPE = 64
VDIM = 128
LATENT = 512
QPAIR = 2 * (NOPE + ROPE)
GPAIR = 2 * VDIM
PAIR = QPAIR + GPAIR
KVPAIR = 2 * (NOPE + VDIM)
LATPAD = 640
LOG2E = 1.4426950408889634
VMEM = 56 * 1024 * 1024
EARLY = 2
LINE = 4


def dot(a, b, dims):
    return lax.dot_general(a, b, (dims, ((), ())), preferred_element_type=jnp.float32)


def pack_kernel(plans, q_ref, g_ref, lat_ref, *refs):
    count = len(plans)
    outs, held, sems, sent = refs[:count], refs[count : 2 * count], refs[-2], refs[-1]
    groups = outs[0].shape[0]
    per_group = q_ref.shape[1] // (groups * QPAIR)
    batches, number = [], 0
    for n, (first, pairs) in enumerate(plans):
        for j in range(groups):
            batch = []
            at = j * per_group + first
            for ref, width, to in ((q_ref, QPAIR, 0), (g_ref, GPAIR, pairs * QPAIR)):
                batch.append(
                    pltpu.make_async_copy(
                        ref.at[:, at * width : (at + pairs) * width],
                        held[n].at[j, :, to : to + pairs * width],
                        sems.at[number],
                    )
                )
                number += 1
            leave = pltpu.make_async_copy(held[n].at[j], outs[n].at[j], sent.at[n, j])
            batches.append((batch, leave))
    for batch, _ in batches:
        for copy in batch:
            copy.start()
    base = plans[0][1] * PAIR
    rows = lat_ref[...].T
    pad = jnp.zeros((rows.shape[0], LATPAD - rows.shape[1]), rows.dtype)
    rows = jnp.concatenate([rows, pad], axis=1)
    for j in range(groups):
        held[0][j, :, base:] = rows
    for batch, leave in batches:
        for copy in batch:
            copy.wait()
        leave.start()
    for _, leave in batches:
        leave.wait()


def pack(q, g, latents, groups, plans):
    tokens = q.shape[0]
    hbm = pl.BlockSpec(memory_space=pl.ANY)
    shapes = []
    for index, (_, pairs) in enumerate(plans):
        width = pairs * PAIR + (LATPAD if index == 0 else 0)
        shapes.append(jax.ShapeDtypeStruct((groups, tokens, width), q.dtype))
    return pl.pallas_call(
        functools.partial(pack_kernel, plans),
        in_specs=[hbm, hbm, pl.BlockSpec(memory_space=pltpu.VMEM)],
        out_specs=[hbm] * len(plans),
        out_shape=shapes,
        scratch_shapes=[pltpu.VMEM(shape.shape, shape.dtype) for shape in shapes]
        + [
            pltpu.SemaphoreType.DMA((2 * groups * len(plans),)),
            pltpu.SemaphoreType.DMA((len(plans), groups)),
        ],
        compiler_params=pltpu.CompilerParams(vmem_limit_bytes=VMEM),
        cost_estimate=pl.CostEstimate(
            flops=0, bytes_accessed=sum(4 * s.size for s in shapes), transcendentals=0
        ),
        name="pack",
    )(q, g, latents)


def unpack_kernel(plans, *refs):
    count = len(plans)
    parts, out_ref, sems = refs[:count], refs[count], refs[count + 1]
    helds = refs[count + 2 :]
    groups = parts[0].shape[0]
    per_group = out_ref.shape[1] // (groups * QPAIR)
    fetches, copies = [], []
    for n, (first, pairs) in enumerate(plans):
        width = pairs * QPAIR
        for j in range(groups):
            at = (j * per_group + first) * QPAIR
            fetches.append(
                pltpu.make_async_copy(parts[n].at[j], helds[n].at[j], sems.at[0, n, j])
            )
            copies.append(
                pltpu.make_async_copy(
                    helds[n].at[j], out_ref.at[:, at : at + width], sems.at[1, n, j]
                )
            )
    for fetch in fetches:
        fetch.start()
    for fetch, copy in zip(fetches, copies, strict=True):
        fetch.wait()
        copy.start()
    for copy in copies:
        copy.wait()


def unpack(parts, plans, per_group):
    groups, tokens, _ = parts[0].shape
    hbm = pl.BlockSpec(memory_space=pl.ANY)
    size = tokens * groups * per_group * QPAIR
    return pl.pallas_call(
        functools.partial(unpack_kernel, plans),
        in_specs=[hbm] * len(parts),
        out_specs=hbm,
        out_shape=jax.ShapeDtypeStruct((tokens, groups * per_group * QPAIR), parts[0].dtype),
        scratch_shapes=[pltpu.SemaphoreType.DMA((2, len(parts), groups))]
        + [pltpu.VMEM(part.shape, part.dtype) for part in parts],
        compiler_params=pltpu.CompilerParams(vmem_limit_bytes=VMEM),
        cost_estimate=pl.CostEstimate(flops=0, bytes_accessed=4 * size, transcendentals=0),
        name="unpack",
    )(*parts)


def collect_kernel(part_ref, out_ref):
    total = part_ref[0].astype(jnp.float32)
    for j in range(1, part_ref.shape[0]):
        total += part_ref[j].astype(jnp.float32)
    out_ref[...] = total.T[: LATENT + ROPE].astype(out_ref.dtype)


def collect(part):
    shape = jax.ShapeDtypeStruct((LATENT + ROPE, part.shape[1]), part.dtype)
    return pl.pallas_call(collect_kernel, out_shape=shape, name="collect")(part)


def one_head(q_ref, q_at, g_ref, g_at, key, value, dk_ref, dv_ref, scale, block):
    span = key.shape[0]
    dq_rows = []
    for index in reversed(range(span // block)):
        first, limit = index * block, (index + 1) * block
        q = q_ref[first:limit, q_at : q_at + 256]
        g = g_ref[first:limit, g_at : g_at + VDIM]
        keys, values = key[:limit], value[:limit]
        scores = dot(keys, q, ((1,), (1,)))
        key_pos = lax.broadcasted_iota(jnp.int32, (block, block), 0)
        query_pos = lax.broadcasted_iota(jnp.int32, (block, block), 1)
        last = jnp.where(key_pos <= query_pos, scores[first:], -jnp.inf)
        scores = jnp.concatenate([scores[:first], last], axis=0) if index else last
        top = jnp.max(scores, axis=0, keepdims=True)
        expo = jnp.exp2((scores - top) * (scale * LOG2E))
        probs = expo * (1.0 / jnp.sum(expo, axis=0, keepdims=True))
        dprobs = dot(values, g, ((1,), (1,)))
        delta = jnp.sum(probs * dprobs, axis=0, keepdims=True)
        dscores = (probs * (dprobs - delta)).astype(jnp.bfloat16)
        dv = dot(probs.astype(jnp.bfloat16), g, ((1,), (0,)))
        dk = dot(dscores, q, ((1,), (0,)))
        if limit == span:
            dv_ref[...] = dv
            dk_ref[...] = dk
        else:
            dv_ref[:limit] += dv
            dk_ref[:limit] += dk
        dq_rows.append(dot(dscores, keys, ((0,), (0,))))
    return jnp.concatenate(dq_rows[::-1], axis=0)


def attend_kernel(has_sum, *refs):
    refs = list(refs)
    place, lat_ref, w_ref, q_ref, g_ref = refs[:5]
    rest = refs[5:]
    sum_in = rest.pop(0) if has_sum else None
    dq_ref, keep_ref, send_ref, out_ref, total, dk0, dv0, dk1, dv1 = rest
    step = pl.program_id(0)
    scale = (NOPE + ROPE) ** (-0.5)
    half = NOPE // 2
    span = lat_ref.shape[0]
    block = min(256, span)
    plain = lat_ref[:, :LATENT]
    rope = lat_ref[:, LATENT:]
    keyval = dot(plain, w_ref[...], ((1,), (0,)))
    lane = lax.broadcasted_iota(jnp.int32, (span, NOPE), 1)
    key0 = jnp.concatenate([keyval[:, :NOPE].astype(jnp.bfloat16), rope], axis=1)
    value0 = keyval[:, NOPE : 2 * NOPE].astype(jnp.bfloat16)
    moved = pltpu.roll(keyval[:, 2 * NOPE : 3 * NOPE], half, 1)
    rope_moved = pltpu.roll(rope.astype(jnp.float32), half, 1)
    key1 = jnp.concatenate(
        [jnp.where(lane < half, 0.0, moved), jnp.where(lane < half, moved, rope_moved)], axis=1
    ).astype(jnp.bfloat16)
    value1 = keyval[:, 3 * NOPE :].astype(jnp.bfloat16)
    dq0 = one_head(q_ref, 0, g_ref, 0, key0, value0, dk0, dv0, scale, block)
    dq1 = one_head(q_ref, NOPE, g_ref, VDIM, key1, value1, dk1, dv1, scale, block)
    dq = jnp.concatenate([dq0[:, :NOPE], dq0[:, NOPE:] + dq1[:, :NOPE], dq1[:, NOPE:]], axis=1)
    dq = (dq * scale).astype(jnp.bfloat16)
    dq_ref[...] = dq
    left = pltpu.roll(dk1[:, :NOPE], half, 1)
    right = pltpu.roll(dk1[:, NOPE:], half, 1)
    dkeyval = jnp.concatenate(
        [
            dk0[:, :NOPE] * scale,
            dv0[...],
            jnp.where(lane < half, left, right) * scale,
            dv1[...],
        ],
        axis=1,
    ).astype(jnp.bfloat16)
    drope = jnp.where(lane < half, (dk0[:, NOPE:] + right) * scale, 0.0)
    back = dot(dkeyval, w_ref[...], ((1,), (1,)))
    dw = dot(plain, dkeyval, ((0,), (0,))).astype(jnp.bfloat16)
    rows = LATENT // 2 // LINE
    for at in range(2 * LINE):
        to = lax.rem(at % LINE - place[1] + LINE, LINE)
        to = pl.ds(pl.multiple_of(to * rows, rows), rows)
        piece = dw[at * rows : (at + 1) * rows]

        @pl.when(place[0] == at // LINE)
        def _():
            keep_ref[to, :] = piece

        @pl.when(place[0] != at // LINE)
        def _():
            send_ref[to, :] = piece

    @pl.when(step == 0)
    def _():
        if has_sum:
            total[:, :LATENT] = back + sum_in[:, :LATENT]
            total[:, LATENT:] = drope + sum_in[:, LATENT:]
        else:
            total[:, :LATENT] = back
            total[:, LATENT:] = drope

    @pl.when(step > 0)
    def _():
        total[:, :LATENT] += back
        total[:, LATENT:] += drope

    @pl.when(step == pl.num_programs(0) - 1)
    def _():
        out_ref[...] = total[...].astype(out_ref.dtype)


def attend(place, lat, lat_block, weight, first, x, pairs, total, total_type):
    span = lat.shape[0]
    f32, bf16 = jnp.float32, jnp.bfloat16
    whole = lambda j: (0, 0)
    column = lambda j: (0, j)
    specs = [
        pl.BlockSpec(memory_space=pltpu.SMEM),
        pl.BlockSpec((span, LATPAD), lambda j: (0, lat_block)),
        pl.BlockSpec((LATENT, KVPAIR), lambda j: (0, first + j)),
        pl.BlockSpec((span, QPAIR), column),
        pl.BlockSpec((span, GPAIR), lambda j: (0, pairs * QPAIR // GPAIR + j)),
    ]
    args = [place, lat, weight, x, x]
    if total is not None:
        specs.append(pl.BlockSpec((span, LATPAD), whole))
        args.append(total)
    dw_shape = jax.ShapeDtypeStruct((LATENT // 2, pairs * KVPAIR), bf16)
    return pl.pallas_call(
        functools.partial(attend_kernel, total is not None),
        grid=(pairs,),
        in_specs=specs,
        out_specs=[
            pl.BlockSpec((span, QPAIR), column),
            pl.BlockSpec((LATENT // 2, KVPAIR), column),
            pl.BlockSpec((LATENT // 2, KVPAIR), column),
            pl.BlockSpec((span, LATPAD), whole),
        ],
        out_shape=[
            jax.ShapeDtypeStruct((span, pairs * QPAIR), bf16),
            dw_shape,
            dw_shape,
            jax.ShapeDtypeStruct((span, LATPAD), total_type),
        ],
        scratch_shapes=[
            pltpu.VMEM((span, LATPAD), f32),
            pltpu.VMEM((span, 2 * NOPE), f32),
            pltpu.VMEM((span, VDIM), f32),
            pltpu.VMEM((span, 2 * NOPE), f32),
            pltpu.VMEM((span, VDIM), f32),
        ],
        compiler_params=pltpu.CompilerParams(vmem_limit_bytes=VMEM),
        cost_estimate=pl.CostEstimate(
            flops=pairs * 5_000_000_000, bytes_accessed=pairs * 6_000_000, transcendentals=0
        ),
        name="attend",
    )(*args)


def exchange(x, axis, groups=None):
    return lax.all_to_all(x, axis, split_axis=0, concat_axis=0, tiled=True, axis_index_groups=groups)


def send(x, step):
    slabs = lax.axis_size("dp")
    return lax.ppermute(x, "dp", [(i, step(i)) for i in range(slabs)])


def along(step):
    def to(i):
        near = 2 * LINE
        return i // near * near + ((i // 2 + step) % LINE) * 2 + i % 2

    return to


def add_kernel(*refs):
    *parts, out_ref = refs
    total = parts[0][...].astype(jnp.float32)
    for part in parts[1:]:
        total += part[...].astype(jnp.float32)
    out_ref[...] = total.astype(out_ref.dtype)


def add(*parts):
    return pl.pallas_call(add_kernel, out_shape=parts[0], name="add")(*parts)


def split_kernel(keep_ref, got_ref, *out_refs):
    total = keep_ref[...].astype(jnp.float32) + got_ref[...].astype(jnp.float32)
    rows = out_refs[0].shape[0]
    for index, out_ref in enumerate(out_refs):
        out_ref[...] = total[index * rows : (index + 1) * rows].astype(out_ref.dtype)


def split(keep, got):
    shape = jax.ShapeDtypeStruct((keep.shape[0] // LINE, keep.shape[1]), keep.dtype)
    return pl.pallas_call(split_kernel, out_shape=[shape] * LINE, name="split")(keep, got)


def swap(x):
    return send(x, lambda i: i ^ 1)


def spread(pieces):
    return [pieces[0]] + [send(x, along(k + 1)) for k, x in enumerate(pieces[1:])]


def across(part):
    slabs = 4 * LINE
    return send(part, lambda i: (i + slabs // 2) % slabs)


def gather_line(part):
    return jnp.concatenate(spread([part] * LINE), axis=0)


def place_kernel(slabs, place, *refs):
    mine, other, out_ref = refs[-3:]
    rows = mine.shape[0] // LINE
    for ref, core in ((mine, place[0]), (other, 1 - place[0])):
        for k in range(LINE):
            at = core * LINE + lax.rem(place[1] - k + LINE, LINE)
            to = pl.ds(pl.multiple_of(at * rows, rows), rows)
            out_ref[to, :] = ref[k * rows : (k + 1) * rows].astype(jnp.float32) * (1.0 / slabs)


def place_slabs(place, total, mine, other, index, count):
    whole = pl.BlockSpec(mine.shape, lambda j: (0, 0))
    has = total is not None
    return pl.pallas_call(
        functools.partial(place_kernel, lax.axis_size("dp")),
        grid=(1,),
        in_specs=[pl.BlockSpec(memory_space=pltpu.SMEM)]
        + [pl.BlockSpec(memory_space=pl.ANY)] * has
        + [whole, whole],
        out_specs=pl.BlockSpec((LATENT, mine.shape[1]), lambda j: (0, index)),
        out_shape=jax.ShapeDtypeStruct((LATENT, count * mine.shape[1]), jnp.float32),
        input_output_aliases={1: 0} if has else {},
        compiler_params=pltpu.CompilerParams(vmem_limit_bytes=VMEM),
        name="place",
    )(*([place] + [total] * has + [mine, other]))


def after(x, *others):
    return lax.optimization_barrier((x,) + others)


def shards(queries, latents, kv_weight, out_grad):
    groups = lax.axis_size("seq")
    tokens = queries.shape[1]
    span = tokens * groups
    per_group = kv_weight.shape[1] // KVPAIR
    late = per_group - EARLY
    q, g, lat = queries[0], out_grad[0], latents[0].T
    me = lax.axis_index("dp")
    place = jnp.stack([me % 2, me // 2 % LINE]).astype(jnp.int32)

    x0, x1 = pack(q, g, lat, groups, ((0, EARLY), (EARLY, late)))
    got0 = exchange(x0, "seq")
    x1, got0 = after(x1, got0)
    got1 = exchange(x1, "seq")
    lat = got0.reshape(span, got0.shape[2])
    kv = (place, lat, EARLY * PAIR // LATPAD, kv_weight)
    dq0, keep0, give0, total = attend(*kv, 0, lat, EARLY, None, jnp.float32)
    part0 = add(*spread(split(keep0, swap(give0))))
    other0 = across(part0)
    dq0, got1, part0 = after(dq0, got1, part0)
    back0 = exchange(dq0.reshape(groups, tokens, EARLY * QPAIR), "seq")
    dq1, keep1, give1, total = attend(
        *kv, EARLY, got1.reshape(span, -1), late, total, jnp.bfloat16
    )
    dq1, back0, other0 = after(dq1, back0, other0)
    back1 = exchange(dq1.reshape(groups, tokens, late * QPAIR), "seq")
    part0 = add(part0, other0)
    got, keep1, part0 = after(swap(give1), keep1, part0)
    part1 = add(*spread(split(keep1, got)))
    other1 = across(part1)
    mine0 = gather_line(part0)
    total, back1, other1, mine0 = after(total, back1, other1, mine0)
    back2 = exchange(total.reshape(groups, tokens, LATPAD), "seq")
    theirs0 = swap(mine0)
    line1 = spread([add(part1, other1)] * LINE)
    query_grad = unpack([back0, back1], ((0, EARLY), (EARLY, late)), per_group)
    weight_grad = place_slabs(place, None, mine0, theirs0, 0, 2)
    query_grad, weight_grad, *line1 = after(query_grad, weight_grad, *line1)
    mine1 = jnp.concatenate(line1, axis=0)
    weight_grad = place_slabs(place, weight_grad, mine1, swap(mine1), 1, 2)
    latent_grad = collect(back2)
    return (query_grad[None], latent_grad.T[None], weight_grad)


def solution(mesh):
    placed = (P("dp", "seq", None), P("dp", "seq", None), P(None, "seq"), P("dp", "seq", None))
    return jax.shard_map(
        shards,
        mesh=mesh,
        in_specs=placed,
        out_specs=(P("dp", "seq", None), P("dp", "seq", None), P(None, "seq")),
        check_vma=False,
    )
```

time: 233 us -> 194 us (0.83)
  waiting for transfers between devices: 80.5 us -> 19.9 us
  blocking collectives: 0 us -> 52.8 us
  starting transfers between devices: 60.5 us -> 42.5 us
  local copies, waits for them, and re-layouts: 12.2 us -> 5.67 us
  Pallas kernels: 73.8 us -> 68.9 us
    all_to_all x5 -> x4, waiting for transfers between devices: 53.1 us -> 0.01 us  [exchange(): lax.all_to_all(x, axis, split_axis=0, concat_axis=0, tiled=True, axis_ind...]
    all_to_all x0 -> x1, blocking collectives: none -> 52.8 us  [exchange(): lax.all_to_all(x, axis, split_axis=0, concat_axis=0, tiled=True, axis_ind...]
    all_to_all x5 -> x4, starting transfers between devices: 31.7 us -> 19.8 us  [exchange(): lax.all_to_all(x, axis, split_axis=0, concat_axis=0, tiled=True, axis_ind...]
    ppermute x18, waiting for transfers between devices: 27.4 us -> 19.9 us  [send(): return lax.ppermute(x, 'dp', [(i, step(i)) for i in range(slabs)])]
    ppermute x18, starting transfers between devices: 28.8 us -> 22.7 us  [send(): return lax.ppermute(x, 'dp', [(i, step(i)) for i in range(slabs)])]
    unnamed x39, local copies, waits for them, and re-layouts: 11.2 us -> 5.65 us
    pallas_call x8 -> x7, Pallas kernels: 62.9 us -> 57.9 us  [the longest x2 40.9 us: attend(): pl.pallas_call(functools.partial(attend_kernel, total is not None), grid=...]
  transfers between devices with their start and end apart: 23 -> 22, of which waited for: 13 -> 11; matrix products, arithmetic and copies ran while one was open for 2% -> 1% of each run, Pallas kernels for 29% -> 31%
where the time goes in v2:
time: 194 us; the launch traced here: 192 us
  Pallas kernels  68.9 us (36%)
  blocking collectives  52.8 us (27%)
  starting transfers between devices  42.5 us (22%)
  waiting for transfers between devices  19.9 us (10%)
  local copies, waits for them, and re-layouts  5.67 us (3%)
    all_to_all x1, blocking collectives, exchange(): lax.all_to_all(x, axis, split_axis=0, concat_axis=0, tiled=True, axis_ind...  52.8 us
    pallas_call x2, Pallas kernels, attend(): pl.pallas_call(functools.partial(attend_kernel, total is not None), grid=...  40.9 us
    ppermute x18, starting transfers between devices, send(): return lax.ppermute(x, 'dp', [(i, step(i)) for i in range(slabs)])  22.7 us
    ppermute x18, waiting for transfers between devices, send(): return lax.ppermute(x, 'dp', [(i, step(i)) for i in range(slabs)])  19.9 us
    all_to_all x4, starting transfers between devices, exchange(): lax.all_to_all(x, axis, split_axis=0, concat_axis=0, tiled=True, axis_ind...  19.8 us
    pallas_call x4, Pallas kernels, add(): return pl.pallas_call(add_kernel, out_shape=parts[0], name='add')(*parts)  6.95 us
    pallas_call x1, Pallas kernels, pack(): pl.pallas_call(functools.partial(pack_kernel, plans), in_specs=[hbm, hbm,...  6.31 us
    unnamed x39, local copies, waits for them, and re-layouts  5.65 us
  transfers between devices with their start and end apart: 22, of which 11 were waited for; matrix products, arithmetic and copies ran while one was open for 1% of the time, Pallas kernels for 31%

profile of v2, /device:TPU:0, one launch (start us, length us, event | category | flops | bytes accessed | tf_op | source)
XLA Modules:
  0.0 192.3 jit_solution(5682046621387056243)
XLA Ops:
  0.6 6.3 %pack.1 = (bf16[8,128,1920]{2,1,0:T(8,128)(2,1)}, bf16[8,128,1280]{2,1,0:T(8,128)(2,1)}) custom-call(bf16[128,12288]{1,0:T(8,128)(2,1)} %bitcast.21, bf16[128,8192]{1,0:T(8,128)(2,1)} %bitcast.24, bf16[576,128]{1,0:T(8,128)(2,1)} %bitcast.29), custom_call_target="tpu_custom_call" | custom-call | bytes 13107200 | tf_op jit(solution)/shard_map/pack/pallas_call | solution.py:74
  6.9 52.8 %all_to_all.25 = bf16[8,128,1920]{2,1,0:T(8,128)(2,1)} all-to-all(bf16[8,128,1920]{2,1,0:T(8,128)(2,1)} %get-tuple-element.43), channel_id=1, replica_groups=mesh['dp'=16,'seq'=8] {'seq'}, dimensions={0} | all-to-all | bytes 7864320 | tf_op jit(solution)/shard_map/all_to_all | solution.py:304
  59.7 3.6 %all-to-all-start.1 = ((bf16[8,128,1280]{2,1,0:T(8,128)(2,1)}), bf16[8,128,1280]{2,1,0:T(8,128)(2,1)S(1)}, u32[]{:S(2)}, u32[]{:S(2)}) async-start(bf16[8,128,1280]{2,1,0:T(8,128)(2,1)} %get-tuple-element.46), calls=%async_computation.1 | async-start | bytes 5242880 | tf_op jit(solution)/shard_map/all_to_all | solution.py:304
  64.0 20.1 %attend.2 = (bf16[1024,768]{1,0:T(8,128)(2,1)}, bf16[256,1024]{1,0:T(8,128)(2,1)}, bf16[256,1024]{1,0:T(8,128)(2,1)}, f32[1024,640]{1,0:T(8,128)}) custom-call(s32[2]{0:T(128)} %pad_add_fusion.refs_0_.place, bf16[1024,1920]{1,0:T(8,128)(2,1)} %bitcast.16, bf16[512,2048]{1,0:T(8,128)(2,1)} %refs_2_.3, bf16[1024,1920]{1,0:T(8,128)(2,1)} %bitcast.17, ...), custom_call_target="tpu_custom_call" | custom-call | flops 10000000000 | bytes 12000000 | tf_op jit(solution)/shard_map/attend/pallas_call | solution.py:272
  84.2 2.1 %collective-permute-done.got_ref = bf16[256,1024]{1,0:T(8,128)(2,1)S(1)} collective-permute-done((bf16[256,1024]{1,0:T(8,128)(2,1)}, bf16[256,1024]{1,0:T(8,128)(2,1)S(1)}, u32[]{:S(2)}, u32[]{:S(2)}) %collective-permute-start) | collective-permute-done | bytes 524320 | tf_op jit(solution)/shard_map/ppermute | solution.py:309
  87.1 2.0 %split.2 = (bf16[64,1024]{1,0:T(8,128)(2,1)}, bf16[64,1024]{1,0:T(8,128)(2,1)}, bf16[64,1024]{1,0:T(8,128)(2,1)}, bf16[64,1024]{1,0:T(8,128)(2,1)}) custom-call(bf16[256,1024]{1,0:T(8,128)(2,1)} %get-tuple-element.47.keep_ref, bf16[256,1024]{1,0:T(8,128)(2,1)} %copy-done.9), custom_call_target="tpu_custom_call" | custom-call | tf_op jit(solution)/shard_map/split/pallas_call | solution.py:341
  89.1 1.5 collective-permute-start.1
  90.6 2.7 %collective-permute-start.2 = (bf16[64,1024]{1,0:T(8,128)(2,1)}, bf16[64,1024]{1,0:T(8,128)(2,1)S(1)}, u32[]{:S(2)}, u32[]{:S(2)}) collective-permute-start(bf16[64,1024]{1,0:T(8,128)(2,1)} %get-tuple-element.51), channel_id=1, source_target_pairs={{0,32},{8,40},{16,48},{24,56},{32,0},{40,8},{48,16},{56,24},{64,96... | collective-permute-start | bytes 393224 | tf_op jit(solution)/shard_map/ppermute | solution.py:309
  96.1 3.8 %collective-permute-done.2.refs_2_ = bf16[64,1024]{1,0:T(8,128)(2,1)S(1)} collective-permute-done((bf16[64,1024]{1,0:T(8,128)(2,1)}, bf16[64,1024]{1,0:T(8,128)(2,1)S(1)}, u32[]{:S(2)}, u32[]{:S(2)}) %collective-permute-start.2) | collective-permute-done | bytes 131104 | tf_op jit(solution)/shard_map/ppermute | solution.py:309
  100.6 1.8 add.16.refs_0_
  102.4 1.5 copy-done.3
  103.9 5.6 %all-to-all-start.2 = ((bf16[8,128,768]{2,1,0:T(8,128)(2,1)}), bf16[8,128,768]{2,1,0:T(8,128)(2,1)S(1)}, u32[]{:S(2)}, u32[]{:S(2)}) async-start(bf16[8,128,768]{2,1,0:T(8,128)(2,1)} %bitcast.26), calls=%async_computation.2 | async-start | bytes 3145728 | tf_op jit(solution)/shard_map/all_to_all | solution.py:304
  109.5 3.8 %collective-permute-start.4 = (bf16[64,1024]{1,0:T(8,128)(2,1)S(1)}, bf16[64,1024]{1,0:T(8,128)(2,1)S(1)}, u32[]{:S(2)}, u32[]{:S(2)}) collective-permute-start(bf16[64,1024]{1,0:T(8,128)(2,1)S(1)} %copy-done.7), channel_id=1, source_target_pairs={{0,64},{8,72},{16,80},{24,88},{32,96},{40,104},{48,112},{56,120},{... | collective-permute-start | bytes 393224 | tf_op jit(solution)/shard_map/ppermute | solution.py:309
  113.4 20.7 %attend.3 = (bf16[1024,768]{1,0:T(8,128)(2,1)}, bf16[256,1024]{1,0:T(8,128)(2,1)}, bf16[256,1024]{1,0:T(8,128)(2,1)}, bf16[1024,640]{1,0:T(8,128)(2,1)}) custom-call(s32[2]{0:T(128)} %pad_add_fusion.refs_0_.place, bf16[1024,1920]{1,0:T(8,128)(2,1)} %bitcast.19, bf16[512,2048]{1,0:T(8,128)(2,1)} %refs_2_.3, bf16[1024,1280]{1,0:T(8,128)(2,1)} %bitcast.22, ...), custom_call_target="tpu_custom_call" | custom-call | flops 10000000000 | bytes 12000000 | tf_op jit(solution)/shard_map/attend/pallas_call | solution.py:272
  134.2 4.9 %all-to-all-start.3 = ((bf16[8,128,768]{2,1,0:T(8,128)(2,1)}), bf16[8,128,768]{2,1,0:T(8,128)(2,1)S(1)}, u32[]{:S(2)}, u32[]{:S(2)}) async-start(bf16[8,128,768]{2,1,0:T(8,128)(2,1)} %bitcast.25), calls=%async_computation.3 | async-start | bytes 3145728 | tf_op jit(solution)/shard_map/all_to_all | solution.py:304
  139.0 1.7 add.17
  141.3 2.0 %split.3 = (bf16[64,1024]{1,0:T(8,128)(2,1)}, bf16[64,1024]{1,0:T(8,128)(2,1)}, bf16[64,1024]{1,0:T(8,128)(2,1)}, bf16[64,1024]{1,0:T(8,128)(2,1)}) custom-call(bf16[256,1024]{1,0:T(8,128)(2,1)} %get-tuple-element.64.keep_ref, bf16[256,1024]{1,0:T(8,128)(2,1)} %collective-permute-done.5.got_ref), custom_call_target="tpu_custom_call" | custom-call | tf_op jit(solution)/shard_map/split/pallas_call | solution.py:341
  144.6 2.4 %collective-permute-start.7 = (bf16[64,1024]{1,0:T(8,128)(2,1)}, bf16[64,1024]{1,0:T(8,128)(2,1)S(1)}, u32[]{:S(2)}, u32[]{:S(2)}) collective-permute-start(bf16[64,1024]{1,0:T(8,128)(2,1)} %get-tuple-element.68), channel_id=1, source_target_pairs={{0,32},{8,40},{16,48},{24,56},{32,0},{40,8},{48,16},{56,24},{64,96... | collective-permute-start | bytes 393224 | tf_op jit(solution)/shard_map/ppermute | solution.py:309
  146.9 1.6 collective-permute-start.8
  148.7 2.4 %collective-permute-start.11 = (bf16[64,1024]{1,0:T(8,128)(2,1)}, bf16[64,1024]{1,0:T(8,128)(2,1)}, u32[]{:S(2)}, u32[]{:S(2)}) collective-permute-start(bf16[64,1024]{1,0:T(8,128)(2,1)} %add.17), channel_id=1, source_target_pairs={{0,32},{8,40},{16,48},{24,56},{32,0},{40,8},{48,16},{56,24},{64,96... | collective-permute-start | bytes 393224 | tf_op jit(solution)/shard_map/ppermute | solution.py:309
  151.1 3.3 %collective-permute-done.7.refs_2_ = bf16[64,1024]{1,0:T(8,128)(2,1)S(1)} collective-permute-done((bf16[64,1024]{1,0:T(8,128)(2,1)}, bf16[64,1024]{1,0:T(8,128)(2,1)S(1)}, u32[]{:S(2)}, u32[]{:S(2)}) %collective-permute-start.7) | collective-permute-done | bytes 131104 | tf_op jit(solution)/shard_map/ppermute | solution.py:309
  155.4 1.8 add.18.refs_0_
  160.3 3.6 %collective-permute-done.9.refs_1_ = bf16[64,1024]{1,0:T(8,128)(2,1)S(1)} collective-permute-done((bf16[64,1024]{1,0:T(8,128)(2,1)}, bf16[64,1024]{1,0:T(8,128)(2,1)S(1)}, u32[]{:S(2)}, u32[]{:S(2)}) %collective-permute-start.9) | collective-permute-done | bytes 131104 | tf_op jit(solution)/shard_map/ppermute | solution.py:309
  164.0 5.7 %all-to-all-start.4 = ((bf16[8,128,640]{2,1,0:T(8,128)(2,1)}), bf16[8,128,640]{2,1,0:T(8,128)(2,1)S(1)}, u32[]{:S(2)}, u32[]{:S(2)}) async-start(bf16[8,128,640]{2,1,0:T(8,128)(2,1)} %bitcast.27), calls=%async_computation.4 | async-start | bytes 2621440 | tf_op jit(solution)/shard_map/all_to_all | solution.py:304
  169.7 1.7 add.19
  171.4 2.2 %collective-permute-start.16 = (bf16[64,1024]{1,0:T(8,128)(2,1)}, bf16[64,1024]{1,0:T(8,128)(2,1)S(1)}, u32[]{:S(2)}, u32[]{:S(2)}) collective-permute-start(bf16[64,1024]{1,0:T(8,128)(2,1)} %add.19), channel_id=1, source_target_pairs={{0,48},{8,56},{16,0},{24,8},{32,16},{40,24},{48,32},{56,40},{64,11... | collective-permute-start | bytes 393224 | tf_op jit(solution)/shard_map/ppermute | solution.py:309
  175.4 3.2 %unpack.1 = bf16[128,12288]{1,0:T(8,128)(2,1)} custom-call(bf16[8,128,768]{2,1,0:T(8,128)(2,1)} %copy-done, bf16[8,128,768]{2,1,0:T(8,128)(2,1)} %copy-done.1), custom_call_target="tpu_custom_call" | custom-call | bytes 6291456 | tf_op jit(solution)/shard_map/unpack/pallas_call | solution.py:124
  178.6 2.7 %place.2.refs_0_ = f32[512,2048]{1,0:T(8,128)} custom-call(s32[2]{0:T(128)} %pad_add_fusion.refs_0_.place, bf16[256,1024]{1,0:T(8,128)(2,1)} %copy-done.4, bf16[256,1024]{1,0:T(8,128)(2,1)} %collective-permute-done.13.refs_1_), custom_call_target="tpu_custom_call" | custom-call | tf_op jit(solution)/shard_map/place/pallas_call | solution.py:374
  181.6 1.8 collective-permute-done.14
  183.6 1.9 collective-permute-done.17.refs_2_
  186.3 2.7 %place.3 = f32[512,2048]{1,0:T(8,128)} custom-call(s32[2]{0:T(128)} %pad_add_fusion.refs_0_.place, f32[512,2048]{1,0:T(8,128)} %place.2.refs_0_, bf16[256,1024]{1,0:T(8,128)(2,1)} %copy-done.5, bf16[256,1024]{1,0:T(8,128)(2,1)} %copy-done.6), custom_call_target="tpu_custom_call", output_to_operand_aliasing={{}: (1, {})} | custom-call | tf_op jit(solution)/shard_map/place/pallas_call | solution.py:374
  190.1 2.2 %collect.1 = bf16[576,128]{1,0:T(8,128)(2,1)} custom-call(bf16[8,128,640]{2,1,0:T(8,128)(2,1)} %copy-done.2), custom_call_target="tpu_custom_call" | custom-call | tf_op jit(solution)/shard_map/collect/pallas_call | solution.py:146
  (68 shorter events, 15.4 us)
Async XLA Ops:
  59.7 42.7 %all-to-all-start.1 = ((bf16[8,128,1280]{2,1,0:T(8,128)(2,1)}), bf16[8,128,1280]{2,1,0:T(8,128)(2,1)S(1)}, u32[]{:S(2)}, u32[]{:S(2)}) async-start(bf16[8,128,1280]{2,1,0:T(8,128)(2,1)} %get-tuple-element.46), calls=%async_computation.1 | async-start | bytes 5242880 | tf_op jit(solution)/shard_map/all_to_all | solution.py:304
  84.1 2.2 %collective-permute-start = (bf16[256,1024]{1,0:T(8,128)(2,1)}, bf16[256,1024]{1,0:T(8,128)(2,1)S(1)}, u32[]{:S(2)}, u32[]{:S(2)}) collective-permute-start(bf16[256,1024]{1,0:T(8,128)(2,1)} %get-tuple-element.48), channel_id=1, source_target_pairs={{0,8},{8,0},{16,24},{24,16},{32,40},{40,32},{48,56},{56,48},{64,72... | collective-permute-start | bytes 1572872 | tf_op jit(solution)/shard_map/ppermute | solution.py:309
  89.1 7.0 %collective-permute-start.1 = (bf16[64,1024]{1,0:T(8,128)(2,1)}, bf16[64,1024]{1,0:T(8,128)(2,1)S(1)}, u32[]{:S(2)}, u32[]{:S(2)}) collective-permute-start(bf16[64,1024]{1,0:T(8,128)(2,1)} %get-tuple-element.50), channel_id=1, source_target_pairs={{0,16},{8,24},{16,32},{24,40},{32,48},{40,56},{48,0},{56,8},{64,80... | collective-permute-start | bytes 393224 | tf_op jit(solution)/shard_map/ppermute | solution.py:309
  90.6 9.3 %collective-permute-start.2 = (bf16[64,1024]{1,0:T(8,128)(2,1)}, bf16[64,1024]{1,0:T(8,128)(2,1)S(1)}, u32[]{:S(2)}, u32[]{:S(2)}) collective-permute-start(bf16[64,1024]{1,0:T(8,128)(2,1)} %get-tuple-element.51), channel_id=1, source_target_pairs={{0,32},{8,40},{16,48},{24,56},{32,0},{40,8},{48,16},{56,24},{64,96... | collective-permute-start | bytes 393224 | tf_op jit(solution)/shard_map/ppermute | solution.py:309
  93.4 6.5 %collective-permute-start.3 = (bf16[64,1024]{1,0:T(8,128)(2,1)}, bf16[64,1024]{1,0:T(8,128)(2,1)S(1)}, u32[]{:S(2)}, u32[]{:S(2)}) collective-permute-start(bf16[64,1024]{1,0:T(8,128)(2,1)} %get-tuple-element.52), channel_id=1, source_target_pairs={{0,48},{8,56},{16,0},{24,8},{32,16},{40,24},{48,32},{56,40},{64,11... | collective-permute-start | bytes 393224 | tf_op jit(solution)/shard_map/ppermute | solution.py:309
  96.1 3.8 %copy-start.15 = (bf16[64,1024]{1,0:T(8,128)(2,1)}, bf16[64,1024]{1,0:T(8,128)(2,1)S(1)}, u32[]{:S(2)}) copy-start(bf16[64,1024]{1,0:T(8,128)(2,1)S(1)} %collective-permute-done.1.refs_1_) | copy-start | bytes 393220
  102.4 7.1 %copy-start.7 = (bf16[64,1024]{1,0:T(8,128)(2,1)S(1)}, bf16[64,1024]{1,0:T(8,128)(2,1)}, u32[]{:S(2)}) copy-start(bf16[64,1024]{1,0:T(8,128)(2,1)} %add.16.refs_0_) | copy-start | bytes 393220
  103.9 30.2 %all-to-all-start.2 = ((bf16[8,128,768]{2,1,0:T(8,128)(2,1)}), bf16[8,128,768]{2,1,0:T(8,128)(2,1)S(1)}, u32[]{:S(2)}, u32[]{:S(2)}) async-start(bf16[8,128,768]{2,1,0:T(8,128)(2,1)} %bitcast.26), calls=%async_computation.2 | async-start | bytes 3145728 | tf_op jit(solution)/shard_map/all_to_all | solution.py:304
  109.5 24.6 %collective-permute-start.4 = (bf16[64,1024]{1,0:T(8,128)(2,1)S(1)}, bf16[64,1024]{1,0:T(8,128)(2,1)S(1)}, u32[]{:S(2)}, u32[]{:S(2)}) collective-permute-start(bf16[64,1024]{1,0:T(8,128)(2,1)S(1)} %copy-done.7), channel_id=1, source_target_pairs={{0,64},{8,72},{16,80},{24,88},{32,96},{40,104},{48,112},{56,120},{... | collective-permute-start | bytes 393224 | tf_op jit(solution)/shard_map/ppermute | solution.py:309
  134.1 4.9 %copy-start.14 = (bf16[64,1024]{1,0:T(8,128)(2,1)}, bf16[64,1024]{1,0:T(8,128)(2,1)S(1)}, u32[]{:S(2)}) copy-start(bf16[64,1024]{1,0:T(8,128)(2,1)S(1)} %collective-permute-done.4.refs_1_) | copy-start | bytes 393220
  134.1 23.1 %copy-start = (bf16[8,128,768]{2,1,0:T(8,128)(2,1)}, bf16[8,128,768]{2,1,0:T(8,128)(2,1)S(1)}, u32[]{:S(2)}) copy-start(bf16[8,128,768]{2,1,0:T(8,128)(2,1)S(1)} %all-to-all-done.2.refs_0_) | copy-start | bytes 4718596
  134.2 29.8 %all-to-all-start.3 = ((bf16[8,128,768]{2,1,0:T(8,128)(2,1)}), bf16[8,128,768]{2,1,0:T(8,128)(2,1)S(1)}, u32[]{:S(2)}, u32[]{:S(2)}) async-start(bf16[8,128,768]{2,1,0:T(8,128)(2,1)} %bitcast.25), calls=%async_computation.3 | async-start | bytes 3145728 | tf_op jit(solution)/shard_map/all_to_all | solution.py:304
  139.0 2.3 %collective-permute-start.5 = (bf16[256,1024]{1,0:T(8,128)(2,1)}, bf16[256,1024]{1,0:T(8,128)(2,1)}, u32[]{:S(2)}, u32[]{:S(2)}) collective-permute-start(bf16[256,1024]{1,0:T(8,128)(2,1)} %get-tuple-element.60), channel_id=1, source_target_pairs={{0,8},{8,0},{16,24},{24,16},{32,40},{40,32},{48,56},{56,48},{64,72... | collective-permute-start | bytes 1572872 | tf_op jit(solution)/shard_map/ppermute | solution.py:309
  143.3 7.8 %collective-permute-start.6 = (bf16[64,1024]{1,0:T(8,128)(2,1)}, bf16[64,1024]{1,0:T(8,128)(2,1)S(1)}, u32[]{:S(2)}, u32[]{:S(2)}) collective-permute-start(bf16[64,1024]{1,0:T(8,128)(2,1)} %get-tuple-element.67), channel_id=1, source_target_pairs={{0,16},{8,24},{16,32},{24,40},{32,48},{40,56},{48,0},{56,8},{64,80... | collective-permute-start | bytes 393224 | tf_op jit(solution)/shard_map/ppermute | solution.py:309
  144.6 9.8 %collective-permute-start.7 = (bf16[64,1024]{1,0:T(8,128)(2,1)}, bf16[64,1024]{1,0:T(8,128)(2,1)S(1)}, u32[]{:S(2)}, u32[]{:S(2)}) collective-permute-start(bf16[64,1024]{1,0:T(8,128)(2,1)} %get-tuple-element.68), channel_id=1, source_target_pairs={{0,32},{8,40},{16,48},{24,56},{32,0},{40,8},{48,16},{56,24},{64,96... | collective-permute-start | bytes 393224 | tf_op jit(solution)/shard_map/ppermute | solution.py:309
  146.9 7.8 %collective-permute-start.8 = (bf16[64,1024]{1,0:T(8,128)(2,1)}, bf16[64,1024]{1,0:T(8,128)(2,1)S(1)}, u32[]{:S(2)}, u32[]{:S(2)}) collective-permute-start(bf16[64,1024]{1,0:T(8,128)(2,1)} %get-tuple-element.69), channel_id=1, source_target_pairs={{0,48},{8,56},{16,0},{24,8},{32,16},{40,24},{48,32},{56,40},{64,11... | collective-permute-start | bytes 393224 | tf_op jit(solution)/shard_map/ppermute | solution.py:309
  148.5 9.9 %collective-permute-start.12 = (bf16[64,1024]{1,0:T(8,128)(2,1)}, bf16[64,1024]{1,0:T(8,128)(2,1)}, u32[]{:S(2)}, u32[]{:S(2)}) collective-permute-start(bf16[64,1024]{1,0:T(8,128)(2,1)} %add.17), channel_id=1, source_target_pairs={{0,48},{8,56},{16,0},{24,8},{32,16},{40,24},{48,32},{56,40},{64,11... | collective-permute-start | bytes 393224 | tf_op jit(solution)/shard_map/ppermute | solution.py:309
  148.7 9.7 %collective-permute-start.11 = (bf16[64,1024]{1,0:T(8,128)(2,1)}, bf16[64,1024]{1,0:T(8,128)(2,1)}, u32[]{:S(2)}, u32[]{:S(2)}) collective-permute-start(bf16[64,1024]{1,0:T(8,128)(2,1)} %add.17), channel_id=1, source_target_pairs={{0,32},{8,40},{16,48},{24,56},{32,0},{40,8},{48,16},{56,24},{64,96... | collective-permute-start | bytes 393224 | tf_op jit(solution)/shard_map/ppermute | solution.py:309
  151.0 3.7 %copy-start.10 = (bf16[64,1024]{1,0:T(8,128)(2,1)}, bf16[64,1024]{1,0:T(8,128)(2,1)S(1)}, u32[]{:S(2)}) copy-start(bf16[64,1024]{1,0:T(8,128)(2,1)S(1)} %collective-permute-done.6.refs_1_) | copy-start | bytes 393220
  151.0 8.2 %collective-permute-start.10 = (bf16[64,1024]{1,0:T(8,128)(2,1)}, bf16[64,1024]{1,0:T(8,128)(2,1)}, u32[]{:S(2)}, u32[]{:S(2)}) collective-permute-start(bf16[64,1024]{1,0:T(8,128)(2,1)} %add.17), channel_id=1, source_target_pairs={{0,16},{8,24},{16,32},{24,40},{32,48},{40,56},{48,0},{56,8},{64,80... | collective-permute-start | bytes 393224 | tf_op jit(solution)/shard_map/ppermute | solution.py:309
  157.2 6.7 %collective-permute-start.9 = (bf16[64,1024]{1,0:T(8,128)(2,1)}, bf16[64,1024]{1,0:T(8,128)(2,1)S(1)}, u32[]{:S(2)}, u32[]{:S(2)}) collective-permute-start(bf16[64,1024]{1,0:T(8,128)(2,1)} %add.18.refs_0_), channel_id=1, source_target_pairs={{0,64},{8,72},{16,80},{24,88},{32,96},{40,104},{48,112},{56,120},{... | collective-permute-start | bytes 393224 | tf_op jit(solution)/shard_map/ppermute | solution.py:309
  160.3 18.3 %copy-start.4 = (bf16[256,1024]{1,0:T(8,128)(2,1)}, bf16[256,1024]{1,0:T(8,128)(2,1)S(1)}, u32[]{:S(2)}) copy-start(bf16[256,1024]{1,0:T(8,128)(2,1)S(1)} %pad_maximum_fusion.refs_0_) | copy-start | bytes 1572868
  163.9 5.8 %copy-start.11 = (bf16[64,1024]{1,0:T(8,128)(2,1)}, bf16[64,1024]{1,0:T(8,128)(2,1)S(1)}, u32[]{:S(2)}) copy-start(bf16[64,1024]{1,0:T(8,128)(2,1)S(1)} %collective-permute-done.9.refs_1_) | copy-start | bytes 393220
  163.9 11.5 %copy-start.1 = (bf16[8,128,768]{2,1,0:T(8,128)(2,1)}, bf16[8,128,768]{2,1,0:T(8,128)(2,1)S(1)}, u32[]{:S(2)}) copy-start(bf16[8,128,768]{2,1,0:T(8,128)(2,1)S(1)} %all-to-all-done.3.refs_1_) | copy-start | bytes 4718596
  163.9 14.7 %collective-permute-start.13 = (bf16[256,1024]{1,0:T(8,128)(2,1)S(1)}, bf16[256,1024]{1,0:T(8,128)(2,1)}, u32[]{:S(2)}, u32[]{:S(2)}) collective-permute-start(bf16[256,1024]{1,0:T(8,128)(2,1)S(1)} %pad_maximum_fusion.refs_0_), channel_id=1, source_target_pairs={{0,8},{8,0},{16,24},{24,16},{32,40},{40,32},{48,56},{56,48},{64,72... | collective-permute-start | bytes 1572872 | tf_op jit(solution)/shard_map/ppermute | solution.py:309
  164.0 25.0 %all-to-all-start.4 = ((bf16[8,128,640]{2,1,0:T(8,128)(2,1)}), bf16[8,128,640]{2,1,0:T(8,128)(2,1)S(1)}, u32[]{:S(2)}, u32[]{:S(2)}) async-start(bf16[8,128,640]{2,1,0:T(8,128)(2,1)} %bitcast.27), calls=%async_computation.4 | async-start | bytes 2621440 | tf_op jit(solution)/shard_map/all_to_all | solution.py:304
  171.4 9.9 %collective-permute-start.16 = (bf16[64,1024]{1,0:T(8,128)(2,1)}, bf16[64,1024]{1,0:T(8,128)(2,1)S(1)}, u32[]{:S(2)}, u32[]{:S(2)}) collective-permute-start(bf16[64,1024]{1,0:T(8,128)(2,1)} %add.19), channel_id=1, source_target_pairs={{0,48},{8,56},{16,0},{24,8},{32,16},{40,24},{48,32},{56,40},{64,11... | collective-permute-start | bytes 393224 | tf_op jit(solution)/shard_map/ppermute | solution.py:309
  173.6 8.1 %collective-permute-start.15 = (bf16[64,1024]{1,0:T(8,128)(2,1)}, bf16[64,1024]{1,0:T(8,128)(2,1)S(1)}, u32[]{:S(2)}, u32[]{:S(2)}) collective-permute-start(bf16[64,1024]{1,0:T(8,128)(2,1)} %add.19), channel_id=1, source_target_pairs={{0,32},{8,40},{16,48},{24,56},{32,0},{40,8},{48,16},{56,24},{64,96... | collective-permute-start | bytes 393224 | tf_op jit(solution)/shard_map/ppermute | solution.py:309
  174.4 9.0 %collective-permute-start.14 = (bf16[64,1024]{1,0:T(8,128)(2,1)}, bf16[64,1024]{1,0:T(8,128)(2,1)S(1)}, u32[]{:S(2)}, u32[]{:S(2)}) collective-permute-start(bf16[64,1024]{1,0:T(8,128)(2,1)} %add.19), channel_id=1, source_target_pairs={{0,16},{8,24},{16,32},{24,40},{32,48},{40,56},{48,0},{56,8},{64,80... | collective-permute-start | bytes 393224 | tf_op jit(solution)/shard_map/ppermute | solution.py:309
  178.6 4.8 %copy-start.8 = (bf16[64,1024]{1,0:T(8,128)(2,1)S(1)}, bf16[64,1024]{1,0:T(8,128)(2,1)}, u32[]{:S(2)}) copy-start(bf16[64,1024]{1,0:T(8,128)(2,1)} %add.19) | copy-start | bytes 393220
  183.5 2.0 %copy-start.5 = (bf16[256,1024]{1,0:T(8,128)(2,1)}, bf16[256,1024]{1,0:T(8,128)(2,1)S(1)}, u32[]{:S(2)}) copy-start(bf16[256,1024]{1,0:T(8,128)(2,1)S(1)} %constant_dynamic-update-slice_fusion.refs_1_) | copy-start | bytes 1572868
  183.5 2.0 %collective-permute-start.17 = (bf16[256,1024]{1,0:T(8,128)(2,1)S(1)}, bf16[256,1024]{1,0:T(8,128)(2,1)S(1)}, u32[]{:S(2)}, u32[]{:S(2)}) collective-permute-start(bf16[256,1024]{1,0:T(8,128)(2,1)S(1)} %constant_dynamic-update-slice_fusion.refs_1_), channel_id=1, source_target_pairs={{0,8},{8,0},{16,24},{24,16},{32,40},{40,32},{48,56},{56,48},{64,72... | collective-permute-start | bytes 1572872 | tf_op jit(solution)/shard_map/ppermute | solution.py:309
  (8 other events, 6.9 us)

commit v3 on v2

--- a/solution.py
+++ b/solution.py
@@ -18,12 +18,18 @@
 LATPAD = 640
 LOG2E = 1.4426950408889634
 VMEM = 56 * 1024 * 1024
-EARLY = 2
+SMALL = pl.CostEstimate(flops=1, bytes_accessed=1, transcendentals=0)
+EARLY = 3
 LINE = 4
+ADD_FLOPS = 40_000_000_000
 
 
 def dot(a, b, dims):
     return lax.dot_general(a, b, (dims, ((), ())), preferred_element_type=jnp.float32)
+
+
+def places(pairs):
+    return (0, QPAIR) if pairs == 1 else (pairs * GPAIR, 0)
 
 
 def pack_kernel(plans, q_ref, g_ref, lat_ref, *refs):
@@ -36,7 +42,8 @@
         for j in range(groups):
             batch = []
             at = j * per_group + first
-            for ref, width, to in ((q_ref, QPAIR, 0), (g_ref, GPAIR, pairs * QPAIR)):
+            q_at, g_at = places(pairs)
+            for ref, width, to in ((q_ref, QPAIR, q_at), (g_ref, GPAIR, g_at)):
                 batch.append(
                     pltpu.make_async_copy(
                         ref.at[:, at * width : (at + pairs) * width],
@@ -89,72 +96,83 @@
     )(q, g, latents)
 
 
-def unpack_kernel(plans, *refs):
-    count = len(plans)
-    parts, out_ref, sems = refs[:count], refs[count], refs[count + 1]
-    helds = refs[count + 2 :]
-    groups = parts[0].shape[0]
+def unpack_kernel(first, pairs, has_total, with_latents, *refs):
+    refs = list(refs)
+    if has_total:
+        refs.pop(0)
+    part_ref, out_ref = refs[:2]
+    groups = part_ref.shape[0]
     per_group = out_ref.shape[1] // (groups * QPAIR)
+    width = pairs * QPAIR
+    sems, held = refs[-2:]
     fetches, copies = [], []
-    for n, (first, pairs) in enumerate(plans):
-        width = pairs * QPAIR
-        for j in range(groups):
-            at = (j * per_group + first) * QPAIR
-            fetches.append(
-                pltpu.make_async_copy(parts[n].at[j], helds[n].at[j], sems.at[0, n, j])
+    for j in range(groups):
+        at = (j * per_group + first) * QPAIR
+        fetches.append(pltpu.make_async_copy(part_ref.at[j], held.at[j], sems.at[0, j]))
+        copies.append(
+            pltpu.make_async_copy(
+                held.at[j, :, :width], out_ref.at[:, at : at + width], sems.at[1, j]
             )
-            copies.append(
-                pltpu.make_async_copy(
-                    helds[n].at[j], out_ref.at[:, at : at + width], sems.at[1, n, j]
-                )
-            )
+        )
     for fetch in fetches:
         fetch.start()
     for fetch, copy in zip(fetches, copies, strict=True):
         fetch.wait()
         copy.start()
+    if with_latents:
+        total = held[0, :, width:].astype(jnp.float32)
+        for j in range(1, groups):
+            total += held[j, :, width:].astype(jnp.float32)
+        refs[2][...] = total.T[: LATENT + ROPE].astype(part_ref.dtype)
     for copy in copies:
         copy.wait()
 
 
-def unpack(parts, plans, per_group):
-    groups, tokens, _ = parts[0].shape
+def unpack(total, part, first, pairs, per_group, with_latents):
+    groups, tokens, _ = part.shape
     hbm = pl.BlockSpec(memory_space=pl.ANY)
-    size = tokens * groups * per_group * QPAIR
+    out_specs = [hbm]
+    shapes = [jax.ShapeDtypeStruct((tokens, groups * per_group * QPAIR), part.dtype)]
+    if with_latents:
+        out_specs.append(pl.BlockSpec(memory_space=pltpu.VMEM))
+        shapes.append(jax.ShapeDtypeStruct((LATENT + ROPE, tokens), part.dtype))
+    has = total is not None
     return pl.pallas_call(
-        functools.partial(unpack_kernel, plans),
-        in_specs=[hbm] * len(parts),
-        out_specs=hbm,
-        out_shape=jax.ShapeDtypeStruct((tokens, groups * per_group * QPAIR), parts[0].dtype),
-        scratch_shapes=[pltpu.SemaphoreType.DMA((2, len(parts), groups))]
-        + [pltpu.VMEM(part.shape, part.dtype) for part in parts],
+        functools.partial(unpack_kernel, first, pairs, has, with_latents),
+        in_specs=[hbm] * (1 + has),
+        out_specs=out_specs,
+        out_shape=shapes,
+        scratch_shapes=[
+            pltpu.SemaphoreType.DMA((2, groups)),
+            pltpu.VMEM(part.shape, part.dtype),
+        ],
+        input_output_aliases={0: 0} if has else {},
         compiler_params=pltpu.CompilerParams(vmem_limit_bytes=VMEM),
-        cost_estimate=pl.CostEstimate(flops=0, bytes_accessed=4 * size, transcendentals=0),
+        cost_estimate=SMALL,
         name="unpack",
-    )(*parts)
-
-
-def collect_kernel(part_ref, out_ref):
-    total = part_ref[0].astype(jnp.float32)
-    for j in range(1, part_ref.shape[0]):
-        total += part_ref[j].astype(jnp.float32)
-    out_ref[...] = total.T[: LATENT + ROPE].astype(out_ref.dtype)
-
-
-def collect(part):
-    shape = jax.ShapeDtypeStruct((LATENT + ROPE, part.shape[1]), part.dtype)
-    return pl.pallas_call(collect_kernel, out_shape=shape, name="collect")(part)
-
-
-def one_head(q_ref, q_at, g_ref, g_at, key, value, dk_ref, dv_ref, scale, block):
-    span = key.shape[0]
-    dq_rows = []
-    for index in reversed(range(span // block)):
+    )(*([total] * has + [part]))
+
+
+def scores_of(head, first, limit):
+    q_ref, q_at, g_ref, g_at, key, value = head[:6]
+    q = q_ref[first:limit, q_at : q_at + 256]
+    g = g_ref[first:limit, g_at : g_at + VDIM]
+    scores = dot(key[:limit], q, ((1,), (1,)))
+    return scores, dot(value[:limit], g, ((1,), (1,))), q, g
+
+
+def two_heads(heads, scale, block):
+    span = heads[0][4].shape[0]
+    steps = [(n, at) for at in reversed(range(span // block)) for n in range(len(heads))]
+    dq_rows = [[] for _ in heads]
+    ahead = scores_of(heads[0], steps[0][1] * block, (steps[0][1] + 1) * block)
+    for number, (n, index) in enumerate(steps):
         first, limit = index * block, (index + 1) * block
-        q = q_ref[first:limit, q_at : q_at + 256]
-        g = g_ref[first:limit, g_at : g_at + VDIM]
-        keys, values = key[:limit], value[:limit]
-        scores = dot(keys, q, ((1,), (1,)))
+        scores, dprobs, q, g = ahead
+        if number + 1 < len(steps):
+            after_n, after_at = steps[number + 1]
+            ahead = scores_of(heads[after_n], after_at * block, (after_at + 1) * block)
+        key, dk_ref, dv_ref = heads[n][4], heads[n][6], heads[n][7]
         key_pos = lax.broadcasted_iota(jnp.int32, (block, block), 0)
         query_pos = lax.broadcasted_iota(jnp.int32, (block, block), 1)
         last = jnp.where(key_pos <= query_pos, scores[first:], -jnp.inf)
@@ -162,7 +180,6 @@
         top = jnp.max(scores, axis=0, keepdims=True)
         expo = jnp.exp2((scores - top) * (scale * LOG2E))
         probs = expo * (1.0 / jnp.sum(expo, axis=0, keepdims=True))
-        dprobs = dot(values, g, ((1,), (1,)))
         delta = jnp.sum(probs * dprobs, axis=0, keepdims=True)
         dscores = (probs * (dprobs - delta)).astype(jnp.bfloat16)
         dv = dot(probs.astype(jnp.bfloat16), g, ((1,), (0,)))
@@ -173,16 +190,24 @@
         else:
             dv_ref[:limit] += dv
             dk_ref[:limit] += dk
-        dq_rows.append(dot(dscores, keys, ((0,), (0,))))
-    return jnp.concatenate(dq_rows[::-1], axis=0)
-
-
-def attend_kernel(has_sum, *refs):
+        dq_rows[n].append(dot(dscores, key[:limit], ((0,), (0,))))
+    return [jnp.concatenate(rows[::-1], axis=0) for rows in dq_rows]
+
+
+def attend_kernel(pairs, has_sum, last, *refs):
     refs = list(refs)
-    place, lat_ref, w_ref, q_ref, g_ref = refs[:5]
-    rest = refs[5:]
+    place, lat_ref, w_ref, q_ref = refs[:4]
+    rest = refs[4:]
+    if pairs == 1:
+        q_ref, g_ref = q_ref.at[:, :QPAIR], q_ref.at[:, QPAIR:]
+    else:
+        g_ref = rest.pop(0)
     sum_in = rest.pop(0) if has_sum else None
-    dq_ref, keep_ref, send_ref, out_ref, total, dk0, dv0, dk1, dv1 = rest
+    if last:
+        dq_ref, keep_ref, send_ref, total, dk0, dv0, dk1, dv1 = rest
+        dq_ref, out_ref = dq_ref.at[:, :QPAIR], dq_ref.at[:, QPAIR:]
+    else:
+        dq_ref, keep_ref, send_ref, out_ref, total, dk0, dv0, dk1, dv1 = rest
     step = pl.program_id(0)
     scale = (NOPE + ROPE) ** (-0.5)
     half = NOPE // 2
@@ -200,8 +225,14 @@
         [jnp.where(lane < half, 0.0, moved), jnp.where(lane < half, moved, rope_moved)], axis=1
     ).astype(jnp.bfloat16)
     value1 = keyval[:, 3 * NOPE :].astype(jnp.bfloat16)
-    dq0 = one_head(q_ref, 0, g_ref, 0, key0, value0, dk0, dv0, scale, block)
-    dq1 = one_head(q_ref, NOPE, g_ref, VDIM, key1, value1, dk1, dv1, scale, block)
+    dq0, dq1 = two_heads(
+        [
+            (q_ref, 0, g_ref, 0, key0, value0, dk0, dv0),
+            (q_ref, NOPE, g_ref, VDIM, key1, value1, dk1, dv1),
+        ],
+        scale,
+        block,
+    )
     dq = jnp.concatenate([dq0[:, :NOPE], dq0[:, NOPE:] + dq1[:, :NOPE], dq1[:, NOPE:]], axis=1)
     dq = (dq * scale).astype(jnp.bfloat16)
     dq_ref[...] = dq
@@ -252,7 +283,7 @@
         out_ref[...] = total[...].astype(out_ref.dtype)
 
 
-def attend(place, lat, lat_block, weight, first, x, pairs, total, total_type):
+def attend(place, lat, lat_block, weight, first, x, pairs, total, last):
     span = lat.shape[0]
     f32, bf16 = jnp.float32, jnp.bfloat16
     whole = lambda j: (0, 0)
@@ -261,30 +292,34 @@
         pl.BlockSpec(memory_space=pltpu.SMEM),
         pl.BlockSpec((span, LATPAD), lambda j: (0, lat_block)),
         pl.BlockSpec((LATENT, KVPAIR), lambda j: (0, first + j)),
-        pl.BlockSpec((span, QPAIR), column),
-        pl.BlockSpec((span, GPAIR), lambda j: (0, pairs * QPAIR // GPAIR + j)),
     ]
-    args = [place, lat, weight, x, x]
+    args = [place, lat, weight, x]
+    if pairs == 1:
+        specs.append(pl.BlockSpec((span, PAIR), whole))
+    else:
+        specs.append(pl.BlockSpec((span, QPAIR), lambda j: (0, pairs * GPAIR // QPAIR + j)))
+        specs.append(pl.BlockSpec((span, GPAIR), column))
+        args.append(x)
     if total is not None:
         specs.append(pl.BlockSpec((span, LATPAD), whole))
         args.append(total)
     dw_shape = jax.ShapeDtypeStruct((LATENT // 2, pairs * KVPAIR), bf16)
+    out_specs = [pl.BlockSpec((LATENT // 2, KVPAIR), column)] * 2
+    shapes = [dw_shape, dw_shape]
+    if last:
+        out_specs = [pl.BlockSpec((span, QPAIR + LATPAD), whole)] + out_specs
+        shapes = [jax.ShapeDtypeStruct((span, QPAIR + LATPAD), bf16)] + shapes
+    else:
+        out_specs = [pl.BlockSpec((span, QPAIR), column)] + out_specs
+        shapes = [jax.ShapeDtypeStruct((span, pairs * QPAIR), bf16)] + shapes
+        out_specs.append(pl.BlockSpec((span, LATPAD), whole))
+        shapes.append(jax.ShapeDtypeStruct((span, LATPAD), f32))
     return pl.pallas_call(
-        functools.partial(attend_kernel, total is not None),
+        functools.partial(attend_kernel, pairs, total is not None, last),
         grid=(pairs,),
         in_specs=specs,
-        out_specs=[
-            pl.BlockSpec((span, QPAIR), column),
-            pl.BlockSpec((LATENT // 2, KVPAIR), column),
-            pl.BlockSpec((LATENT // 2, KVPAIR), column),
-            pl.BlockSpec((span, LATPAD), whole),
-        ],
-        out_shape=[
-            jax.ShapeDtypeStruct((span, pairs * QPAIR), bf16),
-            dw_shape,
-            dw_shape,
-            jax.ShapeDtypeStruct((span, LATPAD), total_type),
-        ],
+        out_specs=out_specs,
+        out_shape=shapes,
         scratch_shapes=[
             pltpu.VMEM((span, LATPAD), f32),
             pltpu.VMEM((span, 2 * NOPE), f32),
@@ -326,7 +361,8 @@
 
 
 def add(*parts):
-    return pl.pallas_call(add_kernel, out_shape=parts[0], name="add")(*parts)
+    cost = pl.CostEstimate(flops=ADD_FLOPS, bytes_accessed=1, transcendentals=0)
+    return pl.pallas_call(add_kernel, out_shape=parts[0], cost_estimate=cost, name="add")(*parts)
 
 
 def split_kernel(keep_ref, got_ref, *out_refs):
@@ -338,7 +374,10 @@
 
 def split(keep, got):
     shape = jax.ShapeDtypeStruct((keep.shape[0] // LINE, keep.shape[1]), keep.dtype)
-    return pl.pallas_call(split_kernel, out_shape=[shape] * LINE, name="split")(keep, got)
+    shapes = [shape] * LINE
+    return pl.pallas_call(split_kernel, out_shape=shapes, cost_estimate=SMALL, name="split")(
+        keep, got
+    )
 
 
 def swap(x):
@@ -347,6 +386,26 @@
 
 def spread(pieces):
     return [pieces[0]] + [send(x, along(k + 1)) for k, x in enumerate(pieces[1:])]
+
+
+def merge_kernel(count, *refs):
+    *parts, out_ref = refs
+    at = 0
+    for group in (parts[:count], parts[count:]):
+        total = group[0][...].astype(jnp.float32)
+        for part in group[1:]:
+            total += part[...].astype(jnp.float32)
+        out_ref[:, at : at + total.shape[1]] = total.astype(out_ref.dtype)
+        at += total.shape[1]
+
+
+def merge(first, second):
+    rows = first[0].shape[0]
+    shape = jax.ShapeDtypeStruct((rows, first[0].shape[1] + second[0].shape[1]), first[0].dtype)
+    kernel = functools.partial(merge_kernel, len(first))
+    return pl.pallas_call(kernel, out_shape=shape, cost_estimate=SMALL, name="merge")(
+        *first, *second
+    )
 
 
 def across(part):
@@ -354,35 +413,27 @@
     return send(part, lambda i: (i + slabs // 2) % slabs)
 
 
-def gather_line(part):
-    return jnp.concatenate(spread([part] * LINE), axis=0)
-
-
 def place_kernel(slabs, place, *refs):
-    mine, other, out_ref = refs[-3:]
-    rows = mine.shape[0] // LINE
-    for ref, core in ((mine, place[0]), (other, 1 - place[0])):
-        for k in range(LINE):
-            at = core * LINE + lax.rem(place[1] - k + LINE, LINE)
-            to = pl.ds(pl.multiple_of(at * rows, rows), rows)
-            out_ref[to, :] = ref[k * rows : (k + 1) * rows].astype(jnp.float32) * (1.0 / slabs)
-
-
-def place_slabs(place, total, mine, other, index, count):
-    whole = pl.BlockSpec(mine.shape, lambda j: (0, 0))
-    has = total is not None
+    *parts, out_ref = refs
+    rows = parts[0].shape[0]
+    for ref, core, k in zip(parts, [0] * LINE + [1] * LINE, 2 * list(range(LINE)), strict=True):
+        core = 1 - place[0] if core else place[0]
+        at = core * LINE + lax.rem(place[1] - k + LINE, LINE)
+        to = pl.ds(pl.multiple_of(at * rows, rows), rows)
+        out_ref[to, :] = ref[...].astype(jnp.float32) * (1.0 / slabs)
+
+
+def place_slabs(place, mine, other):
+    vmem = pl.BlockSpec(memory_space=pltpu.VMEM)
     return pl.pallas_call(
         functools.partial(place_kernel, lax.axis_size("dp")),
-        grid=(1,),
-        in_specs=[pl.BlockSpec(memory_space=pltpu.SMEM)]
-        + [pl.BlockSpec(memory_space=pl.ANY)] * has
-        + [whole, whole],
-        out_specs=pl.BlockSpec((LATENT, mine.shape[1]), lambda j: (0, index)),
-        out_shape=jax.ShapeDtypeStruct((LATENT, count * mine.shape[1]), jnp.float32),
-        input_output_aliases={1: 0} if has else {},
+        in_specs=[pl.BlockSpec(memory_space=pltpu.SMEM)] + [vmem] * (2 * LINE),
+        out_specs=vmem,
+        out_shape=jax.ShapeDtypeStruct((LATENT, mine[0].shape[1]), jnp.float32),
         compiler_params=pltpu.CompilerParams(vmem_limit_bytes=VMEM),
+        cost_estimate=SMALL,
         name="place",
-    )(*([place] + [total] * has + [mine, other]))
+    )(place, *mine, *other)
 
 
 def after(x, *others):
@@ -400,36 +451,27 @@
     place = jnp.stack([me % 2, me // 2 % LINE]).astype(jnp.int32)
 
     x0, x1 = pack(q, g, lat, groups, ((0, EARLY), (EARLY, late)))
+    x0, place = after(x0, place)
     got0 = exchange(x0, "seq")
     x1, got0 = after(x1, got0)
     got1 = exchange(x1, "seq")
     lat = got0.reshape(span, got0.shape[2])
     kv = (place, lat, EARLY * PAIR // LATPAD, kv_weight)
-    dq0, keep0, give0, total = attend(*kv, 0, lat, EARLY, None, jnp.float32)
-    part0 = add(*spread(split(keep0, swap(give0))))
-    other0 = across(part0)
-    dq0, got1, part0 = after(dq0, got1, part0)
+    dq0, keep0, give0, total = attend(*kv, 0, lat, EARLY, None, False)
     back0 = exchange(dq0.reshape(groups, tokens, EARLY * QPAIR), "seq")
-    dq1, keep1, give1, total = attend(
-        *kv, EARLY, got1.reshape(span, -1), late, total, jnp.bfloat16
-    )
-    dq1, back0, other0 = after(dq1, back0, other0)
-    back1 = exchange(dq1.reshape(groups, tokens, late * QPAIR), "seq")
-    part0 = add(part0, other0)
-    got, keep1, part0 = after(swap(give1), keep1, part0)
-    part1 = add(*spread(split(keep1, got)))
-    other1 = across(part1)
-    mine0 = gather_line(part0)
-    total, back1, other1, mine0 = after(total, back1, other1, mine0)
-    back2 = exchange(total.reshape(groups, tokens, LATPAD), "seq")
-    theirs0 = swap(mine0)
-    line1 = spread([add(part1, other1)] * LINE)
-    query_grad = unpack([back0, back1], ((0, EARLY), (EARLY, late)), per_group)
-    weight_grad = place_slabs(place, None, mine0, theirs0, 0, 2)
-    query_grad, weight_grad, *line1 = after(query_grad, weight_grad, *line1)
-    mine1 = jnp.concatenate(line1, axis=0)
-    weight_grad = place_slabs(place, weight_grad, mine1, swap(mine1), 1, 2)
-    latent_grad = collect(back2)
+    swap0 = swap(give0)
+    send1, keep1, give1 = attend(*kv, EARLY, got1.reshape(span, PAIR), late, total, True)
+    send1, keep1, give1, keep0, swap0 = after(send1, keep1, give1, keep0, swap0)
+    pieces0 = spread(split(keep0, swap0))
+    pieces1 = spread(split(keep1, swap(give1)))
+    part = merge(pieces0, pieces1)
+    other = across(part)
+    (query_grad,) = unpack(None, back0, 0, EARLY, per_group, False)
+    send1, query_grad, part = after(send1, query_grad, part)
+    back1 = exchange(send1.reshape(groups, tokens, QPAIR + LATPAD), "seq")
+    line = spread([add(part, other)] * LINE)
+    weight_grad = place_slabs(place, line, [swap(x) for x in line])
+    query_grad, latent_grad = unpack(query_grad, back1, EARLY, late, per_group, True)
     return (query_grad[None], latent_grad.T[None], weight_grad)
 
 

time: 194 us -> 187 us (0.964)
  blocking collectives: 52.8 us -> 67 us
  Pallas kernels: 68.9 us -> 57.9 us
  starting transfers between devices: 42.5 us -> 32 us
    all_to_all x1, blocking collectives: 52.8 us -> 67 us  [exchange(): lax.all_to_all(x, axis, split_axis=0, concat_axis=0, tiled=True, axis_ind...]
    pallas_call x12 -> x9, Pallas kernels: 62.6 us -> 51.9 us  [the longest x2 34.7 us: attend(): pl.pallas_call(functools.partial(attend_kernel, pairs, total is not None,...]
    all_to_all x4 -> x3, starting transfers between devices: 19.8 us -> 14.3 us  [exchange(): lax.all_to_all(x, axis, split_axis=0, concat_axis=0, tiled=True, axis_ind...]
    ppermute x18 -> x16, starting transfers between devices: 22.7 us -> 17.7 us  [send(): return lax.ppermute(x, 'dp', [(i, step(i)) for i in range(slabs)])]
    unnamed x39 -> x38, local copies, waits for them, and re-layouts: 5.65 us -> 6.98 us
    ppermute x18 -> x16, waiting for transfers between devices: 19.9 us -> 18.9 us  [send(): return lax.ppermute(x, 'dp', [(i, step(i)) for i in range(slabs)])]
  transfers between devices with their start and end apart: 22 -> 19, of which waited for: 11 -> 7; matrix products, arithmetic and copies ran while one was open for 1% -> 0% of each run, Pallas kernels for 31% -> 26%
where the time goes in v3:
time: 187 us; the launch traced here: 186 us
  blocking collectives  67 us (36%)
  Pallas kernels  57.9 us (31%)
  starting transfers between devices  32 us (17%)
  waiting for transfers between devices  20.2 us (11%)
  local copies, waits for them, and re-layouts  6.98 us (4%)
    all_to_all x1, blocking collectives, exchange(): lax.all_to_all(x, axis, split_axis=0, concat_axis=0, tiled=True, axis_ind...  67 us
    pallas_call x2, Pallas kernels, attend(): pl.pallas_call(functools.partial(attend_kernel, pairs, total is not None,...  34.7 us
    ppermute x16, waiting for transfers between devices, send(): return lax.ppermute(x, 'dp', [(i, step(i)) for i in range(slabs)])  18.9 us
    ppermute x16, starting transfers between devices, send(): return lax.ppermute(x, 'dp', [(i, step(i)) for i in range(slabs)])  17.7 us
    all_to_all x3, starting transfers between devices, exchange(): lax.all_to_all(x, axis, split_axis=0, concat_axis=0, tiled=True, axis_ind...  14.3 us
    unnamed x38, local copies, waits for them, and re-layouts  6.98 us
    pallas_call x1, Pallas kernels, pack(): pl.pallas_call(functools.partial(pack_kernel, plans), in_specs=[hbm, hbm,...  5.99 us
    pallas_call x2, Pallas kernels, unpack(): pl.pallas_call(functools.partial(unpack_kernel, first, pairs, has, with_l...  5.43 us
  transfers between devices with their start and end apart: 19, of which 7 were waited for; matrix products, arithmetic and copies ran while one was open for 0% of the time, Pallas kernels for 26%

profile of v3, /device:TPU:0, one launch (start us, length us, event | category | flops | bytes accessed | tf_op | source)
XLA Modules:
  0.0 185.8 jit_solution(1883283386655610031)
XLA Ops:
  1.3 6.0 %pack.1 = (bf16[8,128,2560]{2,1,0:T(8,128)(2,1)}, bf16[8,128,640]{2,1,0:T(8,128)(2,1)}) custom-call(bf16[128,12288]{1,0:T(8,128)(2,1)} %bitcast.20, bf16[128,8192]{1,0:T(8,128)(2,1)} %bitcast.23, bf16[576,128]{1,0:T(8,128)(2,1)} %bitcast.25), custom_call_target="tpu_custom_call" | custom-call | bytes 13107200 | tf_op jit(solution)/shard_map/pack/pallas_call | solution.py:81
  7.3 67.0 %all_to_all.20 = bf16[8,128,2560]{2,1,0:T(8,128)(2,1)} all-to-all(bf16[8,128,2560]{2,1,0:T(8,128)(2,1)} %get-tuple-element.37), channel_id=1, replica_groups=mesh['dp'=16,'seq'=8] {'seq'}, dimensions={0} | all-to-all | bytes 10485760 | tf_op jit(solution)/shard_map/all_to_all | solution.py:339
  74.4 3.6 %all-to-all-start.1 = ((bf16[8,128,640]{2,1,0:T(8,128)(2,1)}), bf16[8,128,640]{2,1,0:T(8,128)(2,1)S(1)}, u32[]{:S(2)}, u32[]{:S(2)}) async-start(bf16[8,128,640]{2,1,0:T(8,128)(2,1)} %get-tuple-element.39), calls=%async_computation.1 | async-start | bytes 2621440 | tf_op jit(solution)/shard_map/all_to_all | solution.py:339
  77.9 24.0 %attend.2 = (bf16[1024,1152]{1,0:T(8,128)(2,1)}, bf16[256,1536]{1,0:T(8,128)(2,1)}, bf16[256,1536]{1,0:T(8,128)(2,1)}, f32[1024,640]{1,0:T(8,128)}) custom-call(s32[2]{0:T(128)} %pad_add_fusion.refs_0_.place, bf16[1024,2560]{1,0:T(8,128)(2,1)} %bitcast.16, bf16[512,2048]{1,0:T(8,128)(2,1)} %refs_2_.3, bf16[1024,2560]{1,0:T(8,128)(2,1)} %bitcast.17, ...), custom_call_target="tpu_custom_call" | custom-call | flops 15000000512 | bytes 18000000 | tf_op jit(solution)/shard_map/attend/pallas_call | solution.py:317
  102.0 1.1 copy-done.2
  103.1 5.6 %all-to-all-start.2 = ((bf16[8,128,1152]{2,1,0:T(8,128)(2,1)}), bf16[8,128,1152]{2,1,0:T(8,128)(2,1)S(1)}, u32[]{:S(2)}, u32[]{:S(2)}) async-start(bf16[8,128,1152]{2,1,0:T(8,128)(2,1)} %bitcast.21), calls=%async_computation.2 | async-start | bytes 4718592 | tf_op jit(solution)/shard_map/all_to_all | solution.py:339
  108.8 10.7 %attend.3 = (bf16[1024,1024]{1,0:T(8,128)(2,1)}, bf16[256,512]{1,0:T(8,128)(2,1)}, bf16[256,512]{1,0:T(8,128)(2,1)}) custom-call(s32[2]{0:T(128)} %pad_add_fusion.refs_0_.place, bf16[1024,2560]{1,0:T(8,128)(2,1)} %bitcast.19, bf16[512,2048]{1,0:T(8,128)(2,1)} %refs_2_.3, bf16[1024,640]{1,0:T(8,128)(2,1)} %bitcast.24, f32[1024,640]{1,0:T(8,128)} %get-tuple-element.40.refs_4_), custom_call_target="tpu_custom_call" | custom-call | flops 5000000000 | bytes 6000000 | tf_op jit(solution)/shard_map/attend/pallas_call | solution.py:317
  120.3 2.3 %split.2 = (bf16[64,1536]{1,0:T(8,128)(2,1)}, bf16[64,1536]{1,0:T(8,128)(2,1)}, bf16[64,1536]{1,0:T(8,128)(2,1)}, bf16[64,1536]{1,0:T(8,128)(2,1)}) custom-call(bf16[256,1536]{1,0:T(8,128)(2,1)} %get-tuple-element.48.keep_ref, bf16[256,1536]{1,0:T(8,128)(2,1)} %copy-done.3), custom_call_target="tpu_custom_call" | custom-call | flops 1 | bytes 1 | tf_op jit(solution)/shard_map/split/pallas_call | solution.py:378
  122.6 1.5 collective-permute-start.1
  124.1 2.7 %collective-permute-start.2 = (bf16[64,1536]{1,0:T(8,128)(2,1)}, bf16[64,1536]{1,0:T(8,128)(2,1)S(1)}, u32[]{:S(2)}, u32[]{:S(2)}) collective-permute-start(bf16[64,1536]{1,0:T(8,128)(2,1)} %get-tuple-element.52), channel_id=1, source_target_pairs={{0,32},{8,40},{16,48},{24,56},{32,0},{40,8},{48,16},{56,24},{64,96... | collective-permute-start | bytes 589832 | tf_op jit(solution)/shard_map/ppermute | solution.py:344
  126.9 1.4 collective-permute-start.3
  129.0 1.7 split.3
  131.3 0.9 collective-permute-start.6
  132.2 1.8 collective-permute-start.7
  134.0 2.9 %collective-permute-done.2.refs_2_ = bf16[64,1536]{1,0:T(8,128)(2,1)S(1)} collective-permute-done((bf16[64,1536]{1,0:T(8,128)(2,1)}, bf16[64,1536]{1,0:T(8,128)(2,1)S(1)}, u32[]{:S(2)}, u32[]{:S(2)}) %collective-permute-start.2) | collective-permute-done | bytes 196640 | tf_op jit(solution)/shard_map/ppermute | solution.py:344
  137.0 1.3 collective-permute-done.5.refs_5_
  138.3 1.1 collective-permute-done.6.refs_6_
  140.1 2.1 %merge.1.refs_0_ = bf16[64,2048]{1,0:T(8,128)(2,1)} custom-call(bf16[64,1536]{1,0:T(8,128)(2,1)} %get-tuple-element.50.refs_0_, bf16[64,1536]{1,0:T(8,128)(2,1)} %copy-done.12, bf16[64,1536]{1,0:T(8,128)(2,1)} %copy-done.13, bf16[64,1536]{1,0:T(8,128)(2,1)} %copy-done.14, bf16[64,512]{1,0:T(8,128)(2,1)} %get-tuple-element.56.refs_4_, ...), custom_call_target="tpu_custom_call" | custom-call | flops 1 | bytes 1 | tf_op jit(solution)/shard_map/merge/pallas_call | solution.py:406
  142.2 3.6 %collective-permute-start.8 = (bf16[64,2048]{1,0:T(8,128)(2,1)}, bf16[64,2048]{1,0:T(8,128)(2,1)S(1)}, u32[]{:S(2)}, u32[]{:S(2)}) collective-permute-start(bf16[64,2048]{1,0:T(8,128)(2,1)} %merge.1.refs_0_), channel_id=1, source_target_pairs={{0,64},{8,72},{16,80},{24,88},{32,96},{40,104},{48,112},{56,120},{... | collective-permute-start | bytes 786440 | tf_op jit(solution)/shard_map/ppermute | solution.py:344
  145.8 1.4 copy-done
  147.2 2.5 %unpack.2.refs_0_ = bf16[128,12288]{1,0:T(8,128)(2,1)} custom-call(bf16[8,128,1152]{2,1,0:T(8,128)(2,1)} %copy-done), custom_call_target="tpu_custom_call" | custom-call | flops 1 | bytes 1 | tf_op jit(solution)/shard_map/unpack/pallas_call | solution.py:140
  149.7 5.1 %all-to-all-start.3 = ((bf16[8,128,1024]{2,1,0:T(8,128)(2,1)}), bf16[8,128,1024]{2,1,0:T(8,128)(2,1)S(1)}, u32[]{:S(2)}, u32[]{:S(2)}) async-start(bf16[8,128,1024]{2,1,0:T(8,128)(2,1)} %bitcast.22), calls=%async_computation.3 | async-start | bytes 4194304 | tf_op jit(solution)/shard_map/all_to_all | solution.py:339
  155.5 1.8 add.13.refs_0_
  157.3 2.2 %collective-permute-start.11 = (bf16[64,2048]{1,0:T(8,128)(2,1)}, bf16[64,2048]{1,0:T(8,128)(2,1)S(1)}, u32[]{:S(2)}, u32[]{:S(2)}) collective-permute-start(bf16[64,2048]{1,0:T(8,128)(2,1)} %add.13.refs_0_), channel_id=1, source_target_pairs={{0,48},{8,56},{16,0},{24,8},{32,16},{40,24},{48,32},{56,40},{64,11... | collective-permute-start | bytes 786440 | tf_op jit(solution)/shard_map/ppermute | solution.py:344
  159.5 1.2 collective-permute-start.10
  161.3 9.3 %collective-permute-done.11.refs_3_ = bf16[64,2048]{1,0:T(8,128)(2,1)S(1)} collective-permute-done((bf16[64,2048]{1,0:T(8,128)(2,1)}, bf16[64,2048]{1,0:T(8,128)(2,1)S(1)}, u32[]{:S(2)}, u32[]{:S(2)}) %collective-permute-start.11) | collective-permute-done | bytes 262176 | tf_op jit(solution)/shard_map/ppermute | solution.py:344
  171.2 2.8 %collective-permute-done.9.refs_1_ = bf16[64,2048]{1,0:T(8,128)(2,1)S(1)} collective-permute-done((bf16[64,2048]{1,0:T(8,128)(2,1)}, bf16[64,2048]{1,0:T(8,128)(2,1)S(1)}, u32[]{:S(2)}, u32[]{:S(2)}) %collective-permute-start.9) | collective-permute-done | bytes 262176 | tf_op jit(solution)/shard_map/ppermute | solution.py:344
  174.0 1.5 collective-permute-done.13.refs_5_
  176.2 3.8 %place.1 = f32[512,2048]{1,0:T(8,128)} custom-call(s32[2]{0:T(128)} %pad_add_fusion.refs_0_.place, bf16[64,2048]{1,0:T(8,128)(2,1)} %add.13.refs_0_, bf16[64,2048]{1,0:T(8,128)(2,1)} %copy-done.6, bf16[64,2048]{1,0:T(8,128)(2,1)} %copy-done.5, bf16[64,2048]{1,0:T(8,128)(2,1)} %copy-done.4, bf16[64,2048]{1,0:T(8,128)(2,1)} %copy-done.7, ...), custom_call_target="tpu_custom_call" | custom-call | flops 1 | bytes 1 | tf_op jit(solution)/shard_map/place/pallas_call | solution.py:428
  180.0 1.3 all-to-all-done.3.refs_1_
  181.3 1.3 copy-done.1
  182.7 2.9 %unpack.3 = (bf16[128,12288]{1,0:T(8,128)(2,1)}, bf16[576,128]{1,0:T(8,128)(2,1)}) custom-call(bf16[128,12288]{1,0:T(8,128)(2,1)} %unpack.2.refs_0_, bf16[8,128,1024]{2,1,0:T(8,128)(2,1)} %copy-done.1), custom_call_target="tpu_custom_call", output_to_operand_aliasing={{0}: (0, {})} | custom-call | flops 1 | bytes 1 | tf_op jit(solution)/shard_map/unpack/pallas_call | solution.py:140
  (56 shorter events, 6.1 us)
Async XLA Ops:
  74.4 27.6 %all-to-all-start.1 = ((bf16[8,128,640]{2,1,0:T(8,128)(2,1)}), bf16[8,128,640]{2,1,0:T(8,128)(2,1)S(1)}, u32[]{:S(2)}, u32[]{:S(2)}) async-start(bf16[8,128,640]{2,1,0:T(8,128)(2,1)} %get-tuple-element.39), calls=%async_computation.1 | async-start | bytes 2621440 | tf_op jit(solution)/shard_map/all_to_all | solution.py:339
  102.0 1.2 copy-start.2
  103.1 42.6 %all-to-all-start.2 = ((bf16[8,128,1152]{2,1,0:T(8,128)(2,1)}), bf16[8,128,1152]{2,1,0:T(8,128)(2,1)S(1)}, u32[]{:S(2)}, u32[]{:S(2)}) async-start(bf16[8,128,1152]{2,1,0:T(8,128)(2,1)} %bitcast.21), calls=%async_computation.2 | async-start | bytes 4718592 | tf_op jit(solution)/shard_map/all_to_all | solution.py:339
  108.8 10.7 %collective-permute-start = (bf16[256,1536]{1,0:T(8,128)(2,1)}, bf16[256,1536]{1,0:T(8,128)(2,1)S(1)}, u32[]{:S(2)}, u32[]{:S(2)}) collective-permute-start(bf16[256,1536]{1,0:T(8,128)(2,1)} %get-tuple-element.45), channel_id=1, source_target_pairs={{0,8},{8,0},{16,24},{24,16},{32,40},{40,32},{48,56},{56,48},{64,72... | collective-permute-start | bytes 2359304 | tf_op jit(solution)/shard_map/ppermute | solution.py:344
  119.4 8.9 %collective-permute-start.4 = (bf16[256,512]{1,0:T(8,128)(2,1)}, bf16[256,512]{1,0:T(8,128)(2,1)S(1)}, u32[]{:S(2)}, u32[]{:S(2)}) collective-permute-start(bf16[256,512]{1,0:T(8,128)(2,1)} %get-tuple-element.55), channel_id=1, source_target_pairs={{0,8},{8,0},{16,24},{24,16},{32,40},{40,32},{48,56},{56,48},{64,72... | collective-permute-start | bytes 786440 | tf_op jit(solution)/shard_map/ppermute | solution.py:344
  122.6 9.6 %collective-permute-start.1 = (bf16[64,1536]{1,0:T(8,128)(2,1)}, bf16[64,1536]{1,0:T(8,128)(2,1)S(1)}, u32[]{:S(2)}, u32[]{:S(2)}) collective-permute-start(bf16[64,1536]{1,0:T(8,128)(2,1)} %get-tuple-element.51), channel_id=1, source_target_pairs={{0,16},{8,24},{16,32},{24,40},{32,48},{40,56},{48,0},{56,8},{64,80... | collective-permute-start | bytes 589832 | tf_op jit(solution)/shard_map/ppermute | solution.py:344
  124.1 12.9 %collective-permute-start.2 = (bf16[64,1536]{1,0:T(8,128)(2,1)}, bf16[64,1536]{1,0:T(8,128)(2,1)S(1)}, u32[]{:S(2)}, u32[]{:S(2)}) collective-permute-start(bf16[64,1536]{1,0:T(8,128)(2,1)} %get-tuple-element.52), channel_id=1, source_target_pairs={{0,32},{8,40},{16,48},{24,56},{32,0},{40,8},{48,16},{56,24},{64,96... | collective-permute-start | bytes 589832 | tf_op jit(solution)/shard_map/ppermute | solution.py:344
  126.9 10.1 %collective-permute-start.3 = (bf16[64,1536]{1,0:T(8,128)(2,1)}, bf16[64,1536]{1,0:T(8,128)(2,1)S(1)}, u32[]{:S(2)}, u32[]{:S(2)}) collective-permute-start(bf16[64,1536]{1,0:T(8,128)(2,1)} %get-tuple-element.53), channel_id=1, source_target_pairs={{0,48},{8,56},{16,0},{24,8},{32,16},{40,24},{48,32},{56,40},{64,11... | collective-permute-start | bytes 589832 | tf_op jit(solution)/shard_map/ppermute | solution.py:344
  130.7 7.6 %collective-permute-start.5 = (bf16[64,512]{1,0:T(8,128)(2,1)}, bf16[64,512]{1,0:T(8,128)(2,1)S(1)}, u32[]{:S(2)}, u32[]{:S(2)}) collective-permute-start(bf16[64,512]{1,0:T(8,128)(2,1)} %get-tuple-element.57), channel_id=1, source_target_pairs={{0,16},{8,24},{16,32},{24,40},{32,48},{40,56},{48,0},{56,8},{64,80... | collective-permute-start | bytes 196616 | tf_op jit(solution)/shard_map/ppermute | solution.py:344
  131.3 8.1 %collective-permute-start.6 = (bf16[64,512]{1,0:T(8,128)(2,1)}, bf16[64,512]{1,0:T(8,128)(2,1)S(1)}, u32[]{:S(2)}, u32[]{:S(2)}) collective-permute-start(bf16[64,512]{1,0:T(8,128)(2,1)} %get-tuple-element.58), channel_id=1, source_target_pairs={{0,32},{8,40},{16,48},{24,56},{32,0},{40,8},{48,16},{56,24},{64,96... | collective-permute-start | bytes 196616 | tf_op jit(solution)/shard_map/ppermute | solution.py:344
  132.2 7.2 %copy-start.12 = (bf16[64,1536]{1,0:T(8,128)(2,1)}, bf16[64,1536]{1,0:T(8,128)(2,1)S(1)}, u32[]{:S(2)}) copy-start(bf16[64,1536]{1,0:T(8,128)(2,1)S(1)} %collective-permute-done.1.refs_1_) | copy-start | bytes 589828
  132.2 7.2 %collective-permute-start.7 = (bf16[64,512]{1,0:T(8,128)(2,1)}, bf16[64,512]{1,0:T(8,128)(2,1)S(1)}, u32[]{:S(2)}, u32[]{:S(2)}) collective-permute-start(bf16[64,512]{1,0:T(8,128)(2,1)} %get-tuple-element.59), channel_id=1, source_target_pairs={{0,48},{8,56},{16,0},{24,8},{32,16},{40,24},{48,32},{56,40},{64,11... | collective-permute-start | bytes 196616 | tf_op jit(solution)/shard_map/ppermute | solution.py:344
  137.0 2.4 %copy-start.13 = (bf16[64,1536]{1,0:T(8,128)(2,1)}, bf16[64,1536]{1,0:T(8,128)(2,1)S(1)}, u32[]{:S(2)}) copy-start(bf16[64,1536]{1,0:T(8,128)(2,1)S(1)} %collective-permute-done.2.refs_2_) | copy-start | bytes 589828
  137.0 2.4 %copy-start.14 = (bf16[64,1536]{1,0:T(8,128)(2,1)}, bf16[64,1536]{1,0:T(8,128)(2,1)S(1)}, u32[]{:S(2)}) copy-start(bf16[64,1536]{1,0:T(8,128)(2,1)S(1)} %collective-permute-done.3.refs_3_) | copy-start | bytes 589828
  138.3 1.1 copy-start.15
  142.2 12.6 %collective-permute-start.8 = (bf16[64,2048]{1,0:T(8,128)(2,1)}, bf16[64,2048]{1,0:T(8,128)(2,1)S(1)}, u32[]{:S(2)}, u32[]{:S(2)}) collective-permute-start(bf16[64,2048]{1,0:T(8,128)(2,1)} %merge.1.refs_0_), channel_id=1, source_target_pairs={{0,64},{8,72},{16,80},{24,88},{32,96},{40,104},{48,112},{56,120},{... | collective-permute-start | bytes 786440 | tf_op jit(solution)/shard_map/ppermute | solution.py:344
  145.8 1.4 copy-start
  149.7 31.7 %all-to-all-start.3 = ((bf16[8,128,1024]{2,1,0:T(8,128)(2,1)}), bf16[8,128,1024]{2,1,0:T(8,128)(2,1)S(1)}, u32[]{:S(2)}, u32[]{:S(2)}) async-start(bf16[8,128,1024]{2,1,0:T(8,128)(2,1)} %bitcast.22), calls=%async_computation.3 | async-start | bytes 4194304 | tf_op jit(solution)/shard_map/all_to_all | solution.py:339
  157.3 13.4 %collective-permute-start.11 = (bf16[64,2048]{1,0:T(8,128)(2,1)}, bf16[64,2048]{1,0:T(8,128)(2,1)S(1)}, u32[]{:S(2)}, u32[]{:S(2)}) collective-permute-start(bf16[64,2048]{1,0:T(8,128)(2,1)} %add.13.refs_0_), channel_id=1, source_target_pairs={{0,48},{8,56},{16,0},{24,8},{32,16},{40,24},{48,32},{56,40},{64,11... | collective-permute-start | bytes 786440 | tf_op jit(solution)/shard_map/ppermute | solution.py:344
  159.5 11.2 %collective-permute-start.10 = (bf16[64,2048]{1,0:T(8,128)(2,1)}, bf16[64,2048]{1,0:T(8,128)(2,1)S(1)}, u32[]{:S(2)}, u32[]{:S(2)}) collective-permute-start(bf16[64,2048]{1,0:T(8,128)(2,1)} %add.13.refs_0_), channel_id=1, source_target_pairs={{0,32},{8,40},{16,48},{24,56},{32,0},{40,8},{48,16},{56,24},{64,96... | collective-permute-start | bytes 786440 | tf_op jit(solution)/shard_map/ppermute | solution.py:344
  160.7 13.2 %collective-permute-start.9 = (bf16[64,2048]{1,0:T(8,128)(2,1)}, bf16[64,2048]{1,0:T(8,128)(2,1)S(1)}, u32[]{:S(2)}, u32[]{:S(2)}) collective-permute-start(bf16[64,2048]{1,0:T(8,128)(2,1)} %add.13.refs_0_), channel_id=1, source_target_pairs={{0,16},{8,24},{16,32},{24,40},{32,48},{40,56},{48,0},{56,8},{64,80... | collective-permute-start | bytes 786440 | tf_op jit(solution)/shard_map/ppermute | solution.py:344
  161.3 12.6 %collective-permute-start.12 = (bf16[64,2048]{1,0:T(8,128)(2,1)}, bf16[64,2048]{1,0:T(8,128)(2,1)S(1)}, u32[]{:S(2)}, u32[]{:S(2)}) collective-permute-start(bf16[64,2048]{1,0:T(8,128)(2,1)} %add.13.refs_0_), channel_id=1, source_target_pairs={{0,8},{8,0},{16,24},{24,16},{32,40},{40,32},{48,56},{56,48},{64,72... | collective-permute-start | bytes 786440 | tf_op jit(solution)/shard_map/ppermute | solution.py:344
  170.6 4.8 %copy-start.4 = (bf16[64,2048]{1,0:T(8,128)(2,1)}, bf16[64,2048]{1,0:T(8,128)(2,1)S(1)}, u32[]{:S(2)}) copy-start(bf16[64,2048]{1,0:T(8,128)(2,1)S(1)} %collective-permute-done.11.refs_3_) | copy-start | bytes 786436
  170.6 3.3 %collective-permute-start.15 = (bf16[64,2048]{1,0:T(8,128)(2,1)S(1)}, bf16[64,2048]{1,0:T(8,128)(2,1)S(1)}, u32[]{:S(2)}, u32[]{:S(2)}) collective-permute-start(bf16[64,2048]{1,0:T(8,128)(2,1)S(1)} %collective-permute-done.11.refs_3_), channel_id=1, source_target_pairs={{0,8},{8,0},{16,24},{24,16},{32,40},{40,32},{48,56},{56,48},{64,72... | collective-permute-start | bytes 786440 | tf_op jit(solution)/shard_map/ppermute | solution.py:344
  170.7 4.8 %copy-start.5 = (bf16[64,2048]{1,0:T(8,128)(2,1)}, bf16[64,2048]{1,0:T(8,128)(2,1)S(1)}, u32[]{:S(2)}) copy-start(bf16[64,2048]{1,0:T(8,128)(2,1)S(1)} %collective-permute-done.10.refs_2_) | copy-start | bytes 786436
  170.7 3.3 %collective-permute-start.14 = (bf16[64,2048]{1,0:T(8,128)(2,1)S(1)}, bf16[64,2048]{1,0:T(8,128)(2,1)S(1)}, u32[]{:S(2)}, u32[]{:S(2)}) collective-permute-start(bf16[64,2048]{1,0:T(8,128)(2,1)S(1)} %collective-permute-done.10.refs_2_), channel_id=1, source_target_pairs={{0,8},{8,0},{16,24},{24,16},{32,40},{40,32},{48,56},{56,48},{64,72... | collective-permute-start | bytes 786440 | tf_op jit(solution)/shard_map/ppermute | solution.py:344
  173.9 1.5 copy-start.6
  173.9 1.5 collective-permute-start.13
  173.9 1.5 copy-start.7
  174.0 1.5 copy-start.8
  174.0 1.5 copy-start.9
  181.3 1.3 copy-start.1
  (6 other events, 4.3 us)

commit v4 on v3

--- a/solution.py
+++ b/solution.py
@@ -147,7 +147,7 @@
             pltpu.VMEM(part.shape, part.dtype),
         ],
         input_output_aliases={0: 0} if has else {},
-        compiler_params=pltpu.CompilerParams(vmem_limit_bytes=VMEM),
+        compiler_params=pltpu.CompilerParams(vmem_limit_bytes=VMEM // 4),
         cost_estimate=SMALL,
         name="unpack",
     )(*([total] * has + [part]))

time: 187 us -> 182 us (0.973)
  local copies, waits for them, and re-layouts: 6.98 us -> 4.21 us
    unnamed x38 -> x34, local copies, waits for them, and re-layouts: 6.98 us -> 4.21 us
  transfers between devices with their start and end apart: 19 -> 19, of which waited for: 7 -> 7; matrix products, arithmetic and copies ran while one was open for 0% -> 0% of each run, Pallas kernels for 26% -> 27%
where the time goes in v4:
time: 182 us; the launch traced here: 181 us
  blocking collectives  67 us (37%)
  Pallas kernels  56.3 us (31%)
  starting transfers between devices  31.9 us (18%)
  waiting for transfers between devices  20.3 us (11%)
  local copies, waits for them, and re-layouts  4.21 us (2%)
    all_to_all x1, blocking collectives, exchange(): lax.all_to_all(x, axis, split_axis=0, concat_axis=0, tiled=True, axis_ind...  67 us
    pallas_call x2, Pallas kernels, attend(): pl.pallas_call(functools.partial(attend_kernel, pairs, total is not None,...  34.7 us
    ppermute x16, waiting for transfers between devices, send(): return lax.ppermute(x, 'dp', [(i, step(i)) for i in range(slabs)])  19 us
    ppermute x16, starting transfers between devices, send(): return lax.ppermute(x, 'dp', [(i, step(i)) for i in range(slabs)])  17.6 us
    all_to_all x3, starting transfers between devices, exchange(): lax.all_to_all(x, axis, split_axis=0, concat_axis=0, tiled=True, axis_ind...  14.3 us
    pallas_call x1, Pallas kernels, pack(): pl.pallas_call(functools.partial(pack_kernel, plans), in_specs=[hbm, hbm,...  5.98 us
    unnamed x34, local copies, waits for them, and re-layouts  4.21 us
    pallas_call x2, Pallas kernels, split(): pl.pallas_call(split_kernel, out_shape=shapes, cost_estimate=SMALL, name=...  4.07 us
  transfers between devices with their start and end apart: 19, of which 7 were waited for; matrix products, arithmetic and copies ran while one was open for 0% of the time, Pallas kernels for 27%

profile of v4, /device:TPU:0, one launch (start us, length us, event | category | flops | bytes accessed | tf_op | source)
XLA Modules:
  0.0 181.3 jit_solution(1513760435618691660)
XLA Ops:
  1.2 6.0 %pack.1 = (bf16[8,128,2560]{2,1,0:T(8,128)(2,1)}, bf16[8,128,640]{2,1,0:T(8,128)(2,1)}) custom-call(bf16[128,12288]{1,0:T(8,128)(2,1)} %bitcast.20, bf16[128,8192]{1,0:T(8,128)(2,1)} %bitcast.23, bf16[576,128]{1,0:T(8,128)(2,1)} %bitcast.25), custom_call_target="tpu_custom_call" | custom-call | bytes 13107200 | tf_op jit(solution)/shard_map/pack/pallas_call | solution.py:81
  7.2 67.0 %all_to_all.20 = bf16[8,128,2560]{2,1,0:T(8,128)(2,1)} all-to-all(bf16[8,128,2560]{2,1,0:T(8,128)(2,1)} %get-tuple-element.37), channel_id=1, replica_groups=mesh['dp'=16,'seq'=8] {'seq'}, dimensions={0} | all-to-all | bytes 10485760 | tf_op jit(solution)/shard_map/all_to_all | solution.py:339
  74.3 3.6 %all-to-all-start.1 = ((bf16[8,128,640]{2,1,0:T(8,128)(2,1)}), bf16[8,128,640]{2,1,0:T(8,128)(2,1)S(1)}, u32[]{:S(2)}, u32[]{:S(2)}) async-start(bf16[8,128,640]{2,1,0:T(8,128)(2,1)} %get-tuple-element.39), calls=%async_computation.1 | async-start | bytes 2621440 | tf_op jit(solution)/shard_map/all_to_all | solution.py:339
  77.9 24.0 %attend.2 = (bf16[1024,1152]{1,0:T(8,128)(2,1)}, bf16[256,1536]{1,0:T(8,128)(2,1)}, bf16[256,1536]{1,0:T(8,128)(2,1)}, f32[1024,640]{1,0:T(8,128)}) custom-call(s32[2]{0:T(128)} %pad_add_fusion.refs_0_.place, bf16[1024,2560]{1,0:T(8,128)(2,1)} %bitcast.16, bf16[512,2048]{1,0:T(8,128)(2,1)} %refs_2_.3, bf16[1024,2560]{1,0:T(8,128)(2,1)} %bitcast.17, ...), custom_call_target="tpu_custom_call" | custom-call | flops 15000000512 | bytes 18000000 | tf_op jit(solution)/shard_map/attend/pallas_call | solution.py:317
  101.9 1.1 copy-done
  103.0 5.6 %all-to-all-start.2 = ((bf16[8,128,1152]{2,1,0:T(8,128)(2,1)}), bf16[8,128,1152]{2,1,0:T(8,128)(2,1)S(1)}, u32[]{:S(2)}, u32[]{:S(2)}) async-start(bf16[8,128,1152]{2,1,0:T(8,128)(2,1)} %bitcast.21), calls=%async_computation.2 | async-start | bytes 4718592 | tf_op jit(solution)/shard_map/all_to_all | solution.py:339
  108.7 10.7 %attend.3 = (bf16[1024,1024]{1,0:T(8,128)(2,1)}, bf16[256,512]{1,0:T(8,128)(2,1)}, bf16[256,512]{1,0:T(8,128)(2,1)}) custom-call(s32[2]{0:T(128)} %pad_add_fusion.refs_0_.place, bf16[1024,2560]{1,0:T(8,128)(2,1)} %bitcast.19, bf16[512,2048]{1,0:T(8,128)(2,1)} %refs_2_.3, bf16[1024,640]{1,0:T(8,128)(2,1)} %bitcast.24, f32[1024,640]{1,0:T(8,128)} %get-tuple-element.40.refs_4_), custom_call_target="tpu_custom_call" | custom-call | flops 5000000000 | bytes 6000000 | tf_op jit(solution)/shard_map/attend/pallas_call | solution.py:317
  120.2 2.3 %split.2 = (bf16[64,1536]{1,0:T(8,128)(2,1)}, bf16[64,1536]{1,0:T(8,128)(2,1)}, bf16[64,1536]{1,0:T(8,128)(2,1)}, bf16[64,1536]{1,0:T(8,128)(2,1)}) custom-call(bf16[256,1536]{1,0:T(8,128)(2,1)} %get-tuple-element.48.keep_ref, bf16[256,1536]{1,0:T(8,128)(2,1)} %copy-done.1), custom_call_target="tpu_custom_call" | custom-call | flops 1 | bytes 1 | tf_op jit(solution)/shard_map/split/pallas_call | solution.py:378
  122.6 1.5 collective-permute-start.1
  124.0 2.7 %collective-permute-start.2 = (bf16[64,1536]{1,0:T(8,128)(2,1)}, bf16[64,1536]{1,0:T(8,128)(2,1)S(1)}, u32[]{:S(2)}, u32[]{:S(2)}) collective-permute-start(bf16[64,1536]{1,0:T(8,128)(2,1)} %get-tuple-element.52), channel_id=1, source_target_pairs={{0,32},{8,40},{16,48},{24,56},{32,0},{40,8},{48,16},{56,24},{64,96... | collective-permute-start | bytes 589832 | tf_op jit(solution)/shard_map/ppermute | solution.py:344
  126.8 1.4 collective-permute-start.3
  128.2 0.7 copy-done.9
  128.9 1.7 split.3
  131.2 0.9 collective-permute-start.6
  132.1 1.8 %collective-permute-start.7 = (bf16[64,512]{1,0:T(8,128)(2,1)}, bf16[64,512]{1,0:T(8,128)(2,1)S(1)}, u32[]{:S(2)}, u32[]{:S(2)}) collective-permute-start(bf16[64,512]{1,0:T(8,128)(2,1)} %get-tuple-element.59), channel_id=1, source_target_pairs={{0,48},{8,56},{16,0},{24,8},{32,16},{40,24},{48,32},{56,40},{64,11... | collective-permute-start | bytes 196616 | tf_op jit(solution)/shard_map/ppermute | solution.py:344
  134.0 3.0 %collective-permute-done.2.refs_2_ = bf16[64,1536]{1,0:T(8,128)(2,1)S(1)} collective-permute-done((bf16[64,1536]{1,0:T(8,128)(2,1)}, bf16[64,1536]{1,0:T(8,128)(2,1)S(1)}, u32[]{:S(2)}, u32[]{:S(2)}) %collective-permute-start.2) | collective-permute-done | bytes 196640 | tf_op jit(solution)/shard_map/ppermute | solution.py:344
  136.9 1.3 collective-permute-done.5.refs_5_
  138.3 1.1 collective-permute-done.6.refs_6_
  140.0 2.1 %merge.1.refs_0_ = bf16[64,2048]{1,0:T(8,128)(2,1)} custom-call(bf16[64,1536]{1,0:T(8,128)(2,1)} %get-tuple-element.50.refs_0_, bf16[64,1536]{1,0:T(8,128)(2,1)} %copy-done.10, bf16[64,1536]{1,0:T(8,128)(2,1)} %copy-done.11, bf16[64,1536]{1,0:T(8,128)(2,1)} %copy-done.12, bf16[64,512]{1,0:T(8,128)(2,1)} %get-tuple-element.56.refs_4_, ...), custom_call_target="tpu_custom_call" | custom-call | flops 1 | bytes 1 | tf_op jit(solution)/shard_map/merge/pallas_call | solution.py:406
  142.1 3.6 %collective-permute-start.8 = (bf16[64,2048]{1,0:T(8,128)(2,1)}, bf16[64,2048]{1,0:T(8,128)(2,1)S(1)}, u32[]{:S(2)}, u32[]{:S(2)}) collective-permute-start(bf16[64,2048]{1,0:T(8,128)(2,1)} %merge.1.refs_0_), channel_id=1, source_target_pairs={{0,64},{8,72},{16,80},{24,88},{32,96},{40,104},{48,112},{56,120},{... | collective-permute-start | bytes 786440 | tf_op jit(solution)/shard_map/ppermute | solution.py:344
  145.7 2.0 %unpack.2.refs_0_ = bf16[128,12288]{1,0:T(8,128)(2,1)} custom-call(bf16[8,128,1152]{2,1,0:T(8,128)(2,1)S(1)} %all-to-all-done.2.refs_0_), custom_call_target="tpu_custom_call" | custom-call | flops 1 | bytes 1 | tf_op jit(solution)/shard_map/unpack/pallas_call | solution.py:140
  147.7 5.1 %all-to-all-start.3 = ((bf16[8,128,1024]{2,1,0:T(8,128)(2,1)}), bf16[8,128,1024]{2,1,0:T(8,128)(2,1)S(1)}, u32[]{:S(2)}, u32[]{:S(2)}) async-start(bf16[8,128,1024]{2,1,0:T(8,128)(2,1)} %bitcast.22), calls=%async_computation.3 | async-start | bytes 4194304 | tf_op jit(solution)/shard_map/all_to_all | solution.py:339
  153.5 1.8 add.13.refs_0_
  155.3 2.2 %collective-permute-start.11 = (bf16[64,2048]{1,0:T(8,128)(2,1)}, bf16[64,2048]{1,0:T(8,128)(2,1)S(1)}, u32[]{:S(2)}, u32[]{:S(2)}) collective-permute-start(bf16[64,2048]{1,0:T(8,128)(2,1)} %add.13.refs_0_), channel_id=1, source_target_pairs={{0,48},{8,56},{16,0},{24,8},{32,16},{40,24},{48,32},{56,40},{64,11... | collective-permute-start | bytes 786440 | tf_op jit(solution)/shard_map/ppermute | solution.py:344
  157.5 1.2 collective-permute-start.10
  159.3 9.3 %collective-permute-done.11.refs_3_ = bf16[64,2048]{1,0:T(8,128)(2,1)S(1)} collective-permute-done((bf16[64,2048]{1,0:T(8,128)(2,1)}, bf16[64,2048]{1,0:T(8,128)(2,1)S(1)}, u32[]{:S(2)}, u32[]{:S(2)}) %collective-permute-start.11) | collective-permute-done | bytes 262176 | tf_op jit(solution)/shard_map/ppermute | solution.py:344
  169.2 2.8 %collective-permute-done.9.refs_1_ = bf16[64,2048]{1,0:T(8,128)(2,1)S(1)} collective-permute-done((bf16[64,2048]{1,0:T(8,128)(2,1)}, bf16[64,2048]{1,0:T(8,128)(2,1)S(1)}, u32[]{:S(2)}, u32[]{:S(2)}) %collective-permute-start.9) | collective-permute-done | bytes 262176 | tf_op jit(solution)/shard_map/ppermute | solution.py:344
  172.0 1.5 collective-permute-done.13.refs_5_
  173.5 0.7 copy-done.8
  174.2 3.8 %place.1 = f32[512,2048]{1,0:T(8,128)} custom-call(s32[2]{0:T(128)} %pad_add_fusion.refs_0_.place, bf16[64,2048]{1,0:T(8,128)(2,1)} %add.13.refs_0_, bf16[64,2048]{1,0:T(8,128)(2,1)} %copy-done.4, bf16[64,2048]{1,0:T(8,128)(2,1)} %copy-done.3, bf16[64,2048]{1,0:T(8,128)(2,1)} %copy-done.2, bf16[64,2048]{1,0:T(8,128)(2,1)} %copy-done.5, ...), custom_call_target="tpu_custom_call" | custom-call | flops 1 | bytes 1 | tf_op jit(solution)/shard_map/place/pallas_call | solution.py:428
  178.0 1.3 all-to-all-done.3.refs_1_
  179.3 1.8 unpack.3
  (52 shorter events, 4.6 us)
Async XLA Ops:
  74.3 27.6 %all-to-all-start.1 = ((bf16[8,128,640]{2,1,0:T(8,128)(2,1)}), bf16[8,128,640]{2,1,0:T(8,128)(2,1)S(1)}, u32[]{:S(2)}, u32[]{:S(2)}) async-start(bf16[8,128,640]{2,1,0:T(8,128)(2,1)} %get-tuple-element.39), calls=%async_computation.1 | async-start | bytes 2621440 | tf_op jit(solution)/shard_map/all_to_all | solution.py:339
  101.9 1.1 copy-start
  103.0 42.6 %all-to-all-start.2 = ((bf16[8,128,1152]{2,1,0:T(8,128)(2,1)}), bf16[8,128,1152]{2,1,0:T(8,128)(2,1)S(1)}, u32[]{:S(2)}, u32[]{:S(2)}) async-start(bf16[8,128,1152]{2,1,0:T(8,128)(2,1)} %bitcast.21), calls=%async_computation.2 | async-start | bytes 4718592 | tf_op jit(solution)/shard_map/all_to_all | solution.py:339
  108.7 10.7 %collective-permute-start = (bf16[256,1536]{1,0:T(8,128)(2,1)}, bf16[256,1536]{1,0:T(8,128)(2,1)S(1)}, u32[]{:S(2)}, u32[]{:S(2)}) collective-permute-start(bf16[256,1536]{1,0:T(8,128)(2,1)} %get-tuple-element.45), channel_id=1, source_target_pairs={{0,8},{8,0},{16,24},{24,16},{32,40},{40,32},{48,56},{56,48},{64,72... | collective-permute-start | bytes 2359304 | tf_op jit(solution)/shard_map/ppermute | solution.py:344
  119.3 0.9 copy-start.1
  119.3 8.9 %collective-permute-start.4 = (bf16[256,512]{1,0:T(8,128)(2,1)}, bf16[256,512]{1,0:T(8,128)(2,1)S(1)}, u32[]{:S(2)}, u32[]{:S(2)}) collective-permute-start(bf16[256,512]{1,0:T(8,128)(2,1)} %get-tuple-element.55), channel_id=1, source_target_pairs={{0,8},{8,0},{16,24},{24,16},{32,40},{40,32},{48,56},{56,48},{64,72... | collective-permute-start | bytes 786440 | tf_op jit(solution)/shard_map/ppermute | solution.py:344
  122.6 9.5 %collective-permute-start.1 = (bf16[64,1536]{1,0:T(8,128)(2,1)}, bf16[64,1536]{1,0:T(8,128)(2,1)S(1)}, u32[]{:S(2)}, u32[]{:S(2)}) collective-permute-start(bf16[64,1536]{1,0:T(8,128)(2,1)} %get-tuple-element.51), channel_id=1, source_target_pairs={{0,16},{8,24},{16,32},{24,40},{32,48},{40,56},{48,0},{56,8},{64,80... | collective-permute-start | bytes 589832 | tf_op jit(solution)/shard_map/ppermute | solution.py:344
  124.0 12.9 %collective-permute-start.2 = (bf16[64,1536]{1,0:T(8,128)(2,1)}, bf16[64,1536]{1,0:T(8,128)(2,1)S(1)}, u32[]{:S(2)}, u32[]{:S(2)}) collective-permute-start(bf16[64,1536]{1,0:T(8,128)(2,1)} %get-tuple-element.52), channel_id=1, source_target_pairs={{0,32},{8,40},{16,48},{24,56},{32,0},{40,8},{48,16},{56,24},{64,96... | collective-permute-start | bytes 589832 | tf_op jit(solution)/shard_map/ppermute | solution.py:344
  126.8 10.1 %collective-permute-start.3 = (bf16[64,1536]{1,0:T(8,128)(2,1)}, bf16[64,1536]{1,0:T(8,128)(2,1)S(1)}, u32[]{:S(2)}, u32[]{:S(2)}) collective-permute-start(bf16[64,1536]{1,0:T(8,128)(2,1)} %get-tuple-element.53), channel_id=1, source_target_pairs={{0,48},{8,56},{16,0},{24,8},{32,16},{40,24},{48,32},{56,40},{64,11... | collective-permute-start | bytes 589832 | tf_op jit(solution)/shard_map/ppermute | solution.py:344
  130.6 7.6 %collective-permute-start.5 = (bf16[64,512]{1,0:T(8,128)(2,1)}, bf16[64,512]{1,0:T(8,128)(2,1)S(1)}, u32[]{:S(2)}, u32[]{:S(2)}) collective-permute-start(bf16[64,512]{1,0:T(8,128)(2,1)} %get-tuple-element.57), channel_id=1, source_target_pairs={{0,16},{8,24},{16,32},{24,40},{32,48},{40,56},{48,0},{56,8},{64,80... | collective-permute-start | bytes 196616 | tf_op jit(solution)/shard_map/ppermute | solution.py:344
  131.2 8.1 %collective-permute-start.6 = (bf16[64,512]{1,0:T(8,128)(2,1)}, bf16[64,512]{1,0:T(8,128)(2,1)S(1)}, u32[]{:S(2)}, u32[]{:S(2)}) collective-permute-start(bf16[64,512]{1,0:T(8,128)(2,1)} %get-tuple-element.58), channel_id=1, source_target_pairs={{0,32},{8,40},{16,48},{24,56},{32,0},{40,8},{48,16},{56,24},{64,96... | collective-permute-start | bytes 196616 | tf_op jit(solution)/shard_map/ppermute | solution.py:344
  132.1 7.2 %copy-start.10 = (bf16[64,1536]{1,0:T(8,128)(2,1)}, bf16[64,1536]{1,0:T(8,128)(2,1)S(1)}, u32[]{:S(2)}) copy-start(bf16[64,1536]{1,0:T(8,128)(2,1)S(1)} %collective-permute-done.1.refs_1_) | copy-start | bytes 589828
  132.1 7.2 %collective-permute-start.7 = (bf16[64,512]{1,0:T(8,128)(2,1)}, bf16[64,512]{1,0:T(8,128)(2,1)S(1)}, u32[]{:S(2)}, u32[]{:S(2)}) collective-permute-start(bf16[64,512]{1,0:T(8,128)(2,1)} %get-tuple-element.59), channel_id=1, source_target_pairs={{0,48},{8,56},{16,0},{24,8},{32,16},{40,24},{48,32},{56,40},{64,11... | collective-permute-start | bytes 196616 | tf_op jit(solution)/shard_map/ppermute | solution.py:344
  136.9 2.4 %copy-start.11 = (bf16[64,1536]{1,0:T(8,128)(2,1)}, bf16[64,1536]{1,0:T(8,128)(2,1)S(1)}, u32[]{:S(2)}) copy-start(bf16[64,1536]{1,0:T(8,128)(2,1)S(1)} %collective-permute-done.2.refs_2_) | copy-start | bytes 589828
  136.9 2.4 %copy-start.12 = (bf16[64,1536]{1,0:T(8,128)(2,1)}, bf16[64,1536]{1,0:T(8,128)(2,1)S(1)}, u32[]{:S(2)}) copy-start(bf16[64,1536]{1,0:T(8,128)(2,1)S(1)} %collective-permute-done.3.refs_3_) | copy-start | bytes 589828
  138.3 1.1 copy-start.13
  142.1 10.7 %collective-permute-start.8 = (bf16[64,2048]{1,0:T(8,128)(2,1)}, bf16[64,2048]{1,0:T(8,128)(2,1)S(1)}, u32[]{:S(2)}, u32[]{:S(2)}) collective-permute-start(bf16[64,2048]{1,0:T(8,128)(2,1)} %merge.1.refs_0_), channel_id=1, source_target_pairs={{0,64},{8,72},{16,80},{24,88},{32,96},{40,104},{48,112},{56,120},{... | collective-permute-start | bytes 786440 | tf_op jit(solution)/shard_map/ppermute | solution.py:344
  147.7 31.7 %all-to-all-start.3 = ((bf16[8,128,1024]{2,1,0:T(8,128)(2,1)}), bf16[8,128,1024]{2,1,0:T(8,128)(2,1)S(1)}, u32[]{:S(2)}, u32[]{:S(2)}) async-start(bf16[8,128,1024]{2,1,0:T(8,128)(2,1)} %bitcast.22), calls=%async_computation.3 | async-start | bytes 4194304 | tf_op jit(solution)/shard_map/all_to_all | solution.py:339
  155.3 13.4 %collective-permute-start.11 = (bf16[64,2048]{1,0:T(8,128)(2,1)}, bf16[64,2048]{1,0:T(8,128)(2,1)S(1)}, u32[]{:S(2)}, u32[]{:S(2)}) collective-permute-start(bf16[64,2048]{1,0:T(8,128)(2,1)} %add.13.refs_0_), channel_id=1, source_target_pairs={{0,48},{8,56},{16,0},{24,8},{32,16},{40,24},{48,32},{56,40},{64,11... | collective-permute-start | bytes 786440 | tf_op jit(solution)/shard_map/ppermute | solution.py:344
  157.5 11.2 %collective-permute-start.10 = (bf16[64,2048]{1,0:T(8,128)(2,1)}, bf16[64,2048]{1,0:T(8,128)(2,1)S(1)}, u32[]{:S(2)}, u32[]{:S(2)}) collective-permute-start(bf16[64,2048]{1,0:T(8,128)(2,1)} %add.13.refs_0_), channel_id=1, source_target_pairs={{0,32},{8,40},{16,48},{24,56},{32,0},{40,8},{48,16},{56,24},{64,96... | collective-permute-start | bytes 786440 | tf_op jit(solution)/shard_map/ppermute | solution.py:344
  158.7 13.2 %collective-permute-start.9 = (bf16[64,2048]{1,0:T(8,128)(2,1)}, bf16[64,2048]{1,0:T(8,128)(2,1)S(1)}, u32[]{:S(2)}, u32[]{:S(2)}) collective-permute-start(bf16[64,2048]{1,0:T(8,128)(2,1)} %add.13.refs_0_), channel_id=1, source_target_pairs={{0,16},{8,24},{16,32},{24,40},{32,48},{40,56},{48,0},{56,8},{64,80... | collective-permute-start | bytes 786440 | tf_op jit(solution)/shard_map/ppermute | solution.py:344
  159.3 12.6 %collective-permute-start.12 = (bf16[64,2048]{1,0:T(8,128)(2,1)}, bf16[64,2048]{1,0:T(8,128)(2,1)S(1)}, u32[]{:S(2)}, u32[]{:S(2)}) collective-permute-start(bf16[64,2048]{1,0:T(8,128)(2,1)} %add.13.refs_0_), channel_id=1, source_target_pairs={{0,8},{8,0},{16,24},{24,16},{32,40},{40,32},{48,56},{56,48},{64,72... | collective-permute-start | bytes 786440 | tf_op jit(solution)/shard_map/ppermute | solution.py:344
  168.6 4.8 %copy-start.2 = (bf16[64,2048]{1,0:T(8,128)(2,1)}, bf16[64,2048]{1,0:T(8,128)(2,1)S(1)}, u32[]{:S(2)}) copy-start(bf16[64,2048]{1,0:T(8,128)(2,1)S(1)} %collective-permute-done.11.refs_3_) | copy-start | bytes 786436
  168.6 3.3 %collective-permute-start.15 = (bf16[64,2048]{1,0:T(8,128)(2,1)S(1)}, bf16[64,2048]{1,0:T(8,128)(2,1)S(1)}, u32[]{:S(2)}, u32[]{:S(2)}) collective-permute-start(bf16[64,2048]{1,0:T(8,128)(2,1)S(1)} %collective-permute-done.11.refs_3_), channel_id=1, source_target_pairs={{0,8},{8,0},{16,24},{24,16},{32,40},{40,32},{48,56},{56,48},{64,72... | collective-permute-start | bytes 786440 | tf_op jit(solution)/shard_map/ppermute | solution.py:344
  168.7 4.8 %copy-start.3 = (bf16[64,2048]{1,0:T(8,128)(2,1)}, bf16[64,2048]{1,0:T(8,128)(2,1)S(1)}, u32[]{:S(2)}) copy-start(bf16[64,2048]{1,0:T(8,128)(2,1)S(1)} %collective-permute-done.10.refs_2_) | copy-start | bytes 786436
  168.7 3.3 %collective-permute-start.14 = (bf16[64,2048]{1,0:T(8,128)(2,1)S(1)}, bf16[64,2048]{1,0:T(8,128)(2,1)S(1)}, u32[]{:S(2)}, u32[]{:S(2)}) collective-permute-start(bf16[64,2048]{1,0:T(8,128)(2,1)S(1)} %collective-permute-done.10.refs_2_), channel_id=1, source_target_pairs={{0,8},{8,0},{16,24},{24,16},{32,40},{40,32},{48,56},{56,48},{64,72... | collective-permute-start | bytes 786440 | tf_op jit(solution)/shard_map/ppermute | solution.py:344
  171.9 1.5 copy-start.4
  171.9 1.5 collective-permute-start.13
  171.9 1.5 copy-start.5
  172.0 1.5 copy-start.6
  172.0 1.5 copy-start.7
  173.5 0.7 copy-start.8
  (4 other events, 2.7 us)

commit v5 on v4

--- a/solution.py
+++ b/solution.py
@@ -18,6 +18,7 @@
 LATPAD = 640
 LOG2E = 1.4426950408889634
 VMEM = 56 * 1024 * 1024
+LITTLE = pltpu.CompilerParams(vmem_limit_bytes=VMEM // 4)
 SMALL = pl.CostEstimate(flops=1, bytes_accessed=1, transcendentals=0)
 EARLY = 3
 LINE = 4
@@ -147,7 +148,7 @@
             pltpu.VMEM(part.shape, part.dtype),
         ],
         input_output_aliases={0: 0} if has else {},
-        compiler_params=pltpu.CompilerParams(vmem_limit_bytes=VMEM // 4),
+        compiler_params=LITTLE,
         cost_estimate=SMALL,
         name="unpack",
     )(*([total] * has + [part]))
@@ -362,7 +363,9 @@
 
 def add(*parts):
     cost = pl.CostEstimate(flops=ADD_FLOPS, bytes_accessed=1, transcendentals=0)
-    return pl.pallas_call(add_kernel, out_shape=parts[0], cost_estimate=cost, name="add")(*parts)
+    return pl.pallas_call(
+        add_kernel, out_shape=parts[0], compiler_params=LITTLE, cost_estimate=cost, name="add"
+    )(*parts)
 
 
 def split_kernel(keep_ref, got_ref, *out_refs):
@@ -375,9 +378,9 @@
 def split(keep, got):
     shape = jax.ShapeDtypeStruct((keep.shape[0] // LINE, keep.shape[1]), keep.dtype)
     shapes = [shape] * LINE
-    return pl.pallas_call(split_kernel, out_shape=shapes, cost_estimate=SMALL, name="split")(
-        keep, got
-    )
+    return pl.pallas_call(
+        split_kernel, out_shape=shapes, compiler_params=LITTLE, cost_estimate=SMALL, name="split"
+    )(keep, got)
 
 
 def swap(x):
@@ -403,9 +406,9 @@
     rows = first[0].shape[0]
     shape = jax.ShapeDtypeStruct((rows, first[0].shape[1] + second[0].shape[1]), first[0].dtype)
     kernel = functools.partial(merge_kernel, len(first))
-    return pl.pallas_call(kernel, out_shape=shape, cost_estimate=SMALL, name="merge")(
-        *first, *second
-    )
+    return pl.pallas_call(
+        kernel, out_shape=shape, compiler_params=LITTLE, cost_estimate=SMALL, name="merge"
+    )(*first, *second)
 
 
 def across(part):
@@ -430,7 +433,7 @@
         in_specs=[pl.BlockSpec(memory_space=pltpu.SMEM)] + [vmem] * (2 * LINE),
         out_specs=vmem,
         out_shape=jax.ShapeDtypeStruct((LATENT, mine[0].shape[1]), jnp.float32),
-        compiler_params=pltpu.CompilerParams(vmem_limit_bytes=VMEM),
+        compiler_params=LITTLE,
         cost_estimate=SMALL,
         name="place",
     )(place, *mine, *other)

time: 182 us -> 176 us (0.967)
  Pallas kernels: 56.3 us -> 47.8 us
  waiting for transfers between devices: 20.3 us -> 23.8 us
  local copies, waits for them, and re-layouts: 4.21 us -> 2.1 us
    pallas_call x4, Pallas kernels: 7.95 us -> 0.44 us  [the longest x2 0.24 us: split(): pl.pallas_call(split_kernel, out_shape=shapes, compiler_params=LITTLE, co...]
    all_to_all x3, waiting for transfers between devices: 1.3 us -> 4.85 us  [exchange(): lax.all_to_all(x, axis, split_axis=0, concat_axis=0, tiled=True, axis_ind...]
    unnamed x34 -> x10, local copies, waits for them, and re-layouts: 4.21 us -> 2.1 us
  transfers between devices with their start and end apart: 19 -> 19, of which waited for: 7 -> 7; matrix products, arithmetic and copies ran while one was open for 0% -> 0% of each run, Pallas kernels for 27% -> 23%
where the time goes in v5:
time: 176 us; the launch traced here: 175 us
  blocking collectives  67 us (38%)
  Pallas kernels  47.8 us (27%)
  starting transfers between devices  32.6 us (19%)
  waiting for transfers between devices  23.8 us (14%)
  local copies, waits for them, and re-layouts  2.1 us (1%)
    all_to_all x1, blocking collectives, exchange(): lax.all_to_all(x, axis, split_axis=0, concat_axis=0, tiled=True, axis_ind...  67 us
    pallas_call x2, Pallas kernels, attend(): pl.pallas_call(functools.partial(attend_kernel, pairs, total is not None,...  34.7 us
    ppermute x16, waiting for transfers between devices, send(): return lax.ppermute(x, 'dp', [(i, step(i)) for i in range(slabs)])  18.9 us
    ppermute x16, starting transfers between devices, send(): return lax.ppermute(x, 'dp', [(i, step(i)) for i in range(slabs)])  18.5 us
    all_to_all x3, starting transfers between devices, exchange(): lax.all_to_all(x, axis, split_axis=0, concat_axis=0, tiled=True, axis_ind...  14 us
    pallas_call x1, Pallas kernels, pack(): pl.pallas_call(functools.partial(pack_kernel, plans), in_specs=[hbm, hbm,...  5.97 us
    all_to_all x3, waiting for transfers between devices, exchange(): lax.all_to_all(x, axis, split_axis=0, concat_axis=0, tiled=True, axis_ind...  4.85 us
    pallas_call x2, Pallas kernels, unpack(): pl.pallas_call(functools.partial(unpack_kernel, first, pairs, has, with_l...  3.82 us
  transfers between devices with their start and end apart: 19, of which 7 were waited for; matrix products, arithmetic and copies ran while one was open for 0% of the time, Pallas kernels for 23%

profile of v5, /device:TPU:0, one launch (start us, length us, event | category | flops | bytes accessed | tf_op | source)
XLA Modules:
  0.0 174.9 jit_solution(4893837333124407919)
XLA Ops:
  0.7 0.7 pad_add_fusion.refs_0_.place
  1.3 6.0 %pack.1 = (bf16[8,128,2560]{2,1,0:T(8,128)(2,1)}, bf16[8,128,640]{2,1,0:T(8,128)(2,1)}) custom-call(bf16[128,12288]{1,0:T(8,128)(2,1)} %bitcast.20, bf16[128,8192]{1,0:T(8,128)(2,1)} %bitcast.23, bf16[576,128]{1,0:T(8,128)(2,1)} %bitcast.25), custom_call_target="tpu_custom_call" | custom-call | bytes 13107200 | tf_op jit(solution)/shard_map/pack/pallas_call | solution.py:82
  7.3 67.0 %all_to_all.20 = bf16[8,128,2560]{2,1,0:T(8,128)(2,1)} all-to-all(bf16[8,128,2560]{2,1,0:T(8,128)(2,1)} %get-tuple-element.37), channel_id=1, replica_groups=mesh['dp'=16,'seq'=8] {'seq'}, dimensions={0} | all-to-all | bytes 10485760 | tf_op jit(solution)/shard_map/all_to_all | solution.py:340
  74.3 3.6 %all-to-all-start.1 = ((bf16[8,128,640]{2,1,0:T(8,128)(2,1)}), bf16[8,128,640]{2,1,0:T(8,128)(2,1)S(1)}, u32[]{:S(2)}, u32[]{:S(2)}) async-start(bf16[8,128,640]{2,1,0:T(8,128)(2,1)} %get-tuple-element.39), calls=%async_computation.1 | async-start | bytes 2621440 | tf_op jit(solution)/shard_map/all_to_all | solution.py:340
  77.9 24.0 %attend.2 = (bf16[1024,1152]{1,0:T(8,128)(2,1)}, bf16[256,1536]{1,0:T(8,128)(2,1)}, bf16[256,1536]{1,0:T(8,128)(2,1)}, f32[1024,640]{1,0:T(8,128)}) custom-call(s32[2]{0:T(128)} %pad_add_fusion.refs_0_.place, bf16[1024,2560]{1,0:T(8,128)(2,1)} %bitcast.16, bf16[512,2048]{1,0:T(8,128)(2,1)} %refs_2_.3, bf16[1024,2560]{1,0:T(8,128)(2,1)} %bitcast.17, ...), custom_call_target="tpu_custom_call" | custom-call | flops 15000000512 | bytes 18000000 | tf_op jit(solution)/shard_map/attend/pallas_call | solution.py:318
  102.0 1.1 copy-done.3
  103.1 5.6 %all-to-all-start.2 = ((bf16[8,128,1152]{2,1,0:T(8,128)(2,1)}), bf16[8,128,1152]{2,1,0:T(8,128)(2,1)S(1)}, u32[]{:S(2)}, u32[]{:S(2)}) async-start(bf16[8,128,1152]{2,1,0:T(8,128)(2,1)} %bitcast.21), calls=%async_computation.2 | async-start | bytes 4718592 | tf_op jit(solution)/shard_map/all_to_all | solution.py:340
  109.0 10.7 %attend.3 = (bf16[1024,1024]{1,0:T(8,128)(2,1)}, bf16[256,512]{1,0:T(8,128)(2,1)}, bf16[256,512]{1,0:T(8,128)(2,1)}) custom-call(s32[2]{0:T(128)} %pad_add_fusion.refs_0_.place, bf16[1024,2560]{1,0:T(8,128)(2,1)} %bitcast.19, bf16[512,2048]{1,0:T(8,128)(2,1)} %refs_2_.3, bf16[1024,640]{1,0:T(8,128)(2,1)} %bitcast.24, f32[1024,640]{1,0:T(8,128)} %get-tuple-element.40.refs_4_), custom_call_target="tpu_custom_call" | custom-call | flops 5000000000 | bytes 6000000 | tf_op jit(solution)/shard_map/attend/pallas_call | solution.py:318
  119.7 0.5 collective-permute-start.4
  120.4 1.6 collective-permute-start.1
  122.0 2.7 %collective-permute-start.2 = (bf16[64,1536]{1,0:T(8,128)(2,1)S(1)}, bf16[64,1536]{1,0:T(8,128)(2,1)S(1)}, u32[]{:S(2)}, u32[]{:S(2)}) collective-permute-start(bf16[64,1536]{1,0:T(8,128)(2,1)S(1)} %get-tuple-element.52), channel_id=1, source_target_pairs={{0,32},{8,40},{16,48},{24,56},{32,0},{40,8},{48,16},{56,24},{64,96... | collective-permute-start | bytes 589832 | tf_op jit(solution)/shard_map/ppermute | solution.py:345
  124.7 1.4 collective-permute-start.3
  126.1 0.9 copy-done.1
  127.1 0.7 collective-permute-start.5
  127.8 0.9 collective-permute-start.6
  128.7 2.3 %collective-permute-start.7 = (bf16[64,512]{1,0:T(8,128)(2,1)S(1)}, bf16[64,512]{1,0:T(8,128)(2,1)S(1)}, u32[]{:S(2)}, u32[]{:S(2)}) collective-permute-start(bf16[64,512]{1,0:T(8,128)(2,1)S(1)} %get-tuple-element.59), channel_id=1, source_target_pairs={{0,48},{8,56},{16,0},{24,8},{32,16},{40,24},{48,32},{56,40},{64,11... | collective-permute-start | bytes 196616 | tf_op jit(solution)/shard_map/ppermute | solution.py:345
  131.0 3.7 %collective-permute-done.2.refs_2_ = bf16[64,1536]{1,0:T(8,128)(2,1)S(1)} collective-permute-done((bf16[64,1536]{1,0:T(8,128)(2,1)S(1)}, bf16[64,1536]{1,0:T(8,128)(2,1)S(1)}, u32[]{:S(2)}, u32[]{:S(2)}) %collective-permute-start.2) | collective-permute-done | bytes 196640 | tf_op jit(solution)/shard_map/ppermute | solution.py:345
  134.7 1.0 collective-permute-done.5.refs_5_
  135.7 0.9 collective-permute-done.6.refs_6_
  136.7 3.7 %collective-permute-start.8 = (bf16[64,2048]{1,0:T(8,128)(2,1)S(1)}, bf16[64,2048]{1,0:T(8,128)(2,1)S(1)}, u32[]{:S(2)}, u32[]{:S(2)}) collective-permute-start(bf16[64,2048]{1,0:T(8,128)(2,1)S(1)} %merge.1.refs_0_), channel_id=1, source_target_pairs={{0,64},{8,72},{16,80},{24,88},{32,96},{40,104},{48,112},{56,120},{... | collective-permute-start | bytes 786440 | tf_op jit(solution)/shard_map/ppermute | solution.py:345
  140.4 2.0 %unpack.2.refs_0_ = bf16[128,12288]{1,0:T(8,128)(2,1)} custom-call(bf16[8,128,1152]{2,1,0:T(8,128)(2,1)S(1)} %all-to-all-done.2.refs_0_), custom_call_target="tpu_custom_call" | custom-call | flops 1 | bytes 1 | tf_op jit(solution)/shard_map/unpack/pallas_call | solution.py:141
  142.4 4.8 %all-to-all-start.3 = ((bf16[8,128,1024]{2,1,0:T(8,128)(2,1)}), bf16[8,128,1024]{2,1,0:T(8,128)(2,1)S(1)}, u32[]{:S(2)}, u32[]{:S(2)}) async-start(bf16[8,128,1024]{2,1,0:T(8,128)(2,1)} %bitcast.22), calls=%async_computation.3 | async-start | bytes 4194304 | tf_op jit(solution)/shard_map/all_to_all | solution.py:340
  147.3 2.3 %collective-permute-start.11 = (bf16[64,2048]{1,0:T(8,128)(2,1)S(1)}, bf16[64,2048]{1,0:T(8,128)(2,1)S(1)}, u32[]{:S(2)}, u32[]{:S(2)}) collective-permute-start(bf16[64,2048]{1,0:T(8,128)(2,1)S(1)} %add.13.refs_0_), channel_id=1, source_target_pairs={{0,48},{8,56},{16,0},{24,8},{32,16},{40,24},{48,32},{56,40},{64,11... | collective-permute-start | bytes 786440 | tf_op jit(solution)/shard_map/ppermute | solution.py:345
  149.6 1.2 collective-permute-start.10
  150.8 0.7 collective-permute-start.9
  151.4 8.9 %collective-permute-done.11.refs_3_ = bf16[64,2048]{1,0:T(8,128)(2,1)S(1)} collective-permute-done((bf16[64,2048]{1,0:T(8,128)(2,1)S(1)}, bf16[64,2048]{1,0:T(8,128)(2,1)S(1)}, u32[]{:S(2)}, u32[]{:S(2)}) %collective-permute-start.11) | collective-permute-done | bytes 262176 | tf_op jit(solution)/shard_map/ppermute | solution.py:345
  160.4 0.5 collective-permute-start.14
  160.8 2.9 %collective-permute-done.9.refs_1_ = bf16[64,2048]{1,0:T(8,128)(2,1)S(1)} collective-permute-done((bf16[64,2048]{1,0:T(8,128)(2,1)S(1)}, bf16[64,2048]{1,0:T(8,128)(2,1)S(1)}, u32[]{:S(2)}, u32[]{:S(2)}) %collective-permute-start.9) | collective-permute-done | bytes 262176 | tf_op jit(solution)/shard_map/ppermute | solution.py:345
  163.8 1.5 collective-permute-done.13.refs_5_
  165.3 2.8 %place.1 = f32[512,2048]{1,0:T(8,128)} custom-call(s32[2]{0:T(128)S(1)} %copy-done.2, bf16[64,2048]{1,0:T(8,128)(2,1)S(1)} %add.13.refs_0_, bf16[64,2048]{1,0:T(8,128)(2,1)S(1)} %collective-permute-done.9.refs_1_, bf16[64,2048]{1,0:T(8,128)(2,1)S(1)} %collective-permute-done.10.refs_2_, bf16[64,2048]{1,0:T(8,128)(2,1)S(1)} %collective-permute-done.11.refs_3_, ...), custom_call_target="tpu_custom_call" | custom-call | flops 1 | bytes 1 | tf_op jit(solution)/shard_map/place/pallas_call | solution.py:431
  168.1 4.8 %all-to-all-done.3.refs_1_ = bf16[8,128,1024]{2,1,0:T(8,128)(2,1)S(1)} async-done(((bf16[8,128,1024]{2,1,0:T(8,128)(2,1)}), bf16[8,128,1024]{2,1,0:T(8,128)(2,1)S(1)}, u32[]{:S(2)}, u32[]{:S(2)}) %all-to-all-start.3) | async-done | bytes 2097184 | tf_op jit(solution)/shard_map/all_to_all | solution.py:340
  172.9 1.8 %unpack.3 = (bf16[128,12288]{1,0:T(8,128)(2,1)}, bf16[576,128]{1,0:T(8,128)(2,1)}) custom-call(bf16[128,12288]{1,0:T(8,128)(2,1)} %unpack.2.refs_0_, bf16[8,128,1024]{2,1,0:T(8,128)(2,1)S(1)} %all-to-all-done.3.refs_1_), custom_call_target="tpu_custom_call", output_to_operand_aliasing={{0}: (0, {})} | custom-call | flops 1 | bytes 1 | tf_op jit(solution)/shard_map/unpack/pallas_call | solution.py:141
  (28 shorter events, 0.8 us)
Async XLA Ops:
  74.3 27.6 %all-to-all-start.1 = ((bf16[8,128,640]{2,1,0:T(8,128)(2,1)}), bf16[8,128,640]{2,1,0:T(8,128)(2,1)S(1)}, u32[]{:S(2)}, u32[]{:S(2)}) async-start(bf16[8,128,640]{2,1,0:T(8,128)(2,1)} %get-tuple-element.39), calls=%async_computation.1 | async-start | bytes 2621440 | tf_op jit(solution)/shard_map/all_to_all | solution.py:340
  102.0 1.2 copy-start.3
  102.0 6.8 %copy-start.4 = (bf16[256,1536]{1,0:T(8,128)(2,1)S(1)}, bf16[256,1536]{1,0:T(8,128)(2,1)}, u32[]{:S(2)}) copy-start(bf16[256,1536]{1,0:T(8,128)(2,1)} %get-tuple-element.45) | copy-start | bytes 2359300
  103.1 37.2 %all-to-all-start.2 = ((bf16[8,128,1152]{2,1,0:T(8,128)(2,1)}), bf16[8,128,1152]{2,1,0:T(8,128)(2,1)S(1)}, u32[]{:S(2)}, u32[]{:S(2)}) async-start(bf16[8,128,1152]{2,1,0:T(8,128)(2,1)} %bitcast.21), calls=%async_computation.2 | async-start | bytes 4718592 | tf_op jit(solution)/shard_map/all_to_all | solution.py:340
  108.8 11.0 %collective-permute-start = (bf16[256,1536]{1,0:T(8,128)(2,1)S(1)}, bf16[256,1536]{1,0:T(8,128)(2,1)S(1)}, u32[]{:S(2)}, u32[]{:S(2)}) collective-permute-start(bf16[256,1536]{1,0:T(8,128)(2,1)S(1)} %copy-done.4), channel_id=1, source_target_pairs={{0,8},{8,0},{16,24},{24,16},{32,40},{40,32},{48,56},{56,48},{64,72... | collective-permute-start | bytes 2359304 | tf_op jit(solution)/shard_map/ppermute | solution.py:345
  109.0 11.2 %copy-start = (bf16[256,1536]{1,0:T(8,128)(2,1)S(1)}, bf16[256,1536]{1,0:T(8,128)(2,1)}, u32[]{:S(2)}) copy-start(bf16[256,1536]{1,0:T(8,128)(2,1)} %get-tuple-element.48.keep_ref) | copy-start | bytes 2359300
  119.7 6.4 %collective-permute-start.4 = (bf16[256,512]{1,0:T(8,128)(2,1)}, bf16[256,512]{1,0:T(8,128)(2,1)S(1)}, u32[]{:S(2)}, u32[]{:S(2)}) collective-permute-start(bf16[256,512]{1,0:T(8,128)(2,1)} %get-tuple-element.55), channel_id=1, source_target_pairs={{0,8},{8,0},{16,24},{24,16},{32,40},{40,32},{48,56},{56,48},{64,72... | collective-permute-start | bytes 786440 | tf_op jit(solution)/shard_map/ppermute | solution.py:345
  120.4 8.3 %collective-permute-start.1 = (bf16[64,1536]{1,0:T(8,128)(2,1)S(1)}, bf16[64,1536]{1,0:T(8,128)(2,1)S(1)}, u32[]{:S(2)}, u32[]{:S(2)}) collective-permute-start(bf16[64,1536]{1,0:T(8,128)(2,1)S(1)} %get-tuple-element.51), channel_id=1, source_target_pairs={{0,16},{8,24},{16,32},{24,40},{32,48},{40,56},{48,0},{56,8},{64,80... | collective-permute-start | bytes 589832 | tf_op jit(solution)/shard_map/ppermute | solution.py:345
  122.0 12.8 %collective-permute-start.2 = (bf16[64,1536]{1,0:T(8,128)(2,1)S(1)}, bf16[64,1536]{1,0:T(8,128)(2,1)S(1)}, u32[]{:S(2)}, u32[]{:S(2)}) collective-permute-start(bf16[64,1536]{1,0:T(8,128)(2,1)S(1)} %get-tuple-element.52), channel_id=1, source_target_pairs={{0,32},{8,40},{16,48},{24,56},{32,0},{40,8},{48,16},{56,24},{64,96... | collective-permute-start | bytes 589832 | tf_op jit(solution)/shard_map/ppermute | solution.py:345
  124.7 10.0 %collective-permute-start.3 = (bf16[64,1536]{1,0:T(8,128)(2,1)S(1)}, bf16[64,1536]{1,0:T(8,128)(2,1)S(1)}, u32[]{:S(2)}, u32[]{:S(2)}) collective-permute-start(bf16[64,1536]{1,0:T(8,128)(2,1)S(1)} %get-tuple-element.53), channel_id=1, source_target_pairs={{0,48},{8,56},{16,0},{24,8},{32,16},{40,24},{48,32},{56,40},{64,11... | collective-permute-start | bytes 589832 | tf_op jit(solution)/shard_map/ppermute | solution.py:345
  126.1 1.0 copy-start.1
  127.1 8.6 %collective-permute-start.5 = (bf16[64,512]{1,0:T(8,128)(2,1)S(1)}, bf16[64,512]{1,0:T(8,128)(2,1)S(1)}, u32[]{:S(2)}, u32[]{:S(2)}) collective-permute-start(bf16[64,512]{1,0:T(8,128)(2,1)S(1)} %get-tuple-element.57), channel_id=1, source_target_pairs={{0,16},{8,24},{16,32},{24,40},{32,48},{40,56},{48,0},{56,8},{64,80... | collective-permute-start | bytes 196616 | tf_op jit(solution)/shard_map/ppermute | solution.py:345
  127.8 8.8 %collective-permute-start.6 = (bf16[64,512]{1,0:T(8,128)(2,1)S(1)}, bf16[64,512]{1,0:T(8,128)(2,1)S(1)}, u32[]{:S(2)}, u32[]{:S(2)}) collective-permute-start(bf16[64,512]{1,0:T(8,128)(2,1)S(1)} %get-tuple-element.58), channel_id=1, source_target_pairs={{0,32},{8,40},{16,48},{24,56},{32,0},{40,8},{48,16},{56,24},{64,96... | collective-permute-start | bytes 196616 | tf_op jit(solution)/shard_map/ppermute | solution.py:345
  128.7 7.9 %collective-permute-start.7 = (bf16[64,512]{1,0:T(8,128)(2,1)S(1)}, bf16[64,512]{1,0:T(8,128)(2,1)S(1)}, u32[]{:S(2)}, u32[]{:S(2)}) collective-permute-start(bf16[64,512]{1,0:T(8,128)(2,1)S(1)} %get-tuple-element.59), channel_id=1, source_target_pairs={{0,48},{8,56},{16,0},{24,8},{32,16},{40,24},{48,32},{56,40},{64,11... | collective-permute-start | bytes 196616 | tf_op jit(solution)/shard_map/ppermute | solution.py:345
  136.7 10.5 %collective-permute-start.8 = (bf16[64,2048]{1,0:T(8,128)(2,1)S(1)}, bf16[64,2048]{1,0:T(8,128)(2,1)S(1)}, u32[]{:S(2)}, u32[]{:S(2)}) collective-permute-start(bf16[64,2048]{1,0:T(8,128)(2,1)S(1)} %merge.1.refs_0_), channel_id=1, source_target_pairs={{0,64},{8,72},{16,80},{24,88},{32,96},{40,104},{48,112},{56,120},{... | collective-permute-start | bytes 786440 | tf_op jit(solution)/shard_map/ppermute | solution.py:345
  142.4 30.6 %all-to-all-start.3 = ((bf16[8,128,1024]{2,1,0:T(8,128)(2,1)}), bf16[8,128,1024]{2,1,0:T(8,128)(2,1)S(1)}, u32[]{:S(2)}, u32[]{:S(2)}) async-start(bf16[8,128,1024]{2,1,0:T(8,128)(2,1)} %bitcast.22), calls=%async_computation.3 | async-start | bytes 4194304 | tf_op jit(solution)/shard_map/all_to_all | solution.py:340
  147.2 18.0 %copy-start.2 = (s32[2]{0:T(128)S(1)}, s32[2]{0:T(128)}, u32[]{:S(2)}) copy-start(s32[2]{0:T(128)} %pad_add_fusion.refs_0_.place) | copy-start | bytes 28
  147.3 13.0 %collective-permute-start.11 = (bf16[64,2048]{1,0:T(8,128)(2,1)S(1)}, bf16[64,2048]{1,0:T(8,128)(2,1)S(1)}, u32[]{:S(2)}, u32[]{:S(2)}) collective-permute-start(bf16[64,2048]{1,0:T(8,128)(2,1)S(1)} %add.13.refs_0_), channel_id=1, source_target_pairs={{0,48},{8,56},{16,0},{24,8},{32,16},{40,24},{48,32},{56,40},{64,11... | collective-permute-start | bytes 786440 | tf_op jit(solution)/shard_map/ppermute | solution.py:345
  149.6 10.8 %collective-permute-start.10 = (bf16[64,2048]{1,0:T(8,128)(2,1)S(1)}, bf16[64,2048]{1,0:T(8,128)(2,1)S(1)}, u32[]{:S(2)}, u32[]{:S(2)}) collective-permute-start(bf16[64,2048]{1,0:T(8,128)(2,1)S(1)} %add.13.refs_0_), channel_id=1, source_target_pairs={{0,32},{8,40},{16,48},{24,56},{32,0},{40,8},{48,16},{56,24},{64,96... | collective-permute-start | bytes 786440 | tf_op jit(solution)/shard_map/ppermute | solution.py:345
  150.8 13.0 %collective-permute-start.9 = (bf16[64,2048]{1,0:T(8,128)(2,1)S(1)}, bf16[64,2048]{1,0:T(8,128)(2,1)S(1)}, u32[]{:S(2)}, u32[]{:S(2)}) collective-permute-start(bf16[64,2048]{1,0:T(8,128)(2,1)S(1)} %add.13.refs_0_), channel_id=1, source_target_pairs={{0,16},{8,24},{16,32},{24,40},{32,48},{40,56},{48,0},{56,8},{64,80... | collective-permute-start | bytes 786440 | tf_op jit(solution)/shard_map/ppermute | solution.py:345
  151.4 12.3 %collective-permute-start.12 = (bf16[64,2048]{1,0:T(8,128)(2,1)S(1)}, bf16[64,2048]{1,0:T(8,128)(2,1)S(1)}, u32[]{:S(2)}, u32[]{:S(2)}) collective-permute-start(bf16[64,2048]{1,0:T(8,128)(2,1)S(1)} %add.13.refs_0_), channel_id=1, source_target_pairs={{0,8},{8,0},{16,24},{24,16},{32,40},{40,32},{48,56},{56,48},{64,72... | collective-permute-start | bytes 786440 | tf_op jit(solution)/shard_map/ppermute | solution.py:345
  160.3 3.4 %collective-permute-start.15 = (bf16[64,2048]{1,0:T(8,128)(2,1)S(1)}, bf16[64,2048]{1,0:T(8,128)(2,1)S(1)}, u32[]{:S(2)}, u32[]{:S(2)}) collective-permute-start(bf16[64,2048]{1,0:T(8,128)(2,1)S(1)} %collective-permute-done.11.refs_3_), channel_id=1, source_target_pairs={{0,8},{8,0},{16,24},{24,16},{32,40},{40,32},{48,56},{56,48},{64,72... | collective-permute-start | bytes 786440 | tf_op jit(solution)/shard_map/ppermute | solution.py:345
  160.4 3.4 %collective-permute-start.14 = (bf16[64,2048]{1,0:T(8,128)(2,1)S(1)}, bf16[64,2048]{1,0:T(8,128)(2,1)S(1)}, u32[]{:S(2)}, u32[]{:S(2)}) collective-permute-start(bf16[64,2048]{1,0:T(8,128)(2,1)S(1)} %collective-permute-done.10.refs_2_), channel_id=1, source_target_pairs={{0,8},{8,0},{16,24},{24,16},{32,40},{40,32},{48,56},{56,48},{64,72... | collective-permute-start | bytes 786440 | tf_op jit(solution)/shard_map/ppermute | solution.py:345
  163.7 1.5 collective-permute-start.13

commit v6 on v5

--- a/solution.py
+++ b/solution.py
@@ -328,7 +328,7 @@
             pltpu.VMEM((span, 2 * NOPE), f32),
             pltpu.VMEM((span, VDIM), f32),
         ],
-        compiler_params=pltpu.CompilerParams(vmem_limit_bytes=VMEM),
+        compiler_params=pltpu.CompilerParams(vmem_limit_bytes=VMEM * 3 // 4 if last else VMEM),
         cost_estimate=pl.CostEstimate(
             flops=pairs * 5_000_000_000, bytes_accessed=pairs * 6_000_000, transcendentals=0
         ),

time: 176 us -> 178 us (1.011)
  local copies, waits for them, and re-layouts: 2.1 us -> 5.71 us
  Pallas kernels: 47.8 us -> 45.1 us
    unnamed x10 -> x16, local copies, waits for them, and re-layouts: 2.1 us -> 5.71 us
    pallas_call x2, Pallas kernels: 34.7 us -> 32 us  [attend(): pl.pallas_call(functools.partial(attend_kernel, pairs, total is not None,...]
  transfers between devices with their start and end apart: 19 -> 19, of which waited for: 7 -> 8; matrix products, arithmetic and copies ran while one was open for 0% -> 0% of each run, Pallas kernels for 23% -> 21%
where the time goes in v6:
time: 178 us; the launch traced here: 177 us
  blocking collectives  67 us (38%)
  Pallas kernels  45.1 us (25%)
  starting transfers between devices  33.1 us (19%)
  waiting for transfers between devices  24.5 us (14%)
  local copies, waits for them, and re-layouts  5.71 us (3%)
    all_to_all x1, blocking collectives, exchange(): lax.all_to_all(x, axis, split_axis=0, concat_axis=0, tiled=True, axis_ind...  67 us
    pallas_call x2, Pallas kernels, attend(): pl.pallas_call(functools.partial(attend_kernel, pairs, total is not None,...  32 us
    ppermute x16, waiting for transfers between devices, send(): return lax.ppermute(x, 'dp', [(i, step(i)) for i in range(slabs)])  19.6 us
    ppermute x16, starting transfers between devices, send(): return lax.ppermute(x, 'dp', [(i, step(i)) for i in range(slabs)])  18.9 us
    all_to_all x3, starting transfers between devices, exchange(): lax.all_to_all(x, axis, split_axis=0, concat_axis=0, tiled=True, axis_ind...  14.2 us
    pallas_call x1, Pallas kernels, pack(): pl.pallas_call(functools.partial(pack_kernel, plans), in_specs=[hbm, hbm,...  5.97 us
    unnamed x16, local copies, waits for them, and re-layouts  5.71 us
    all_to_all x3, waiting for transfers between devices, exchange(): lax.all_to_all(x, axis, split_axis=0, concat_axis=0, tiled=True, axis_ind...  4.86 us
  transfers between devices with their start and end apart: 19, of which 8 were waited for; matrix products, arithmetic and copies ran while one was open for 0% of the time, Pallas kernels for 21%

profile of v6, /device:TPU:0, one launch (start us, length us, event | category | flops | bytes accessed | tf_op | source)
XLA Modules:
  0.0 177.0 jit_solution(9293077089284868075)
XLA Ops:
  0.7 0.7 pad_add_fusion.refs_0_.place
  1.3 6.0 %pack.1 = (bf16[8,128,2560]{2,1,0:T(8,128)(2,1)}, bf16[8,128,640]{2,1,0:T(8,128)(2,1)}) custom-call(bf16[128,12288]{1,0:T(8,128)(2,1)} %bitcast.22, bf16[128,8192]{1,0:T(8,128)(2,1)} %bitcast.24, bf16[576,128]{1,0:T(8,128)(2,1)} %bitcast.25), custom_call_target="tpu_custom_call" | custom-call | bytes 13107200 | tf_op jit(solution)/shard_map/pack/pallas_call | solution.py:82
  7.3 67.0 %all_to_all.20 = bf16[8,128,2560]{2,1,0:T(8,128)(2,1)} all-to-all(bf16[8,128,2560]{2,1,0:T(8,128)(2,1)} %get-tuple-element.37), channel_id=1, replica_groups=mesh['dp'=16,'seq'=8] {'seq'}, dimensions={0} | all-to-all | bytes 10485760 | tf_op jit(solution)/shard_map/all_to_all | solution.py:340
  74.3 3.6 %all-to-all-start.1 = ((bf16[8,128,640]{2,1,0:T(8,128)(2,1)}), bf16[8,128,640]{2,1,0:T(8,128)(2,1)S(1)}, u32[]{:S(2)}, u32[]{:S(2)}) async-start(bf16[8,128,640]{2,1,0:T(8,128)(2,1)} %get-tuple-element.39), calls=%async_computation.1 | async-start | bytes 2621440 | tf_op jit(solution)/shard_map/all_to_all | solution.py:340
  77.9 24.0 %attend.2 = (bf16[1024,1152]{1,0:T(8,128)(2,1)}, bf16[256,1536]{1,0:T(8,128)(2,1)}, bf16[256,1536]{1,0:T(8,128)(2,1)}, f32[1024,640]{1,0:T(8,128)}) custom-call(s32[2]{0:T(128)} %pad_add_fusion.refs_0_.place, bf16[1024,2560]{1,0:T(8,128)(2,1)} %bitcast.18, bf16[512,2048]{1,0:T(8,128)(2,1)} %refs_2_.3, bf16[1024,2560]{1,0:T(8,128)(2,1)} %bitcast.19, ...), custom_call_target="tpu_custom_call" | custom-call | flops 15000000512 | bytes 18000000 | tf_op jit(solution)/shard_map/attend/pallas_call | solution.py:318
  102.0 1.1 copy-done.1
  103.0 5.8 %all-to-all-start.2 = ((bf16[8,128,1152]{2,1,0:T(8,128)(2,1)}), bf16[8,128,1152]{2,1,0:T(8,128)(2,1)S(1)}, u32[]{:S(2)}, u32[]{:S(2)}) async-start(bf16[8,128,1152]{2,1,0:T(8,128)(2,1)} %bitcast.23), calls=%async_computation.2 | async-start | bytes 4718592 | tf_op jit(solution)/shard_map/all_to_all | solution.py:340
  109.1 1.3 copy-done.2
  110.4 1.6 copy-done.5
  112.0 1.7 copy-done.6
  113.7 8.0 %attend.3 = (bf16[1024,1024]{1,0:T(8,128)(2,1)S(1)}, bf16[256,512]{1,0:T(8,128)(2,1)S(1)}, bf16[256,512]{1,0:T(8,128)(2,1)S(1)}) custom-call(s32[2]{0:T(128)S(1)} %copy-done.4, bf16[1024,2560]{1,0:T(8,128)(2,1)} %bitcast.21, bf16[512,2048]{1,0:T(8,128)(2,1)S(1)} %copy-done.5, bf16[1024,640]{1,0:T(8,128)(2,1)S(1)} %bitcast.16, f32[1024,640]{1,0:T(8,128)S(1)} %copy-done.6), custom_call_target="tpu_custom_call" | custom-call | flops 5000000000 | bytes 6000000 | tf_op jit(solution)/shard_map/attend/pallas_call | solution.py:318
  122.5 1.6 collective-permute-start.1
  124.1 2.7 %collective-permute-start.2 = (bf16[64,1536]{1,0:T(8,128)(2,1)S(1)}, bf16[64,1536]{1,0:T(8,128)(2,1)S(1)}, u32[]{:S(2)}, u32[]{:S(2)}) collective-permute-start(bf16[64,1536]{1,0:T(8,128)(2,1)S(1)} %get-tuple-element.52), channel_id=1, source_target_pairs={{0,32},{8,40},{16,48},{24,56},{32,0},{40,8},{48,16},{56,24},{64,96... | collective-permute-start | bytes 589832 | tf_op jit(solution)/shard_map/ppermute | solution.py:345
  126.8 1.4 collective-permute-start.3
  128.3 0.6 collective-permute-start.5
  129.0 0.9 collective-permute-start.6
  129.8 0.8 collective-permute-done.1.refs_1_
  130.6 2.5 %collective-permute-start.7 = (bf16[64,512]{1,0:T(8,128)(2,1)S(1)}, bf16[64,512]{1,0:T(8,128)(2,1)S(1)}, u32[]{:S(2)}, u32[]{:S(2)}) collective-permute-start(bf16[64,512]{1,0:T(8,128)(2,1)S(1)} %get-tuple-element.59), channel_id=1, source_target_pairs={{0,48},{8,56},{16,0},{24,8},{32,16},{40,24},{48,32},{56,40},{64,11... | collective-permute-start | bytes 196616 | tf_op jit(solution)/shard_map/ppermute | solution.py:345
  133.1 3.7 %collective-permute-done.2.refs_2_ = bf16[64,1536]{1,0:T(8,128)(2,1)S(1)} collective-permute-done((bf16[64,1536]{1,0:T(8,128)(2,1)S(1)}, bf16[64,1536]{1,0:T(8,128)(2,1)S(1)}, u32[]{:S(2)}, u32[]{:S(2)}) %collective-permute-start.2) | collective-permute-done | bytes 196640 | tf_op jit(solution)/shard_map/ppermute | solution.py:345
  136.9 1.7 collective-permute-done.6.refs_6_
  138.8 3.7 %collective-permute-start.8 = (bf16[64,2048]{1,0:T(8,128)(2,1)S(1)}, bf16[64,2048]{1,0:T(8,128)(2,1)S(1)}, u32[]{:S(2)}, u32[]{:S(2)}) collective-permute-start(bf16[64,2048]{1,0:T(8,128)(2,1)S(1)} %merge.1.refs_0_), channel_id=1, source_target_pairs={{0,64},{8,72},{16,80},{24,88},{32,96},{40,104},{48,112},{56,120},{... | collective-permute-start | bytes 786440 | tf_op jit(solution)/shard_map/ppermute | solution.py:345
  142.5 2.0 %unpack.2.refs_0_ = bf16[128,12288]{1,0:T(8,128)(2,1)} custom-call(bf16[8,128,1152]{2,1,0:T(8,128)(2,1)S(1)} %all-to-all-done.2.refs_0_), custom_call_target="tpu_custom_call" | custom-call | flops 1 | bytes 1 | tf_op jit(solution)/shard_map/unpack/pallas_call | solution.py:141
  144.5 4.8 %all-to-all-start.3 = ((bf16[8,128,1024]{2,1,0:T(8,128)(2,1)}), bf16[8,128,1024]{2,1,0:T(8,128)(2,1)S(1)}, u32[]{:S(2)}, u32[]{:S(2)}) async-start(bf16[8,128,1024]{2,1,0:T(8,128)(2,1)} %bitcast.15), calls=%async_computation.3 | async-start | bytes 4194304 | tf_op jit(solution)/shard_map/all_to_all | solution.py:340
  149.4 2.3 %collective-permute-start.11 = (bf16[64,2048]{1,0:T(8,128)(2,1)S(1)}, bf16[64,2048]{1,0:T(8,128)(2,1)S(1)}, u32[]{:S(2)}, u32[]{:S(2)}) collective-permute-start(bf16[64,2048]{1,0:T(8,128)(2,1)S(1)} %add.13.refs_0_), channel_id=1, source_target_pairs={{0,48},{8,56},{16,0},{24,8},{32,16},{40,24},{48,32},{56,40},{64,11... | collective-permute-start | bytes 786440 | tf_op jit(solution)/shard_map/ppermute | solution.py:345
  151.7 1.2 collective-permute-start.10
  152.9 0.7 collective-permute-start.9
  153.6 8.8 %collective-permute-done.11.refs_3_ = bf16[64,2048]{1,0:T(8,128)(2,1)S(1)} collective-permute-done((bf16[64,2048]{1,0:T(8,128)(2,1)S(1)}, bf16[64,2048]{1,0:T(8,128)(2,1)S(1)}, u32[]{:S(2)}, u32[]{:S(2)}) %collective-permute-start.11) | collective-permute-done | bytes 262176 | tf_op jit(solution)/shard_map/ppermute | solution.py:345
  162.9 2.9 %collective-permute-done.9.refs_1_ = bf16[64,2048]{1,0:T(8,128)(2,1)S(1)} collective-permute-done((bf16[64,2048]{1,0:T(8,128)(2,1)S(1)}, bf16[64,2048]{1,0:T(8,128)(2,1)S(1)}, u32[]{:S(2)}, u32[]{:S(2)}) %collective-permute-start.9) | collective-permute-done | bytes 262176 | tf_op jit(solution)/shard_map/ppermute | solution.py:345
  165.9 1.5 collective-permute-done.13.refs_5_
  167.4 2.8 %place.1 = f32[512,2048]{1,0:T(8,128)} custom-call(s32[2]{0:T(128)S(1)} %copy-done.4, bf16[64,2048]{1,0:T(8,128)(2,1)S(1)} %add.13.refs_0_, bf16[64,2048]{1,0:T(8,128)(2,1)S(1)} %collective-permute-done.9.refs_1_, bf16[64,2048]{1,0:T(8,128)(2,1)S(1)} %collective-permute-done.10.refs_2_, bf16[64,2048]{1,0:T(8,128)(2,1)S(1)} %collective-permute-done.11.refs_3_, ...), custom_call_target="tpu_custom_call" | custom-call | flops 1 | bytes 1 | tf_op jit(solution)/shard_map/place/pallas_call | solution.py:431
  170.2 4.9 %all-to-all-done.3.refs_1_ = bf16[8,128,1024]{2,1,0:T(8,128)(2,1)S(1)} async-done(((bf16[8,128,1024]{2,1,0:T(8,128)(2,1)}), bf16[8,128,1024]{2,1,0:T(8,128)(2,1)S(1)}, u32[]{:S(2)}, u32[]{:S(2)}) %all-to-all-start.3) | async-done | bytes 2097184 | tf_op jit(solution)/shard_map/all_to_all | solution.py:340
  175.1 1.8 %unpack.3 = (bf16[128,12288]{1,0:T(8,128)(2,1)}, bf16[576,128]{1,0:T(8,128)(2,1)}) custom-call(bf16[128,12288]{1,0:T(8,128)(2,1)} %unpack.2.refs_0_, bf16[8,128,1024]{2,1,0:T(8,128)(2,1)S(1)} %all-to-all-done.3.refs_1_), custom_call_target="tpu_custom_call", output_to_operand_aliasing={{0}: (0, {})} | custom-call | flops 1 | bytes 1 | tf_op jit(solution)/shard_map/unpack/pallas_call | solution.py:141
  (34 shorter events, 1.9 us)
Async XLA Ops:
  74.3 27.6 %all-to-all-start.1 = ((bf16[8,128,640]{2,1,0:T(8,128)(2,1)}), bf16[8,128,640]{2,1,0:T(8,128)(2,1)S(1)}, u32[]{:S(2)}, u32[]{:S(2)}) async-start(bf16[8,128,640]{2,1,0:T(8,128)(2,1)} %get-tuple-element.39), calls=%async_computation.1 | async-start | bytes 2621440 | tf_op jit(solution)/shard_map/all_to_all | solution.py:340
  102.0 1.1 copy-start.1
  103.0 5.8 %copy-start.7 = (bf16[256,1536]{1,0:T(8,128)(2,1)S(1)}, bf16[256,1536]{1,0:T(8,128)(2,1)}, u32[]{:S(2)}) copy-start(bf16[256,1536]{1,0:T(8,128)(2,1)} %get-tuple-element.45) | copy-start | bytes 2359300
  103.0 6.0 %copy-start.4 = (s32[2]{0:T(128)S(1)}, s32[2]{0:T(128)}, u32[]{:S(2)}) copy-start(s32[2]{0:T(128)} %pad_add_fusion.refs_0_.place) | copy-start | bytes 28
  103.0 39.5 %all-to-all-start.2 = ((bf16[8,128,1152]{2,1,0:T(8,128)(2,1)}), bf16[8,128,1152]{2,1,0:T(8,128)(2,1)S(1)}, u32[]{:S(2)}, u32[]{:S(2)}) async-start(bf16[8,128,1152]{2,1,0:T(8,128)(2,1)} %bitcast.23), calls=%async_computation.2 | async-start | bytes 4718592 | tf_op jit(solution)/shard_map/all_to_all | solution.py:340
  108.8 13.0 %collective-permute-start = (bf16[256,1536]{1,0:T(8,128)(2,1)S(1)}, bf16[256,1536]{1,0:T(8,128)(2,1)S(1)}, u32[]{:S(2)}, u32[]{:S(2)}) collective-permute-start(bf16[256,1536]{1,0:T(8,128)(2,1)S(1)} %copy-done.7), channel_id=1, source_target_pairs={{0,8},{8,0},{16,24},{24,16},{32,40},{40,32},{48,56},{56,48},{64,72... | collective-permute-start | bytes 2359304 | tf_op jit(solution)/shard_map/ppermute | solution.py:345
  109.1 1.3 copy-start.2
  110.4 1.6 copy-start.5
  112.0 1.7 copy-start.6
  113.7 8.6 %copy-start.3 = (bf16[256,1536]{1,0:T(8,128)(2,1)S(1)}, bf16[256,1536]{1,0:T(8,128)(2,1)}, u32[]{:S(2)}) copy-start(bf16[256,1536]{1,0:T(8,128)(2,1)} %get-tuple-element.48.keep_ref) | copy-start | bytes 2359300
  121.7 17.1 %copy-start = (bf16[1024,1024]{1,0:T(8,128)(2,1)}, bf16[1024,1024]{1,0:T(8,128)(2,1)S(1)}, u32[]{:S(2)}) copy-start(bf16[1024,1024]{1,0:T(8,128)(2,1)S(1)} %get-tuple-element.61) | copy-start | bytes 6291460
  121.8 6.5 %collective-permute-start.4 = (bf16[256,512]{1,0:T(8,128)(2,1)S(1)}, bf16[256,512]{1,0:T(8,128)(2,1)S(1)}, u32[]{:S(2)}, u32[]{:S(2)}) collective-permute-start(bf16[256,512]{1,0:T(8,128)(2,1)S(1)} %get-tuple-element.55), channel_id=1, source_target_pairs={{0,8},{8,0},{16,24},{24,16},{32,40},{40,32},{48,56},{56,48},{64,72... | collective-permute-start | bytes 786440 | tf_op jit(solution)/shard_map/ppermute | solution.py:345
  122.5 8.1 %collective-permute-start.1 = (bf16[64,1536]{1,0:T(8,128)(2,1)S(1)}, bf16[64,1536]{1,0:T(8,128)(2,1)S(1)}, u32[]{:S(2)}, u32[]{:S(2)}) collective-permute-start(bf16[64,1536]{1,0:T(8,128)(2,1)S(1)} %get-tuple-element.51), channel_id=1, source_target_pairs={{0,16},{8,24},{16,32},{24,40},{32,48},{40,56},{48,0},{56,8},{64,80... | collective-permute-start | bytes 589832 | tf_op jit(solution)/shard_map/ppermute | solution.py:345
  124.1 12.8 %collective-permute-start.2 = (bf16[64,1536]{1,0:T(8,128)(2,1)S(1)}, bf16[64,1536]{1,0:T(8,128)(2,1)S(1)}, u32[]{:S(2)}, u32[]{:S(2)}) collective-permute-start(bf16[64,1536]{1,0:T(8,128)(2,1)S(1)} %get-tuple-element.52), channel_id=1, source_target_pairs={{0,32},{8,40},{16,48},{24,56},{32,0},{40,8},{48,16},{56,24},{64,96... | collective-permute-start | bytes 589832 | tf_op jit(solution)/shard_map/ppermute | solution.py:345
  126.8 10.0 %collective-permute-start.3 = (bf16[64,1536]{1,0:T(8,128)(2,1)S(1)}, bf16[64,1536]{1,0:T(8,128)(2,1)S(1)}, u32[]{:S(2)}, u32[]{:S(2)}) collective-permute-start(bf16[64,1536]{1,0:T(8,128)(2,1)S(1)} %get-tuple-element.53), channel_id=1, source_target_pairs={{0,48},{8,56},{16,0},{24,8},{32,16},{40,24},{48,32},{56,40},{64,11... | collective-permute-start | bytes 589832 | tf_op jit(solution)/shard_map/ppermute | solution.py:345
  128.3 8.6 %collective-permute-start.5 = (bf16[64,512]{1,0:T(8,128)(2,1)S(1)}, bf16[64,512]{1,0:T(8,128)(2,1)S(1)}, u32[]{:S(2)}, u32[]{:S(2)}) collective-permute-start(bf16[64,512]{1,0:T(8,128)(2,1)S(1)} %get-tuple-element.57), channel_id=1, source_target_pairs={{0,16},{8,24},{16,32},{24,40},{32,48},{40,56},{48,0},{56,8},{64,80... | collective-permute-start | bytes 196616 | tf_op jit(solution)/shard_map/ppermute | solution.py:345
  129.0 9.7 %collective-permute-start.6 = (bf16[64,512]{1,0:T(8,128)(2,1)S(1)}, bf16[64,512]{1,0:T(8,128)(2,1)S(1)}, u32[]{:S(2)}, u32[]{:S(2)}) collective-permute-start(bf16[64,512]{1,0:T(8,128)(2,1)S(1)} %get-tuple-element.58), channel_id=1, source_target_pairs={{0,32},{8,40},{16,48},{24,56},{32,0},{40,8},{48,16},{56,24},{64,96... | collective-permute-start | bytes 196616 | tf_op jit(solution)/shard_map/ppermute | solution.py:345
  130.6 8.0 %collective-permute-start.7 = (bf16[64,512]{1,0:T(8,128)(2,1)S(1)}, bf16[64,512]{1,0:T(8,128)(2,1)S(1)}, u32[]{:S(2)}, u32[]{:S(2)}) collective-permute-start(bf16[64,512]{1,0:T(8,128)(2,1)S(1)} %get-tuple-element.59), channel_id=1, source_target_pairs={{0,48},{8,56},{16,0},{24,8},{32,16},{40,24},{48,32},{56,40},{64,11... | collective-permute-start | bytes 196616 | tf_op jit(solution)/shard_map/ppermute | solution.py:345
  138.8 10.5 %collective-permute-start.8 = (bf16[64,2048]{1,0:T(8,128)(2,1)S(1)}, bf16[64,2048]{1,0:T(8,128)(2,1)S(1)}, u32[]{:S(2)}, u32[]{:S(2)}) collective-permute-start(bf16[64,2048]{1,0:T(8,128)(2,1)S(1)} %merge.1.refs_0_), channel_id=1, source_target_pairs={{0,64},{8,72},{16,80},{24,88},{32,96},{40,104},{48,112},{56,120},{... | collective-permute-start | bytes 786440 | tf_op jit(solution)/shard_map/ppermute | solution.py:345
  144.5 30.6 %all-to-all-start.3 = ((bf16[8,128,1024]{2,1,0:T(8,128)(2,1)}), bf16[8,128,1024]{2,1,0:T(8,128)(2,1)S(1)}, u32[]{:S(2)}, u32[]{:S(2)}) async-start(bf16[8,128,1024]{2,1,0:T(8,128)(2,1)} %bitcast.15), calls=%async_computation.3 | async-start | bytes 4194304 | tf_op jit(solution)/shard_map/all_to_all | solution.py:340
  149.4 13.0 %collective-permute-start.11 = (bf16[64,2048]{1,0:T(8,128)(2,1)S(1)}, bf16[64,2048]{1,0:T(8,128)(2,1)S(1)}, u32[]{:S(2)}, u32[]{:S(2)}) collective-permute-start(bf16[64,2048]{1,0:T(8,128)(2,1)S(1)} %add.13.refs_0_), channel_id=1, source_target_pairs={{0,48},{8,56},{16,0},{24,8},{32,16},{40,24},{48,32},{56,40},{64,11... | collective-permute-start | bytes 786440 | tf_op jit(solution)/shard_map/ppermute | solution.py:345
  151.7 10.8 %collective-permute-start.10 = (bf16[64,2048]{1,0:T(8,128)(2,1)S(1)}, bf16[64,2048]{1,0:T(8,128)(2,1)S(1)}, u32[]{:S(2)}, u32[]{:S(2)}) collective-permute-start(bf16[64,2048]{1,0:T(8,128)(2,1)S(1)} %add.13.refs_0_), channel_id=1, source_target_pairs={{0,32},{8,40},{16,48},{24,56},{32,0},{40,8},{48,16},{56,24},{64,96... | collective-permute-start | bytes 786440 | tf_op jit(solution)/shard_map/ppermute | solution.py:345
  152.9 12.9 %collective-permute-start.9 = (bf16[64,2048]{1,0:T(8,128)(2,1)S(1)}, bf16[64,2048]{1,0:T(8,128)(2,1)S(1)}, u32[]{:S(2)}, u32[]{:S(2)}) collective-permute-start(bf16[64,2048]{1,0:T(8,128)(2,1)S(1)} %add.13.refs_0_), channel_id=1, source_target_pairs={{0,16},{8,24},{16,32},{24,40},{32,48},{40,56},{48,0},{56,8},{64,80... | collective-permute-start | bytes 786440 | tf_op jit(solution)/shard_map/ppermute | solution.py:345
  153.6 12.2 %collective-permute-start.12 = (bf16[64,2048]{1,0:T(8,128)(2,1)S(1)}, bf16[64,2048]{1,0:T(8,128)(2,1)S(1)}, u32[]{:S(2)}, u32[]{:S(2)}) collective-permute-start(bf16[64,2048]{1,0:T(8,128)(2,1)S(1)} %add.13.refs_0_), channel_id=1, source_target_pairs={{0,8},{8,0},{16,24},{24,16},{32,40},{40,32},{48,56},{56,48},{64,72... | collective-permute-start | bytes 786440 | tf_op jit(solution)/shard_map/ppermute | solution.py:345
  162.4 3.4 %collective-permute-start.15 = (bf16[64,2048]{1,0:T(8,128)(2,1)S(1)}, bf16[64,2048]{1,0:T(8,128)(2,1)S(1)}, u32[]{:S(2)}, u32[]{:S(2)}) collective-permute-start(bf16[64,2048]{1,0:T(8,128)(2,1)S(1)} %collective-permute-done.11.refs_3_), channel_id=1, source_target_pairs={{0,8},{8,0},{16,24},{24,16},{32,40},{40,32},{48,56},{56,48},{64,72... | collective-permute-start | bytes 786440 | tf_op jit(solution)/shard_map/ppermute | solution.py:345
  162.5 3.4 %collective-permute-start.14 = (bf16[64,2048]{1,0:T(8,128)(2,1)S(1)}, bf16[64,2048]{1,0:T(8,128)(2,1)S(1)}, u32[]{:S(2)}, u32[]{:S(2)}) collective-permute-start(bf16[64,2048]{1,0:T(8,128)(2,1)S(1)} %collective-permute-done.10.refs_2_), channel_id=1, source_target_pairs={{0,8},{8,0},{16,24},{24,16},{32,40},{40,32},{48,56},{56,48},{64,72... | collective-permute-start | bytes 786440 | tf_op jit(solution)/shard_map/ppermute | solution.py:345
  165.8 1.5 collective-permute-start.13
